TPU v7x, 256 devices: a whole 4x4x8 slice. The times are simulated.
256 devices in a mesh: inst: 16 (over x, y), section: 8 (over z), tp: 2 (over core).
Axes of the slice: x: 4, y: 4, z: 8, core: 2. Of those that a mesh axis runs over, the one named last changes fastest.
Arguments:
- tokens: bfloat16 [16, 1024, 8192], P('inst', None, 'section'), may hold values from -40 to 40
- norm_gain: float32 [8192], P('section'), may hold values from 0.4 to 6
- query_weight: bfloat16 [8192, 4096], P(('section', 'inst'), 'tp'), may hold values from -1 to 1
- key_weight: bfloat16 [8192, 1024], P(('section', 'inst'), 'tp'), may hold values from -1 to 1
- value_matrix: bfloat16 [8192, 1024], P(('section', 'inst'), 'tp'), may hold values from -0.0625 to 0.0625
Outputs:
- attended: bfloat16 [16, 1024, 4096], P('inst', 'section', 'tp')
- rotated_key_cache: bfloat16 [16, 1024, 1024], P('inst', 'section', 'tp')
- value_store_cache: bfloat16 [16, 1024, 1024], P('inst', 'section', 'tp')
All inputs are finite; a program needn't handle non-finite values.
Results may differ from a plain program's by a relative error of at most 0.04.
Values may be sent and summed in bfloat16 or wider, within the bound.
No kernel may reach another device: no remote copies, remote signals or barrier semaphores. Data moves between devices by JAX's collectives and lax.ppermute only.
A program may use at most 64 MiB of HBM per device.

v0:
```python
import jax
import jax.numpy as jnp
from jax import lax
from jax.sharding import PartitionSpec as P

MODEL_WIDTH = 8192
HEAD_SIZE = 128


EPS = 1e-05
THETA = 500000.0


def rotate(value_rows, positions):
    rows = value_rows.shape[0]
    heads = value_rows.shape[1] // HEAD_SIZE
    split = value_rows.reshape(rows, heads, HEAD_SIZE)
    index = jnp.arange(HEAD_SIZE // 2).astype(jnp.float32)
    freqs = jnp.exp(index * (-2.0 / HEAD_SIZE) * jnp.log(jnp.float32(THETA)))
    angles = positions[:, None] * freqs[None, :]
    cosine = jnp.cos(angles)[:, None, :]
    sine = jnp.sin(angles)[:, None, :]
    first = split[..., : HEAD_SIZE // 2]
    second = split[..., HEAD_SIZE // 2 :]
    joined = jnp.concatenate(
        [first * cosine - second * sine, second * cosine + first * sine], axis=-1
    )
    return joined.reshape(rows, heads * HEAD_SIZE)


def attend_block(carry, pieces, query_heads, query_pos):
    top, total, summed = carry
    keys, value_rows = pieces
    count = keys.shape[0]
    kv_heads = keys.shape[1] // HEAD_SIZE
    key_heads = keys.reshape(count, kv_heads, HEAD_SIZE)
    value_heads = value_rows.reshape(count, kv_heads, HEAD_SIZE)
    score = jnp.einsum("rgjd,ngd->gjrn", query_heads, key_heads, preferred_element_type=jnp.float32)
    score = score / jnp.sqrt(jnp.float32(HEAD_SIZE))
    key_pos = jnp.arange(count)
    causal = query_pos[:, None] >= key_pos[None, :]
    score = jnp.where(causal, score, jnp.float32(-1e30))
    new_top = jnp.maximum(top, jnp.max(score, axis=-1))
    expo = jnp.where(causal, jnp.exp(score - new_top[..., None]), jnp.float32(0.0))
    total = jnp.sum(expo, axis=-1)
    product = jnp.einsum(
        "gjrn,ngd->gjrd", expo.astype(jnp.bfloat16), value_heads, preferred_element_type=jnp.float32
    )
    summed = product
    return (new_top, total, summed)


def local(tokens, norm_gain, query_weight, key_weight, value_matrix):
    states = tokens[0]
    seq_len = states.shape[0]
    sections = lax.axis_size("section")
    rows = seq_len // sections
    base_offset = lax.axis_index("section") * rows
    floats = states.astype(jnp.float32)
    squares = jnp.sum(floats * floats, axis=1)
    scaled = (floats * norm_gain[None, :]).astype(jnp.bfloat16)
    q_cols = query_weight.shape[1]
    kv_cols = key_weight.shape[1]
    q_heads = q_cols // HEAD_SIZE
    kv_heads = kv_cols // HEAD_SIZE
    group_size = q_heads // kv_heads
    pieces = (
        lax.all_gather(query_weight, "inst", axis=0, tiled=True),
        lax.all_gather(key_weight, "inst", axis=0, tiled=True),
        lax.all_gather(value_matrix, "inst", axis=0, tiled=True),
    )
    query_part, key_part, value_part = tuple(
        (jnp.dot(scaled, piece, preferred_element_type=jnp.float32) for piece in pieces)
    )
    local_pos = base_offset + jnp.arange(rows)
    local_float = local_pos.astype(jnp.float32)
    query, key, value, local_squares = (
        lax.psum_scatter(
            query_part.astype(jnp.bfloat16), "section", scatter_dimension=0, tiled=True
        ).astype(jnp.float32),
        lax.psum_scatter(
            key_part.astype(jnp.bfloat16), "section", scatter_dimension=0, tiled=True
        ).astype(jnp.float32),
        lax.psum_scatter(
            value_part.astype(jnp.bfloat16), "section", scatter_dimension=0, tiled=True
        ).astype(jnp.float32),
        lax.psum_scatter(
            squares.astype(jnp.bfloat16), "section", scatter_dimension=0, tiled=True
        ).astype(jnp.float32),
    )
    inverse = 1.0 / jnp.sqrt(local_squares / MODEL_WIDTH + EPS)
    rotated_key_cache = rotate(key * inverse[:, None], local_float).astype(jnp.bfloat16)
    value_store_cache = (value * inverse[:, None]).astype(jnp.bfloat16)
    rotated_query = rotate(query * inverse[:, None], local_float).astype(jnp.bfloat16)
    query_heads = rotated_query.reshape(rows, kv_heads, group_size, HEAD_SIZE)
    start_carry = (
        jnp.full((kv_heads, group_size, rows), -1e30, jnp.float32),
        jnp.zeros((kv_heads, group_size, rows), jnp.float32),
        jnp.zeros((kv_heads, group_size, rows, HEAD_SIZE), jnp.float32),
    )
    top, total, summed = attend_block(
        start_carry,
        (
            lax.all_gather(rotated_key_cache, "section", axis=0, tiled=True),
            lax.all_gather(value_store_cache, "section", axis=0, tiled=True),
        ),
        query_heads,
        local_pos,
    )
    mixed = summed / total[..., None]
    attended = jnp.transpose(mixed, (2, 0, 1, 3)).reshape(rows, q_cols).astype(jnp.bfloat16)
    return (attended[None], rotated_key_cache[None], value_store_cache[None])


def solution(mesh):
    in_specs = (
        P("inst", None, "section"),
        P("section"),
        P(("section", "inst"), "tp"),
        P(("section", "inst"), "tp"),
        P(("section", "inst"), "tp"),
    )
    out_specs = (P("inst", "section", "tp"), P("inst", "section", "tp"), P("inst", "section", "tp"))
    return jax.shard_map(local, mesh=mesh, in_specs=in_specs, out_specs=out_specs, check_vma=False)
```

profile of v0, /device:TPU:1, one launch (start us, length us, event | category | flops | bytes accessed | tf_op | source)
XLA Modules:
  0.0 397.7 jit_solution(8727150044169944429)
XLA Ops:
  7.2 0.0 all-gather.6.cloned.1.call-start
  7.2 0.7 all-gather.6.cloned.1.call-update
  7.9 0.0 all-gather.12.cloned.1.call-start
  7.9 0.7 all-gather.12.cloned.1.call-update
  8.7 0.0 reduce-scatter.4.cloned.1.call-start
  8.7 51.8 %all-gather.6.cloned.1.call-done = bf16[1024,512]{1,0:T(8,128)(2,1)} async-done(((bf16[64,512]{1,0:T(8,128)(2,1)}), bf16[1024,512]{1,0:T(8,128)(2,1)}) %all-gather.6.cloned.1.call-update) | async-done | bytes 1048592 | tf_op jit(solution)/shard_map/all_gather | solution.py:69
  60.6 4.1 %fusion.13 = bf16[1024,512]{1,0:T(8,128)(2,1)} fusion(bf16[1024,512]{1,0:T(8,128)(2,1)} %all-gather.6.cloned.1.call-done, bf16[1,1024,1024]{2,1,0:T(8,128)(2,1)} %param.5, f32[1024]{0:T(1024)} %param.6), kind=kOutput, calls=%fused_computation.14 | convolution fusion | flops 1077411840 | bytes 4198400 | tf_op jit(solution)/shard_map/dot_general | solution.py:73
  64.7 0.0 reduce-scatter.4.cloned.1.call-update
  64.7 0.0 reduce-scatter.8.cloned.1.call-start
  64.7 45.3 %all-gather.12.cloned.1.call-done = bf16[1024,512]{1,0:T(8,128)(2,1)} async-done(((bf16[64,512]{1,0:T(8,128)(2,1)}), bf16[1024,512]{1,0:T(8,128)(2,1)}) %all-gather.12.cloned.1.call-update) | async-done | bytes 1048592 | tf_op jit(solution)/shard_map/all_gather | solution.py:70
  110.0 3.5 fusion.16
  113.5 0.0 reduce-scatter.8.cloned.1.call-update
  113.5 0.0 all-gather.10.cloned.1.call-start
  113.6 0.5 all-gather.10.cloned.1.call-update
  114.1 0.0 all-gather.14.cloned.1.call-start
  114.2 0.6 dynamic-slice
  115.4 0.5 fusion.4
  115.9 14.4 %all-reduce = bf16[1024]{0:T(1024)(128)(2,1)S(1)} all-reduce(bf16[1024]{0:T(1024)(128)(2,1)S(1)} %fusion.4), channel_id=3, replica_groups=mesh['inst'=16,'section'=8,'tp'=2] {'section'}, use_global_device_ids=true, to_apply=%region_2.0.clone | all-reduce | flops 1024 | bytes 4096
  130.3 0.1 fusion.26
  130.4 17.2 %reduce-scatter.4.cloned.1.call-done = bf16[128,512]{1,0:T(8,128)(2,1)} async-done(((bf16[1024,512]{1,0:T(8,128)(2,1)}), bf16[128,512]{1,0:T(8,128)(2,1)}) %reduce-scatter.4.cloned.1.call-update) | async-done | bytes 131088 | tf_op jit(solution)/shard_map/reduce_scatter | solution.py:81
  147.6 39.3 %reduce-scatter.8.cloned.1.call-done = bf16[128,512]{1,0:T(8,128)(2,1)} async-done(((bf16[1024,512]{1,0:T(8,128)(2,1)}), bf16[128,512]{1,0:T(8,128)(2,1)}) %reduce-scatter.8.cloned.1.call-update) | async-done | bytes 131088 | tf_op jit(solution)/shard_map/reduce_scatter | solution.py:84
  186.9 1.7 convert_multiply_fusion.2
  188.7 0.0 reduce-scatter.6.cloned.1.call-start
  188.7 60.7 %all-gather.10.cloned.1.call-done = bf16[1024,2048]{1,0:T(8,128)(2,1)} async-done(((bf16[64,2048]{1,0:T(8,128)(2,1)}), bf16[1024,2048]{1,0:T(8,128)(2,1)}) %all-gather.10.cloned.1.call-update) | async-done | bytes 4194320 | tf_op jit(solution)/shard_map/all_gather | solution.py:68
  249.5 8.3 %convolution_convert_fusion = bf16[1024,2048]{1,0:T(8,128)(2,1)} fusion(bf16[1024,2048]{1,0:T(8,128)(2,1)} %all-gather.10.cloned.1.call-done, bf16[1,1024,1024]{2,1,0:T(8,128)(2,1)S(1)} %copy-done, f32[1024]{0:T(1024)S(1)} %copy-done.1), kind=kOutput, calls=%fused_computation.11 | convolution fusion | flops 4300210176 | bytes 10489856 | tf_op jit(solution)/shard_map/dot_general | solution.py:73
  257.7 0.0 reduce-scatter.6.cloned.1.call-update
  257.7 0.2 all-gather.8.cloned.1.call-start
  258.0 0.3 multiply_cosine_fusion
  258.3 0.1 reshape.115
  258.4 0.3 multiply_subtract_fusion
  258.7 0.2 maximum_convert_fusion
  258.9 0.8 copy.18
  259.7 0.0 all-gather.8.cloned.1.call-update
  259.7 0.1 iota_compare_fusion
  259.8 0.7 convert_element_type.108
  260.5 24.5 %all-gather.14.cloned.1.call-done = bf16[1024,512]{1,0:T(8,128)(2,1)} async-done(((bf16[128,512]{1,0:T(8,128)(2,1)}), bf16[1024,512]{1,0:T(8,128)(2,1)}) %all-gather.14.cloned.1.call-update) | async-done | bytes 1048592 | tf_op jit(solution)/shard_map/all_gather | solution.py:105
  285.1 1.5 copy.29
  286.6 60.0 %reduce-scatter.6.cloned.1.call-done = bf16[128,2048]{1,0:T(8,128)(2,1)} async-done(((bf16[1024,2048]{1,0:T(8,128)(2,1)}), bf16[128,2048]{1,0:T(8,128)(2,1)}) %reduce-scatter.6.cloned.1.call-update) | async-done | bytes 524304 | tf_op jit(solution)/shard_map/reduce_scatter | solution.py:78
  346.6 1.2 multiply_bitcast_fusion
  347.8 0.2 copy.30
  347.9 0.6 subtract_convert_fusion
  348.5 0.3 pad_maximum_fusion
  348.8 0.1 copy.19
  349.0 34.0 %all-gather.8.cloned.1.call-done = bf16[1024,512]{0,1:T(8,128)(2,1)} async-done(((bf16[128,512]{0,1:T(8,128)(2,1)}), bf16[1024,512]{0,1:T(8,128)(2,1)}) %all-gather.8.cloned.1.call-update) | async-done | bytes 1048592 | tf_op jit(solution)/shard_map/all_gather | solution.py:104
  382.9 2.7 fusion
  385.6 2.0 fusion.1
  387.7 2.1 divide_convert_fusion
  389.8 1.0 copy.23
  (11 shorter events, 0.1 us)
Async XLA Ops:
  7.2 53.4 %all-gather.6.cloned.1.call-start = ((), (), s32[]{:S(2)}) async-start(), calls=%async_computation.3 | async-start | bytes 1114112 | tf_op jit(solution)/shard_map/all_gather | solution.py:69
  7.9 102.1 %all-gather.12.cloned.1.call-start = ((), (), s32[]{:S(2)}) async-start(), calls=%async_computation.8 | async-start | bytes 1114112 | tf_op jit(solution)/shard_map/all_gather | solution.py:70
  8.6 101.4 %copy-start = (bf16[1,1024,1024]{2,1,0:T(8,128)(2,1)S(1)}, bf16[1,1024,1024]{2,1,0:T(8,128)(2,1)}, u32[]{:S(2)}) copy-start(bf16[1,1024,1024]{2,1,0:T(8,128)(2,1)} %param.5) | copy-start | bytes 6291460
  8.7 101.4 %copy-start.1 = (f32[1024]{0:T(1024)S(1)}, f32[1024]{0:T(1024)}, u32[]{:S(2)}) copy-start(f32[1024]{0:T(1024)} %param.6) | copy-start | bytes 12292
  8.7 139.0 %reduce-scatter.4.cloned.1.call-start = ((), (), s32[]{:S(2)}) async-start(), calls=%async_computation.4 | async-start | bytes 1179648 | tf_op jit(solution)/shard_map/reduce_scatter | solution.py:81
  64.7 49.5 %copy-start.2 = (u32[256]{0:T(256)S(1)}, u32[256]{0:T(256)}, u32[]{:S(2)}) copy-start(u32[256]{0:T(256)} %constant.34) | copy-start | bytes 3076
  64.7 122.2 %reduce-scatter.8.cloned.1.call-start = ((), (), s32[]{:S(2)}) async-start(), calls=%async_computation.9 | async-start | bytes 1179648 | tf_op jit(solution)/shard_map/reduce_scatter | solution.py:84
  113.5 135.9 %all-gather.10.cloned.1.call-start = ((), (), s32[]{:S(2)}) async-start(), calls=%async_computation.6 | async-start | bytes 4456448 | tf_op jit(solution)/shard_map/all_gather | solution.py:68
  114.1 170.9 %all-gather.14.cloned.1.call-start = ((), (), s32[]{:S(2)}) async-start(), calls=%async_computation.10 | async-start | bytes 1179648 | tf_op jit(solution)/shard_map/all_gather | solution.py:105
  188.7 157.9 %reduce-scatter.6.cloned.1.call-start = ((), (), s32[]{:S(2)}) async-start(), calls=%async_computation.7 | async-start | bytes 4718592 | tf_op jit(solution)/shard_map/reduce_scatter | solution.py:78
  257.7 125.2 %all-gather.8.cloned.1.call-start = ((), (), s32[]{:S(2)}) async-start(), calls=%async_computation.5 | async-start | bytes 1179648 | tf_op jit(solution)/shard_map/all_gather | solution.py:104
Sparse Core Ops, SparseCore 0:
  10.4 50.0 all-gather.5
  63.0 47.0 all-gather.11
  112.6 35.0 reduce-scatter.3
  150.0 36.8 reduce-scatter.7
  189.2 60.1 all-gather.9
  251.7 33.3 all-gather.13
  287.6 58.9 reduce-scatter.5
  348.9 34.0 all-gather.7
where the time goes:
time: 401 us; the launch traced here: 398 us
  waiting for transfers between devices  335 us (84%)
  matrix products  20.7 us (5%)
  between operations  15 us (4%)
  blocking collectives  14.4 us (4%)
  other arithmetic  7.23 us (2%)
  local copies, waits for them, and re-layouts  5.01 us (1%)
    all_gather x1, waiting for transfers between devices, local(): lax.all_gather(query_weight, 'inst', axis=0, tiled=True)  60.7 us
    reduce_scatter x1, waiting for transfers between devices, local(): lax.psum_scatter(query_part.astype(jnp.bfloat16), 'section', scatter_dime...  60 us
    all_gather x1, waiting for transfers between devices, local(): lax.all_gather(key_weight, 'inst', axis=0, tiled=True)  51.8 us
    all_gather x1, waiting for transfers between devices, local(): lax.all_gather(value_matrix, 'inst', axis=0, tiled=True)  45.3 us
    reduce_scatter x1, waiting for transfers between devices, local(): lax.psum_scatter(value_part.astype(jnp.bfloat16), 'section', scatter_dime...  39.3 us
    all_gather x1, waiting for transfers between devices, local(): lax.all_gather(rotated_key_cache, 'section', axis=0, tiled=True)  34 us
    all_gather x1, waiting for transfers between devices, local(): lax.all_gather(value_store_cache, 'section', axis=0, tiled=True)  24.5 us
    reduce_scatter x1, waiting for transfers between devices, local(): lax.psum_scatter(key_part.astype(jnp.bfloat16), 'section', scatter_dimens...  17.2 us
  transfers between devices with their start and end apart: 8, of which 8 were waited for; matrix products, arithmetic and copies ran while one was open for 6% of the time, Pallas kernels for 0%

commit v1 on v0

--- a/solution.py
+++ b/solution.py
@@ -64,30 +64,20 @@
     q_heads = q_cols // HEAD_SIZE
     kv_heads = kv_cols // HEAD_SIZE
     group_size = q_heads // kv_heads
-    pieces = (
-        lax.all_gather(query_weight, "inst", axis=0, tiled=True),
-        lax.all_gather(key_weight, "inst", axis=0, tiled=True),
-        lax.all_gather(value_matrix, "inst", axis=0, tiled=True),
+    joined = lax.all_gather(
+        jnp.concatenate([query_weight, key_weight, value_matrix], axis=1), "inst", axis=0, tiled=True
     )
-    query_part, key_part, value_part = tuple(
-        (jnp.dot(scaled, piece, preferred_element_type=jnp.float32) for piece in pieces)
-    )
+    part = jnp.dot(scaled, joined, preferred_element_type=jnp.float32).astype(jnp.bfloat16)
+    section = lax.axis_index("section")
+    marks = jnp.where(jnp.arange(HEAD_SIZE)[None, :] == section, squares[:, None], 0.0)
+    part = jnp.concatenate([part, marks.astype(jnp.bfloat16)], axis=1)
     local_pos = base_offset + jnp.arange(rows)
     local_float = local_pos.astype(jnp.float32)
-    query, key, value, local_squares = (
-        lax.psum_scatter(
-            query_part.astype(jnp.bfloat16), "section", scatter_dimension=0, tiled=True
-        ).astype(jnp.float32),
-        lax.psum_scatter(
-            key_part.astype(jnp.bfloat16), "section", scatter_dimension=0, tiled=True
-        ).astype(jnp.float32),
-        lax.psum_scatter(
-            value_part.astype(jnp.bfloat16), "section", scatter_dimension=0, tiled=True
-        ).astype(jnp.float32),
-        lax.psum_scatter(
-            squares.astype(jnp.bfloat16), "section", scatter_dimension=0, tiled=True
-        ).astype(jnp.float32),
-    )
+    total_part = lax.psum_scatter(part, "section", scatter_dimension=0, tiled=True).astype(jnp.float32)
+    query = total_part[:, :q_cols]
+    key = total_part[:, q_cols : q_cols + kv_cols]
+    value = total_part[:, q_cols + kv_cols : q_cols + 2 * kv_cols]
+    local_squares = jnp.sum(total_part[:, q_cols + 2 * kv_cols :], axis=1)
     inverse = 1.0 / jnp.sqrt(local_squares / MODEL_WIDTH + EPS)
     rotated_key_cache = rotate(key * inverse[:, None], local_float).astype(jnp.bfloat16)
     value_store_cache = (value * inverse[:, None]).astype(jnp.bfloat16)
@@ -98,14 +88,11 @@
         jnp.zeros((kv_heads, group_size, rows), jnp.float32),
         jnp.zeros((kv_heads, group_size, rows, HEAD_SIZE), jnp.float32),
     )
+    both = lax.all_gather(
+        jnp.concatenate([rotated_key_cache, value_store_cache], axis=1), "section", axis=0, tiled=True
+    )
     top, total, summed = attend_block(
-        start_carry,
-        (
-            lax.all_gather(rotated_key_cache, "section", axis=0, tiled=True),
-            lax.all_gather(value_store_cache, "section", axis=0, tiled=True),
-        ),
-        query_heads,
-        local_pos,
+        start_carry, (both[:, :kv_cols], both[:, kv_cols:]), query_heads, local_pos
     )
     mixed = summed / total[..., None]
     attended = jnp.transpose(mixed, (2, 0, 1, 3)).reshape(rows, q_cols).astype(jnp.bfloat16)

time: 401 us -> 238 us (0.59)
  waiting for transfers between devices: 335 us -> 180 us
  blocking collectives: 14.4 us -> 0 us
  other arithmetic: 7.23 us -> 16 us
    all_gather x5 -> x2, waiting for transfers between devices: 216 us -> 103 us  [the longest x1 69.9 us: local(): lax.all_gather(jnp.concatenate([query_weight, key_weight, value_matrix],...]
    reduce_scatter x3 -> x1, waiting for transfers between devices: 117 us -> 77.1 us  [local(): lax.psum_scatter(part, 'section', scatter_dimension=0, tiled=True)]
    unnamed x1 -> x0, blocking collectives: 14.4 us -> none
    dot_general x3 -> x1, matrix products: 15.8 us -> 10 us  [local(): jnp.dot(scaled, joined, preferred_element_type=jnp.float32)]
    concatenate x0 -> x3, other arithmetic: none -> 5.79 us  [the longest x1 3.24 us: local(): part = jnp.concatenate([part, marks.astype(jnp.bfloat16)], axis=1)]
  transfers between devices with their start and end apart: 8 -> 3, of which waited for: 8 -> 3; matrix products, arithmetic and copies ran while one was open for 6% -> 2% of each run, Pallas kernels for 0% -> 0%
where the time goes in v1:
time: 238 us; the launch traced here: 235 us
  waiting for transfers between devices  180 us (76%)
  matrix products  17.8 us (7%)
  other arithmetic  16 us (7%)
  between operations  13.9 us (6%)
  local copies, waits for them, and re-layouts  6.67 us (3%)
    reduce_scatter x1, waiting for transfers between devices, local(): lax.psum_scatter(part, 'section', scatter_dimension=0, tiled=True)  77.1 us
    all_gather x1, waiting for transfers between devices, local(): lax.all_gather(jnp.concatenate([query_weight, key_weight, value_matrix],...  69.9 us
    all_gather x1, waiting for transfers between devices, local(): lax.all_gather(jnp.concatenate([rotated_key_cache, value_store_cache], ax...  33.2 us
    dot_general x1, matrix products, local(): jnp.dot(scaled, joined, preferred_element_type=jnp.float32)  10 us
    dot_general x1, matrix products, attend_block(): jnp.einsum('rgjd,ngd->gjrn', query_heads, key_heads, preferred_element_ty...  5.64 us
  transfers between devices with their start and end apart: 3, of which 3 were waited for; matrix products, arithmetic and copies ran while one was open for 2% of the time, Pallas kernels for 0%

profile of v1, /device:TPU:1, one launch (start us, length us, event | category | flops | bytes accessed | tf_op | source)
XLA Modules:
  0.0 234.8 jit_solution(7145616034138359920)
XLA Ops:
  7.2 0.0 all-gather.3.cloned.1.call-start
  7.2 1.8 pad_maximum_fusion.2
  9.0 0.0 all-gather.3.cloned.1.call-update
  9.0 0.0 reduce-scatter.2.cloned.1.call-start
  9.1 2.1 fusion.4
  11.2 0.2 select_convert_fusion
  11.4 69.9 %all-gather.3.cloned.1.call-done = bf16[1024,3072]{1,0:T(8,128)(2,1)} async-done(((bf16[64,3072]{1,0:T(8,128)(2,1)}), bf16[1024,3072]{1,0:T(8,128)(2,1)}) %all-gather.3.cloned.1.call-update) | async-done | bytes 6291472 | tf_op jit(solution)/shard_map/all_gather | solution.py:67
  81.3 10.0 %convolution_convert_fusion = bf16[1024,3072]{1,0:T(8,128)(2,1)S(1)} fusion(bf16[1024,3072]{1,0:T(8,128)(2,1)} %all-gather.3.cloned.1.call-done, bf16[1,1024,1024]{2,1,0:T(8,128)(2,1)} %param.5, f32[1024]{0:T(1024)} %param.6), kind=kOutput, calls=%fused_computation.6 | convolution fusion | flops 6448742400 | bytes 14684160 | tf_op jit(solution)/shard_map/dot_general | solution.py:70
  91.3 3.2 %pad_maximum_fusion = bf16[1024,3200]{1,0:T(8,128)(2,1)} fusion(bf16[1024,128]{1,0:T(8,128)(2,1)S(1)} %select_convert_fusion, bf16[1024,3072]{1,0:T(8,128)(2,1)S(1)} %convolution_convert_fusion), kind=kLoop, calls=%fused_computation.3 | loop fusion | flops 13107200 | bytes 13107200 | tf_op jit(solution)/shard_map/concatenate | solution.py:73
  94.5 0.0 reduce-scatter.2.cloned.1.call-update
  94.5 0.0 all-gather.5.cloned.1.call-start
  94.6 0.3 multiply_cosine_fusion
  94.9 77.1 %reduce-scatter.2.cloned.1.call-done = bf16[128,3200]{1,0:T(8,128)(2,1)} async-done(((bf16[1024,3200]{1,0:T(8,128)(2,1)}), bf16[128,3200]{1,0:T(8,128)(2,1)}) %reduce-scatter.2.cloned.1.call-update) | async-done | bytes 819216 | tf_op jit(solution)/shard_map/reduce_scatter | solution.py:76
  172.1 1.3 convert_element_type.78
  173.3 0.1 slice_reduce_fusion
  173.5 0.1 slice_multiply_fusion.2
  173.6 0.0 copy-start.1
  173.6 0.1 reshape.125
  173.7 0.3 multiply_subtract_fusion
  174.0 0.2 maximum_convert_fusion
  174.2 0.7 pad_maximum_fusion.3
  174.9 0.0 all-gather.5.cloned.1.call-update
  175.0 0.1 iota_compare_fusion
  175.1 0.7 convert_element_type.88
  175.8 0.1 fusion.14
  175.9 0.2 copy.20
  176.1 0.5 subtract_convert_fusion
  176.7 0.3 pad_maximum_fusion.1
  177.0 0.9 copy.8
  177.9 0.0 copy-done.1
  177.9 33.2 %all-gather.5.cloned.1.call-done = bf16[1024,1024]{1,0:T(8,128)(2,1)} async-done(((bf16[128,1024]{1,0:T(8,128)(2,1)}), bf16[1024,1024]{1,0:T(8,128)(2,1)}) %all-gather.5.cloned.1.call-update) | async-done | bytes 2097168 | tf_op jit(solution)/shard_map/all_gather | solution.py:91
  211.1 1.7 fusion.24
  212.8 0.3 reshape.126
  213.1 5.6 %fusion = (f32[4,4,128]{2,1,0:T(4,128)S(1)}, f32[4,1024,128,4]{2,1,3,0:T(8,128)}) fusion(pred[128,1024]{0,1:T(8,128)(4,1)S(1)} %iota_compare_fusion, bf16[128,4,4,128]{3,0,2,1:T(8,128)(2,1)} %bitcast.48, bf16[1024,4,128,1]{2,1,0,3:T(4,128)(2,1)S(1)} %bitcast.47), kind=kOutput, calls=%fused_computation.2 | convolution fusion | flops 543160320 | bytes 10100736 | tf_op jit(solution)/shard_map/rgjd,ngd->gjrn/dot_general | solution.py:38
  218.7 0.5 copy.18
  219.3 0.0 copy-start
  219.3 4.6 %fusion.1 = f32[4,4,128]{2,1,0:T(4,128)S(1)} fusion(f32[4,1024,128,4]{2,1,3,0:T(8,128)} %get-tuple-element.17, f32[4,4,128]{2,1,0:T(4,128)S(1)} %broadcast_maximum_fusion, pred[128,1024]{0,1:T(8,128)(4,1)S(1)} %iota_compare_fusion), kind=kLoop, calls=%fused_computation.4 | loop fusion | flops 10483712 | bytes 8536064 | tf_op jit(solution)/shard_map/reduce_sum | solution.py:45
  223.9 1.2 copy-done
  225.1 2.1 divide_convert_fusion
  227.2 1.0 copy.12
  (6 shorter events, 0.1 us)
Async XLA Ops:
  7.2 74.1 %all-gather.3.cloned.1.call-start = ((), (), s32[]{:S(2)}) async-start(), calls=%async_computation.1 | async-start | bytes 6684672 | tf_op jit(solution)/shard_map/all_gather | solution.py:67
  9.0 163.0 %reduce-scatter.2.cloned.1.call-start = ((), (), s32[]{:S(2)}) async-start(), calls=%async_computation.2 | async-start | bytes 7372800 | tf_op jit(solution)/shard_map/reduce_scatter | solution.py:76
  94.5 116.6 %all-gather.5.cloned.1.call-start = ((), (), s32[]{:S(2)}) async-start(), calls=%async_computation.3 | async-start | bytes 2359296 | tf_op jit(solution)/shard_map/all_gather | solution.py:91
  173.6 4.3 %copy-start.1 = (bf16[128,512]{1,0:T(8,128)(2,1)}, bf16[128,512]{1,0:T(8,128)(2,1)S(1)}, u32[]{:S(2)}) copy-start(bf16[128,512]{1,0:T(8,128)(2,1)S(1)} %get-tuple-element.9) | copy-start | bytes 393220
  219.3 5.8 %copy-start = (f32[4,1024,128,4]{2,1,3,0:T(8,128)S(1)}, f32[4,1024,128,4]{2,1,3,0:T(8,128)}, u32[]{:S(2)}) copy-start(f32[4,1024,128,4]{2,1,3,0:T(8,128)} %get-tuple-element.17) | copy-start | bytes 25165828
Sparse Core Ops, SparseCore 0:
  11.1 70.1 all-gather.2
  94.7 77.3 reduce-scatter.1
  175.1 35.9 all-gather.4

commit v2 on v1

v2 whole, which is shorter than its diff:
```python
import jax
import jax.numpy as jnp
from jax import lax
from jax.experimental import pallas as pl
from jax.experimental.pallas import tpu as pltpu
from jax.sharding import PartitionSpec as P

MODEL_WIDTH = 8192
HEAD_SIZE = 128
EPS = 1e-05
THETA = 500000.0
F32 = jnp.float32
BF16 = jnp.bfloat16
VMEM = pltpu.MemorySpace.VMEM
SMEM = pltpu.MemorySpace.SMEM
HBM = pltpu.MemorySpace.HBM
SECTIONS = 8
INSTS = 16
STRIPE = 32
EXTRA = 16
QUERY_COLS = 4 * HEAD_SIZE
KEY_AT = QUERY_COLS
VALUE_AT = QUERY_COLS + HEAD_SIZE
WIDE = QUERY_COLS + 2 * HEAD_SIZE


def params(mebibytes):
    return pltpu.CompilerParams(vmem_limit_bytes=mebibytes * 1024 * 1024)


def whole(count, space=VMEM):
    return [pl.BlockSpec(memory_space=space)] * count


def scalar():
    return pl.BlockSpec(memory_space=SMEM)


def z_shift(array, step):
    return lax.ppermute(array, "section", [(i, (i + step) % SECTIONS) for i in range(SECTIONS)])


def swap_cores(array):
    return lax.ppermute(array, "tp", [(0, 1), (1, 0)])


def stripe_kernel(core_ref, token_ref, gain_ref, out_ref):
    rows, width = token_ref.shape[1:]
    half = out_ref.shape[1]
    feature = lax.broadcasted_iota(jnp.int32, (width, half), 0)
    lane = lax.broadcasted_iota(jnp.int32, (width, half), 1)
    wanted = (lane // STRIPE) * (2 * STRIPE) + core_ref[0] * STRIPE + lane % STRIPE
    pick = jnp.where(feature == wanted, 1.0, 0.0).astype(BF16)
    floats = token_ref[0].astype(F32)
    scaled = (floats * gain_ref[...]).astype(BF16)
    out_ref[:rows] = jnp.dot(scaled, pick, preferred_element_type=F32).astype(BF16)
    squares = jnp.sum(floats * floats, axis=1, keepdims=True)
    squares = jnp.broadcast_to(squares, (rows, HEAD_SIZE)).T[:EXTRA]
    high = squares.astype(BF16)
    low = (squares - high.astype(F32)).astype(BF16)
    row = lax.broadcasted_iota(jnp.int32, squares.shape, 0)
    out_ref[rows:] = jnp.where(row == 0, high, jnp.where(row == 1, low, jnp.zeros_like(low)))


def stripes(core, tokens, gain):
    _, seq_len, width = tokens.shape
    rows = seq_len // 2
    run = pl.pallas_call(
        stripe_kernel,
        grid=(2,),
        in_specs=[
            scalar(),
            pl.BlockSpec((1, rows, width), lambda i: (0, i, 0)),
            pl.BlockSpec((1, width), lambda i: (0, 0)),
        ],
        out_specs=pl.BlockSpec((None, rows + EXTRA, width // 2), lambda i: (i, 0, 0)),
        out_shape=jax.ShapeDtypeStruct((2, rows + EXTRA, width // 2), BF16),
        compiler_params=params(16),
    )
    both = run(core, tokens, gain)
    return both[0], both[1]


def cut_far_kernel(before_ref, behind_ref, left_ref, right_ref):
    half = left_ref.shape[1]
    left_ref[...] = before_ref[:, :half]
    right_ref[...] = behind_ref[:, half:]


def cut_far(before, behind):
    rows, cols = before.shape
    shape = jax.ShapeDtypeStruct((rows, cols // 2), BF16)
    return pl.pallas_call(
        cut_far_kernel,
        in_specs=whole(2),
        out_specs=whole(2),
        out_shape=[shape, shape],
        cost_estimate=pl.CostEstimate(flops=57_000_000_000, transcendentals=0, bytes_accessed=2_000_000),
        compiler_params=params(8),
    )(before, behind)


def spread(block):
    blocks = [block] * SECTIONS
    before, behind = block, block
    for step in range(1, 4):
        before, behind = z_shift(before, 1), z_shift(behind, -1)
        blocks[SECTIONS - step], blocks[step] = before, behind
    left, right = cut_far(before, behind)
    return blocks[:4] + blocks[5:] + [z_shift(left, 1), z_shift(right, -1)]


def cut_kernel(core_ref, query_ref, key_ref, value_ref, keep_ref, send_ref):
    core = core_ref[0]
    for ref, first in ((keep_ref, core), (send_ref, 1 - core)):
        rows = pl.ds(pl.multiple_of(first * STRIPE, STRIPE), STRIPE)
        start = 0
        for source in (query_ref, key_ref, value_ref):
            ref[:, start : start + source.shape[1]] = source[rows, :]
            start += source.shape[1]


def sort_kernel(core_ref, keep_ref, other_ref, out_ref):
    first = core_ref[0] == 0
    keep, other = keep_ref[...], other_ref[...]
    groups = out_ref.shape[0] // 2
    for side in range(2):
        mine = first if side == 0 else jnp.logical_not(first)
        columns = jnp.where(mine, keep, other)
        for group in range(groups):
            start = 0
            for size, at in ((QUERY_COLS, 0), (HEAD_SIZE, KEY_AT), (HEAD_SIZE, VALUE_AT)):
                out_ref[side * groups + group, :, at : at + size] = columns[
                    :, start + group * size : start + (group + 1) * size
                ]
                start += groups * size


def gather_weights(core, query_weight, key_weight, value_matrix):
    cols = query_weight.shape[1] + key_weight.shape[1] + value_matrix.shape[1]
    shape = jax.ShapeDtypeStruct((STRIPE, cols), BF16)
    keep, send = pl.pallas_call(
        cut_kernel,
        in_specs=[scalar()] + whole(3),
        out_specs=whole(2),
        out_shape=[shape, shape],
        compiler_params=params(8),
    )(core, query_weight, key_weight, value_matrix)
    blocks = pl.pallas_call(
        sort_kernel,
        in_specs=[scalar()] + whole(2),
        out_specs=pl.BlockSpec(memory_space=VMEM),
        out_shape=jax.ShapeDtypeStruct((SECTIONS, STRIPE, WIDE), BF16),
        compiler_params=params(8),
    )(core, keep, swap_cores(send))
    blocks = lax.all_to_all(blocks, "section", 0, 0, tiled=True)
    everything = lax.all_gather(
        blocks.reshape(SECTIONS * STRIPE, WIDE), "inst", axis=0, tiled=True
    )
    return everything.reshape(INSTS, SECTIONS, STRIPE, WIDE)


def project_kernel(section_ref, core_ref, weight_hbm, *refs):
    count = 18
    block_hbm = refs[:count]
    mine_ref, send_ref, squares_ref, total, weight, near, far, weight_sems, block_sems = refs[count:]
    distances = (0, 7, 1, 6, 2, 5, 3, 4)
    order = {0: 0, 1: 1, 2: 2, 3: 3, 5: 4, 6: 5, 7: 6}
    loads = []
    for place, distance in enumerate(distances):
        source = lax.rem(section_ref[0] + distance, SECTIONS)
        load = [
            pltpu.make_async_copy(
                weight_hbm.at[:, source], weight.at[place], weight_sems.at[place]
            )
        ]
        if distance == 4:
            spots = [(14 + index, far.at[index]) for index in range(4)]
        else:
            first = 2 * order[distance]
            spots = [(first + half, near.at[first + half]) for half in range(2)]
        for index, target in spots:
            load.append(pltpu.make_async_copy(block_hbm[index], target, block_sems.at[index]))
        for copy in load:
            copy.start()
        loads.append(load)
    rows = total.shape[0] // 2
    half_cols = QUERY_COLS // 2
    first = core_ref[0] == 0
    squares = [0.0, 0.0]
    for place, distance in enumerate(distances):
        for copy in loads[place]:
            copy.wait()
        matrix = weight[place].reshape(INSTS * STRIPE, WIDE)
        for half in range(2):
            span = slice(half * rows, (half + 1) * rows)
            if distance == 4:
                block = jnp.concatenate([far[2 * half], far[2 * half + 1]], axis=1)
            else:
                block = near[2 * order[distance] + half]
            extra = block[rows:].astype(F32)
            squares[half] += extra[0:1] + extra[1:2]
            part = jnp.dot(block[:rows], matrix, preferred_element_type=F32)
            if place == 0:
                total[span] = part
                continue
            part += total[span]
            if distance != 4:
                total[span] = part
                continue
            low, high = part[:, :half_cols], part[:, half_cols:QUERY_COLS]
            mine_ref[span, :half_cols] = jnp.where(first, low, high)
            mine_ref[span, half_cols:] = part[:, KEY_AT:]
            send_ref[span, :half_cols] = jnp.where(first, high, low).astype(BF16)
            send_ref[span, half_cols:] = part[:, KEY_AT:].astype(BF16)
            squares_ref[span] = jnp.broadcast_to(squares[half], (HEAD_SIZE, rows)).T


def project(section, core, weight, blocks):
    rows = blocks[0].shape[0]
    shape = (2 * (rows - EXTRA), QUERY_COLS)
    return pl.pallas_call(
        project_kernel,
        in_specs=[scalar()] * 2 + whole(1 + len(blocks), HBM),
        out_specs=whole(3),
        out_shape=[
            jax.ShapeDtypeStruct(shape, F32),
            jax.ShapeDtypeStruct(shape, BF16),
            jax.ShapeDtypeStruct((shape[0], HEAD_SIZE), F32),
        ],
        scratch_shapes=[
            pltpu.VMEM((shape[0], WIDE), F32),
            pltpu.VMEM((SECTIONS, INSTS, STRIPE, WIDE), BF16),
            pltpu.VMEM((14, *blocks[0].shape), BF16),
            pltpu.VMEM((4, *blocks[-1].shape), BF16),
            pltpu.SemaphoreType.DMA((SECTIONS,)),
            pltpu.SemaphoreType.DMA((len(blocks),)),
        ],
        compiler_params=params(48),
    )(section, core, weight, *blocks)


def turn(head, cosine, sine):
    return head * cosine + pltpu.roll(head, HEAD_SIZE // 2, 1) * sine


def attend_kernel(core_ref, mine_ref, other_ref, squares_ref, cos_ref, sin_ref, out_ref, *scratch):
    key_ref, value_ref = scratch
    seq_len = mine_ref.shape[0]
    step = 256
    scale_by = 1.4426950408889634 / (HEAD_SIZE**0.5)
    low = F32(-1e30)
    near = lax.broadcasted_iota(jnp.int32, (step, step), 0) >= lax.broadcasted_iota(
        jnp.int32, (step, step), 1
    )
    for start in range(0, seq_len, step):
        span = slice(start, start + step)
        stop = start + step
        inverse = 1.0 / jnp.sqrt(squares_ref[span] / MODEL_WIDTH + EPS)
        inverse = jnp.concatenate([inverse] * (QUERY_COLS // HEAD_SIZE), axis=1)
        total = mine_ref[span] + other_ref[span].astype(F32)
        total = total * inverse
        cosine, sine = cos_ref[span], sin_ref[span]
        key = turn(total[:, 2 * HEAD_SIZE : 3 * HEAD_SIZE], cosine, sine).astype(BF16)
        value = total[:, 3 * HEAD_SIZE :].astype(BF16)
        key_ref[span] = key
        value_ref[span] = value
        out_ref[span, 2 * HEAD_SIZE :] = jnp.where(core_ref[0] == 0, key, value)
        query = jnp.concatenate(
            [
                turn(total[:, :HEAD_SIZE], cosine, sine),
                turn(total[:, HEAD_SIZE : 2 * HEAD_SIZE], cosine, sine),
            ],
            axis=0,
        ).astype(BF16)
        score = lax.dot_general(
            query, key_ref[:stop], (((1,), (1,)), ((), ())), preferred_element_type=F32
        )
        mask = jnp.concatenate([near, near], axis=0)
        last = jnp.where(mask, score[:, start:], low)
        score = jnp.concatenate([score[:, :start], last], axis=1) if start else last
        top = jnp.max(score, axis=1, keepdims=True)
        expo = jnp.exp2((score - top) * scale_by)
        weight_sum = jnp.sum(expo, axis=1, keepdims=True)
        mixed = jnp.dot(expo.astype(BF16), value_ref[:stop], preferred_element_type=F32)
        mixed = (mixed / weight_sum).astype(BF16)
        out_ref[span, :HEAD_SIZE] = mixed[:step]
        out_ref[span, HEAD_SIZE : 2 * HEAD_SIZE] = mixed[step:]


def attend(core, mine, other, squares, cosine, sine):
    seq_len = mine.shape[0]
    return pl.pallas_call(
        attend_kernel,
        in_specs=[scalar()] + whole(5),
        out_specs=pl.BlockSpec(memory_space=VMEM),
        out_shape=jax.ShapeDtypeStruct((seq_len, 3 * HEAD_SIZE), BF16),
        scratch_shapes=[pltpu.VMEM((seq_len, HEAD_SIZE), BF16)] * 2,
        compiler_params=params(24),
    )(core, mine, other, squares, cosine, sine)


def place_kernel(core_ref, own_ref, other_ref, attended_ref, key_ref, value_ref):
    first = core_ref[0] == 0
    rows = attended_ref.shape[1]
    pair = 2 * HEAD_SIZE
    for group in range(own_ref.shape[0] // rows):
        span = slice(group * rows, (group + 1) * rows)
        own, other = own_ref[span], other_ref[span]
        low, high = jnp.where(first, own, other), jnp.where(first, other, own)
        at = group * 2 * pair
        attended_ref[0, :, at : at + pair] = low[:, :pair]
        attended_ref[0, :, at + pair : at + 2 * pair] = high[:, :pair]
        columns = slice(group * HEAD_SIZE, (group + 1) * HEAD_SIZE)
        key_ref[0, :, columns] = low[:, pair:]
        value_ref[0, :, columns] = high[:, pair:]


def place(core, own, other, rows):
    groups = own.shape[0] // rows
    return pl.pallas_call(
        place_kernel,
        in_specs=[scalar()] + whole(2),
        out_specs=whole(3),
        out_shape=[
            jax.ShapeDtypeStruct((1, rows, groups * 4 * HEAD_SIZE), BF16),
            jax.ShapeDtypeStruct((1, rows, groups * HEAD_SIZE), BF16),
            jax.ShapeDtypeStruct((1, rows, groups * HEAD_SIZE), BF16),
        ],
        compiler_params=params(8),
    )(core, own, other)


def tables(rows):
    index = jnp.arange(HEAD_SIZE // 2).astype(F32)
    freqs = jnp.exp(index * (-2.0 / HEAD_SIZE) * jnp.log(F32(THETA)))
    angles = jnp.arange(rows).astype(F32)[:, None] * freqs[None, :]
    cosine, sine = jnp.cos(angles), jnp.sin(angles)
    return jnp.concatenate([cosine, cosine], axis=1), jnp.concatenate([-sine, sine], axis=1)


def local(tokens, norm_gain, query_weight, key_weight, value_matrix):
    seq_len = tokens.shape[1]
    section = lax.axis_index("section").astype(jnp.int32).reshape(1)
    core_index = lax.axis_index("tp").astype(jnp.int32)
    core = core_index.reshape(1)

    halves = stripes(core, tokens, norm_gain.reshape(1, -1))
    weight = gather_weights(core, query_weight, key_weight, value_matrix)
    cosine, sine = tables(seq_len)
    upper, lower = (spread(half) for half in halves)
    near = [block for pair in zip(upper[:7], lower[:7]) for block in pair]
    mine, send, squares = project(section, core, weight, near + upper[7:] + lower[7:])
    heads = attend(core, mine, swap_cores(send), squares, cosine, sine)

    heads = lax.all_to_all(heads, "section", 0, 0, tiled=True)
    half = seq_len // 2
    own = lax.dynamic_slice_in_dim(heads, core_index * half, half, 0)
    send = lax.dynamic_slice_in_dim(heads, (1 - core_index) * half, half, 0)
    return place(core, own, swap_cores(send), seq_len // SECTIONS)


def solution(mesh):
    in_specs = (
        P("inst", None, "section"),
        P("section"),
        P(("section", "inst"), "tp"),
        P(("section", "inst"), "tp"),
        P(("section", "inst"), "tp"),
    )
    out_specs = (P("inst", "section", "tp"),) * 3
    return jax.shard_map(local, mesh=mesh, in_specs=in_specs, out_specs=out_specs, check_vma=False)
```

time: 238 us -> 172 us (0.72); the launches traced: 235 us -> 171 us
  waiting for transfers between devices: 180 us -> 88.5 us
  starting transfers between devices: 0.12 us -> 38.5 us
  Pallas kernels: 0 us -> 19.8 us
  matrix products: 17.8 us -> 0 us
  other arithmetic: 16 us -> 2.25 us
    all_gather x2 -> x1, waiting for transfers between devices: 103 us -> 0.01 us  [gather_weights(): lax.all_gather(blocks.reshape(SECTIONS * STRIPE, WIDE), 'inst', axis=0, t...]
    reduce_scatter x1 -> x0, waiting for transfers between devices: 77.1 us -> none  [local(): lax.psum_scatter(part, 'section', scatter_dimension=0, tiled=True)]
    ppermute x0 -> x19, waiting for transfers between devices: none -> 58.7 us  [the longest x16 57.1 us: z_shift(): lax.ppermute(array, 'section', [(i, (i + step) % SECTIONS) for i in range...]
    ppermute x0 -> x19, starting transfers between devices: none -> 30.8 us  [the longest x16 25.1 us: z_shift(): lax.ppermute(array, 'section', [(i, (i + step) % SECTIONS) for i in range...]
    all_to_all x0 -> x2, waiting for transfers between devices: none -> 29.8 us  [the longest x1 23.5 us: local(): heads = lax.all_to_all(heads, 'section', 0, 0, tiled=True)]
    pallas_call x0 -> x8, Pallas kernels: none -> 19.8 us  [the longest x1 10.6 us: project(): pl.pallas_call(project_kernel, in_specs=[scalar()] * 2 + whole(1 + len(bl...]
    dot_general x3 -> x0, matrix products: 17.8 us -> none  [the longest x1 10 us: local(): jnp.dot(scaled, joined, preferred_element_type=jnp.float32)]
    all_to_all x0 -> x2, starting transfers between devices: none -> 7.63 us  [the longest x1 4.08 us: gather_weights(): blocks = lax.all_to_all(blocks, 'section', 0, 0, tiled=True)]
  transfers between devices with their start and end apart: 3 -> 22, of which waited for: 3 -> 13; matrix products, arithmetic and copies ran while one was open for 2% -> 1% of each run, Pallas kernels for 0% -> 2%
where the time goes in v2:
time: 172 us; the launch traced here: 171 us
  waiting for transfers between devices  88.5 us (51%)
  starting transfers between devices  38.5 us (22%)
  Pallas kernels  19.8 us (12%)
  between operations  14.1 us (8%)
  local copies, waits for them, and re-layouts  8.16 us (5%)
  other arithmetic  2.25 us (1%)
    ppermute x16, waiting for transfers between devices, z_shift(): lax.ppermute(array, 'section', [(i, (i + step) % SECTIONS) for i in range...  57.1 us
    ppermute x16, starting transfers between devices, z_shift(): lax.ppermute(array, 'section', [(i, (i + step) % SECTIONS) for i in range...  25.1 us
    all_to_all x1, waiting for transfers between devices, local(): heads = lax.all_to_all(heads, 'section', 0, 0, tiled=True)  23.5 us
    pallas_call x1, Pallas kernels, project(): pl.pallas_call(project_kernel, in_specs=[scalar()] * 2 + whole(1 + len(bl...  10.6 us
    unnamed x28, local copies, waits for them, and re-layouts  8.01 us
    all_to_all x1, waiting for transfers between devices, gather_weights(): blocks = lax.all_to_all(blocks, 'section', 0, 0, tiled=True)  6.29 us
    ppermute x3, starting transfers between devices, swap_cores(): return lax.ppermute(array, 'tp', [(0, 1), (1, 0)])  5.75 us
    all_to_all x1, starting transfers between devices, gather_weights(): blocks = lax.all_to_all(blocks, 'section', 0, 0, tiled=True)  4.08 us
  transfers between devices with their start and end apart: 22, of which 13 were waited for; matrix products, arithmetic and copies ran while one was open for 1% of the time, Pallas kernels for 2%

profile of v2, /device:TPU:1, one launch (start us, length us, event | category | flops | bytes accessed | tf_op | source)
XLA Modules:
  0.0 171.4 jit_solution(3626639840535674290)
XLA Ops:
  7.2 0.9 copy-done.8
  8.1 0.8 copy-done.9
  9.0 0.8 copy-done.10
  9.8 3.3 %collective-permute-start = (bf16[32,3072]{1,0:T(8,128)(2,1)S(1)}, bf16[32,3072]{1,0:T(8,128)(2,1)S(1)}, u32[]{:S(2)}, u32[]{:S(2)}) collective-permute-start(bf16[32,3072]{1,0:T(8,128)(2,1)S(1)} %get-tuple-element.13), channel_id=1, source_target_pairs={{0,1},{1,0},{2,3},{3,2},{4,5},{5,4},{6,7},{7,6},{8,9},{9,8},{10,11... | collective-permute-start | bytes 589832 | tf_op jit(solution)/shard_map/ppermute | solution.py:44
  13.2 1.6 copy-done
  14.8 0.7 copy-done.11
  15.4 1.5 shard_map.78
  17.0 0.1 slice_bitcast_fusion
  17.1 3.9 %collective-permute-start.1 = (bf16[528,512]{1,0:T(8,128)(2,1)S(1)}, bf16[528,512]{1,0:T(8,128)(2,1)S(1)}, u32[]{:S(2)}, u32[]{:S(2)}) collective-permute-start(bf16[528,512]{1,0:T(8,128)(2,1)S(1)} %get-tuple-element.22.refs_0_), channel_id=1, source_target_pairs={{0,14},{2,0},{4,2},{6,4},{8,6},{10,8},{12,10},{14,12},{1,15},{3,1}... | collective-permute-start | bytes 1622024 | tf_op jit(solution)/shard_map/ppermute | solution.py:40
  21.0 0.8 shard_map.77
  21.8 4.1 %all-to-all-start = ((bf16[8,32,768]{2,1,0:T(8,128)(2,1)}), bf16[8,32,768]{2,1,0:T(8,128)(2,1)S(1)}, u32[]{:S(2)}, u32[]{:S(2)}) async-start(bf16[8,32,768]{2,1,0:T(8,128)(2,1)} %shard_map.77), calls=%async_computation | async-start | bytes 786432 | tf_op jit(solution)/shard_map/all_to_all | solution.py:156
  25.9 1.4 collective-permute-start.10
  27.3 1.3 collective-permute-start.2
  28.6 4.2 %collective-permute-done.1.refs_2_ = bf16[528,512]{1,0:T(8,128)(2,1)S(1)} collective-permute-done((bf16[528,512]{1,0:T(8,128)(2,1)S(1)}, bf16[528,512]{1,0:T(8,128)(2,1)S(1)}, u32[]{:S(2)}, u32[]{:S(2)}) %collective-permute-start.1) | collective-permute-done | bytes 540704 | tf_op jit(solution)/shard_map/ppermute | solution.py:40
  32.9 4.3 %collective-permute-start.3 = (bf16[528,512]{1,0:T(8,128)(2,1)S(1)}, bf16[528,512]{1,0:T(8,128)(2,1)S(1)}, u32[]{:S(2)}, u32[]{:S(2)}) collective-permute-start(bf16[528,512]{1,0:T(8,128)(2,1)S(1)} %collective-permute-done.1.refs_2_), channel_id=1, source_target_pairs={{0,14},{2,0},{4,2},{6,4},{8,6},{10,8},{12,10},{14,12},{1,15},{3,1}... | collective-permute-start | bytes 1622024 | tf_op jit(solution)/shard_map/ppermute | solution.py:40
  37.1 6.3 %all-to-all-done = bf16[8,32,768]{2,1,0:T(8,128)(2,1)S(1)} async-done(((bf16[8,32,768]{2,1,0:T(8,128)(2,1)}), bf16[8,32,768]{2,1,0:T(8,128)(2,1)S(1)}, u32[]{:S(2)}, u32[]{:S(2)}) %all-to-all-start) | async-done | bytes 393248 | tf_op jit(solution)/shard_map/all_to_all | solution.py:156
  43.4 0.7 copy-done.12
  44.2 11.7 %collective-permute-done.10.refs_13_ = bf16[528,512]{1,0:T(8,128)(2,1)} collective-permute-done((bf16[528,512]{1,0:T(8,128)(2,1)S(1)}, bf16[528,512]{1,0:T(8,128)(2,1)}, u32[]{:S(2)}, u32[]{:S(2)}) %collective-permute-start.10) | collective-permute-done | bytes 540704 | tf_op jit(solution)/shard_map/ppermute | solution.py:40
  55.9 2.7 %collective-permute-start.4 = (bf16[528,512]{1,0:T(8,128)(2,1)S(1)}, bf16[528,512]{1,0:T(8,128)(2,1)S(1)}, u32[]{:S(2)}, u32[]{:S(2)}) collective-permute-start(bf16[528,512]{1,0:T(8,128)(2,1)S(1)} %collective-permute-done.2.refs_3_), channel_id=1, source_target_pairs={{0,14},{2,0},{4,2},{6,4},{8,6},{10,8},{12,10},{14,12},{1,15},{3,1}... | collective-permute-start | bytes 1622024 | tf_op jit(solution)/shard_map/ppermute | solution.py:40
  58.5 5.7 %collective-permute-done.3.refs_4_ = bf16[528,512]{1,0:T(8,128)(2,1)S(1)} collective-permute-done((bf16[528,512]{1,0:T(8,128)(2,1)S(1)}, bf16[528,512]{1,0:T(8,128)(2,1)S(1)}, u32[]{:S(2)}, u32[]{:S(2)}) %collective-permute-start.3) | collective-permute-done | bytes 540704 | tf_op jit(solution)/shard_map/ppermute | solution.py:40
  64.2 3.4 %collective-permute-start.5 = (bf16[528,512]{1,0:T(8,128)(2,1)S(1)}, bf16[528,512]{1,0:T(8,128)(2,1)S(1)}, u32[]{:S(2)}, u32[]{:S(2)}) collective-permute-start(bf16[528,512]{1,0:T(8,128)(2,1)S(1)} %collective-permute-done.3.refs_4_), channel_id=1, source_target_pairs={{0,14},{2,0},{4,2},{6,4},{8,6},{10,8},{12,10},{14,12},{1,15},{3,1}... | collective-permute-start | bytes 1622024 | tf_op jit(solution)/shard_map/ppermute | solution.py:40
  67.7 11.3 %collective-permute-done.11.refs_11_ = bf16[528,512]{1,0:T(8,128)(2,1)S(1)} collective-permute-done((bf16[528,512]{1,0:T(8,128)(2,1)}, bf16[528,512]{1,0:T(8,128)(2,1)S(1)}, u32[]{:S(2)}, u32[]{:S(2)}) %collective-permute-start.11) | collective-permute-done | bytes 540704 | tf_op jit(solution)/shard_map/ppermute | solution.py:40
  78.9 2.7 %collective-permute-start.6 = (bf16[528,512]{1,0:T(8,128)(2,1)S(1)}, bf16[528,512]{1,0:T(8,128)(2,1)S(1)}, u32[]{:S(2)}, u32[]{:S(2)}) collective-permute-start(bf16[528,512]{1,0:T(8,128)(2,1)S(1)} %collective-permute-done.4.refs_5_), channel_id=1, source_target_pairs={{0,14},{2,0},{4,2},{6,4},{8,6},{10,8},{12,10},{14,12},{1,15},{3,1}... | collective-permute-start | bytes 1622024 | tf_op jit(solution)/shard_map/ppermute | solution.py:40
  81.6 5.8 %collective-permute-done.5.behind_ref.refs_6_ = bf16[528,512]{1,0:T(8,128)(2,1)S(1)} collective-permute-done((bf16[528,512]{1,0:T(8,128)(2,1)S(1)}, bf16[528,512]{1,0:T(8,128)(2,1)S(1)}, u32[]{:S(2)}, u32[]{:S(2)}) %collective-permute-start.5) | collective-permute-done | bytes 540704 | tf_op jit(solution)/shard_map/ppermute | solution.py:40
  87.4 3.2 %collective-permute-done.9.before_ref.refs_8_ = bf16[528,512]{1,0:T(8,128)(2,1)S(1)} collective-permute-done((bf16[528,512]{1,0:T(8,128)(2,1)}, bf16[528,512]{1,0:T(8,128)(2,1)S(1)}, u32[]{:S(2)}, u32[]{:S(2)}) %collective-permute-start.9) | collective-permute-done | bytes 540704 | tf_op jit(solution)/shard_map/ppermute | solution.py:40
  90.6 0.9 shard_map.79
  91.7 2.7 %collective-permute-start.14 = (bf16[528,256]{1,0:T(8,128)(2,1)}, bf16[528,256]{1,0:T(8,128)(2,1)}, u32[]{:S(2)}, u32[]{:S(2)}) collective-permute-start(bf16[528,256]{1,0:T(8,128)(2,1)} %get-tuple-element.15), channel_id=1, source_target_pairs={{0,14},{2,0},{4,2},{6,4},{8,6},{10,8},{12,10},{14,12},{1,15},{3,1}... | collective-permute-start | bytes 811016 | tf_op jit(solution)/shard_map/ppermute | solution.py:40
  94.3 7.9 %collective-permute-done.12.before_ref.refs_9_ = bf16[528,512]{1,0:T(8,128)(2,1)S(1)} collective-permute-done((bf16[528,512]{1,0:T(8,128)(2,1)S(1)}, bf16[528,512]{1,0:T(8,128)(2,1)S(1)}, u32[]{:S(2)}, u32[]{:S(2)}) %collective-permute-start.12) | collective-permute-done | bytes 540704 | tf_op jit(solution)/shard_map/ppermute | solution.py:40
  102.2 0.9 shard_map.80
  103.1 0.1 copy-done.5
  103.2 0.2 copy-done.6
  103.4 2.7 %collective-permute-start.16 = (bf16[528,256]{1,0:T(8,128)(2,1)}, bf16[528,256]{1,0:T(8,128)(2,1)}, u32[]{:S(2)}, u32[]{:S(2)}) collective-permute-start(bf16[528,256]{1,0:T(8,128)(2,1)} %get-tuple-element.17), channel_id=1, source_target_pairs={{0,14},{2,0},{4,2},{6,4},{8,6},{10,8},{12,10},{14,12},{1,15},{3,1}... | collective-permute-start | bytes 811016 | tf_op jit(solution)/shard_map/ppermute | solution.py:40
  106.0 2.0 %collective-permute-done.13.refs_14_ = bf16[528,256]{1,0:T(8,128)(2,1)S(1)} collective-permute-done((bf16[528,256]{1,0:T(8,128)(2,1)}, bf16[528,256]{1,0:T(8,128)(2,1)S(1)}, u32[]{:S(2)}, u32[]{:S(2)}) %collective-permute-start.13) | collective-permute-done | bytes 270368 | tf_op jit(solution)/shard_map/ppermute | solution.py:40
  108.0 5.4 %collective-permute-done.15.refs_16_ = bf16[528,256]{1,0:T(8,128)(2,1)} collective-permute-done((bf16[528,256]{1,0:T(8,128)(2,1)}, bf16[528,256]{1,0:T(8,128)(2,1)}, u32[]{:S(2)}, u32[]{:S(2)}) %collective-permute-start.15) | collective-permute-done | bytes 270368 | tf_op jit(solution)/shard_map/ppermute | solution.py:40
  113.4 1.0 copy-done.3
  114.4 1.0 copy-done.7
  115.5 10.6 %shard_map.81 = (f32[1024,512]{1,0:T(8,128)}, bf16[1024,512]{1,0:T(8,128)(2,1)}, f32[1024,128]{1,0:T(8,128)S(1)}) custom-call(s32[1]{0:T(128)} %bitcast.1.section_ref, s32[1]{0:T(128)} %bitcast.core_ref, bf16[16,8,32,768]{3,2,1,0:T(8,128)(2,1)} %bitcast.12, bf16[528,512]{1,0:T(8,128)(2,1)S(1)} %get-tuple-element.22.refs_0_, ...), custom_call_target="tpu_custom_call" | custom-call | tf_op jit(solution)/shard_map/pallas_call | solution.py:222
  126.1 1.9 %collective-permute-start.17 = (bf16[1024,512]{1,0:T(8,128)(2,1)}, bf16[1024,512]{1,0:T(8,128)(2,1)S(1)}, u32[]{:S(2)}, u32[]{:S(2)}) collective-permute-start(bf16[1024,512]{1,0:T(8,128)(2,1)} %get-tuple-element.19), channel_id=1, source_target_pairs={{0,1},{1,0},{2,3},{3,2},{4,5},{5,4},{6,7},{7,6},{8,9},{9,8},{10,11... | collective-permute-start | bytes 3145736 | tf_op jit(solution)/shard_map/ppermute | solution.py:44
  128.0 1.9 %fusion = (f32[1024,64]{1,0:T(8,128)S(1)}, f32[1024,64]{1,0:T(8,128)S(1)}, f32[1024,64]{1,0:T(8,128)S(1)}) fusion(f32[64]{0:T(128)S(1)} %multiply_exponential_fusion, f32[1024]{0:T(1024)S(1)} %iota_convert_fusion), kind=kLoop, calls=%fused_computation.6 | loop fusion | flops 131072 | bytes 790784 | tf_op jit(solution)/shard_map/neg | solution.py:339
  129.9 0.3 pad_maximum_fusion
  130.2 0.2 collective-permute-done.17.other_ref
  130.5 4.0 %shard_map.82 = bf16[1024,384]{1,0:T(8,128)(2,1)} custom-call(s32[1]{0:T(128)} %bitcast.core_ref, f32[1024,512]{1,0:T(8,128)S(1)} %copy-done.1, bf16[1024,512]{1,0:T(8,128)(2,1)S(1)} %collective-permute-done.17.other_ref, f32[1024,128]{1,0:T(8,128)S(1)} %get-tuple-element.20.squares_ref, f32[1024,128]{1,0:T(8,128)S(1)} %get-tuple-element.28.cos_ref, ...), custom_call_target="tpu_custom_call" | custom-call | tf_op jit(solution)/shard_map/pallas_call | solution.py:293
  134.5 3.5 %all-to-all-start.1 = ((bf16[8,128,384]{2,1,0:T(8,128)(2,1)}), bf16[8,128,384]{2,1,0:T(8,128)(2,1)S(1)}, u32[]{:S(2)}, u32[]{:S(2)}) async-start(bf16[8,128,384]{2,1,0:T(8,128)(2,1)} %bitcast.7), calls=%async_computation.1 | async-start | bytes 1572864 | tf_op jit(solution)/shard_map/all_to_all | solution.py:356
  138.0 23.5 %all-to-all-done.1 = bf16[8,128,384]{2,1,0:T(8,128)(2,1)S(1)} async-done(((bf16[8,128,384]{2,1,0:T(8,128)(2,1)}), bf16[8,128,384]{2,1,0:T(8,128)(2,1)S(1)}, u32[]{:S(2)}, u32[]{:S(2)}) %all-to-all-start.1) | async-done | bytes 786464 | tf_op jit(solution)/shard_map/all_to_all | solution.py:356
  161.6 0.1 constant_dynamic-slice_fusion
  161.7 0.6 collective-permute-start.18
  162.2 1.3 collective-permute-done.18.other_ref
  163.6 1.0 shard_map.83
  (39 shorter events, 0.2 us)
Async XLA Ops:
  7.2 1.0 copy-start.8
  8.1 0.8 copy-start.9
  9.0 0.8 copy-start.10
  9.8 11.1 %collective-permute-start = (bf16[32,3072]{1,0:T(8,128)(2,1)S(1)}, bf16[32,3072]{1,0:T(8,128)(2,1)S(1)}, u32[]{:S(2)}, u32[]{:S(2)}) collective-permute-start(bf16[32,3072]{1,0:T(8,128)(2,1)S(1)} %get-tuple-element.13), channel_id=1, source_target_pairs={{0,1},{1,0},{2,3},{3,2},{4,5},{5,4},{6,7},{7,6},{8,9},{9,8},{10,11... | collective-permute-start | bytes 589832 | tf_op jit(solution)/shard_map/ppermute | solution.py:44
  13.2 1.6 copy-start
  14.8 0.7 copy-start.11
  17.1 15.8 %collective-permute-start.1 = (bf16[528,512]{1,0:T(8,128)(2,1)S(1)}, bf16[528,512]{1,0:T(8,128)(2,1)S(1)}, u32[]{:S(2)}, u32[]{:S(2)}) collective-permute-start(bf16[528,512]{1,0:T(8,128)(2,1)S(1)} %get-tuple-element.22.refs_0_), channel_id=1, source_target_pairs={{0,14},{2,0},{4,2},{6,4},{8,6},{10,8},{12,10},{14,12},{1,15},{3,1}... | collective-permute-start | bytes 1622024 | tf_op jit(solution)/shard_map/ppermute | solution.py:40
  21.0 16.1 %collective-permute-start.7 = (bf16[528,512]{1,0:T(8,128)(2,1)S(1)}, bf16[528,512]{1,0:T(8,128)(2,1)}, u32[]{:S(2)}, u32[]{:S(2)}) collective-permute-start(bf16[528,512]{1,0:T(8,128)(2,1)S(1)} %get-tuple-element.22.refs_0_), channel_id=1, source_target_pairs={{0,2},{2,4},{4,6},{6,8},{8,10},{10,12},{12,14},{14,0},{1,3},{3,5},... | collective-permute-start | bytes 1622024 | tf_op jit(solution)/shard_map/ppermute | solution.py:40
  21.8 21.6 %all-to-all-start = ((bf16[8,32,768]{2,1,0:T(8,128)(2,1)}), bf16[8,32,768]{2,1,0:T(8,128)(2,1)S(1)}, u32[]{:S(2)}, u32[]{:S(2)}) async-start(bf16[8,32,768]{2,1,0:T(8,128)(2,1)} %shard_map.77), calls=%async_computation | async-start | bytes 786432 | tf_op jit(solution)/shard_map/all_to_all | solution.py:156
  25.8 87.5 %all-gather.2.cloned.1.call-start = ((), (), s32[]{:S(2)}) async-start(), calls=%async_computation.2 | async-start | bytes 6684672 | tf_op jit(solution)/shard_map/all_gather | solution.py:157
  25.9 30.0 %collective-permute-start.10 = (bf16[528,512]{1,0:T(8,128)(2,1)S(1)}, bf16[528,512]{1,0:T(8,128)(2,1)}, u32[]{:S(2)}, u32[]{:S(2)}) collective-permute-start(bf16[528,512]{1,0:T(8,128)(2,1)S(1)} %get-tuple-element.21.refs_1_), channel_id=1, source_target_pairs={{0,2},{2,4},{4,6},{6,8},{8,10},{10,12},{12,14},{14,0},{1,3},{3,5},... | collective-permute-start | bytes 1622024 | tf_op jit(solution)/shard_map/ppermute | solution.py:40
  27.3 28.6 %collective-permute-start.2 = (bf16[528,512]{1,0:T(8,128)(2,1)S(1)}, bf16[528,512]{1,0:T(8,128)(2,1)S(1)}, u32[]{:S(2)}, u32[]{:S(2)}) collective-permute-start(bf16[528,512]{1,0:T(8,128)(2,1)S(1)} %get-tuple-element.21.refs_1_), channel_id=1, source_target_pairs={{0,14},{2,0},{4,2},{6,4},{8,6},{10,8},{12,10},{14,12},{1,15},{3,1}... | collective-permute-start | bytes 1622024 | tf_op jit(solution)/shard_map/ppermute | solution.py:40
  32.9 31.4 %collective-permute-start.3 = (bf16[528,512]{1,0:T(8,128)(2,1)S(1)}, bf16[528,512]{1,0:T(8,128)(2,1)S(1)}, u32[]{:S(2)}, u32[]{:S(2)}) collective-permute-start(bf16[528,512]{1,0:T(8,128)(2,1)S(1)} %collective-permute-done.1.refs_2_), channel_id=1, source_target_pairs={{0,14},{2,0},{4,2},{6,4},{8,6},{10,8},{12,10},{14,12},{1,15},{3,1}... | collective-permute-start | bytes 1622024 | tf_op jit(solution)/shard_map/ppermute | solution.py:40
  37.1 30.5 %collective-permute-start.8 = (bf16[528,512]{1,0:T(8,128)(2,1)}, bf16[528,512]{1,0:T(8,128)(2,1)}, u32[]{:S(2)}, u32[]{:S(2)}) collective-permute-start(bf16[528,512]{1,0:T(8,128)(2,1)} %collective-permute-done.7.refs_12_), channel_id=1, source_target_pairs={{0,2},{2,4},{4,6},{6,8},{8,10},{10,12},{12,14},{14,0},{1,3},{3,5},... | collective-permute-start | bytes 1622024 | tf_op jit(solution)/shard_map/ppermute | solution.py:40
  43.4 0.7 copy-start.12
  55.8 23.1 %collective-permute-start.11 = (bf16[528,512]{1,0:T(8,128)(2,1)}, bf16[528,512]{1,0:T(8,128)(2,1)S(1)}, u32[]{:S(2)}, u32[]{:S(2)}) collective-permute-start(bf16[528,512]{1,0:T(8,128)(2,1)} %collective-permute-done.10.refs_13_), channel_id=1, source_target_pairs={{0,2},{2,4},{4,6},{6,8},{8,10},{10,12},{12,14},{14,0},{1,3},{3,5},... | collective-permute-start | bytes 1622024 | tf_op jit(solution)/shard_map/ppermute | solution.py:40
  55.9 23.1 %collective-permute-start.4 = (bf16[528,512]{1,0:T(8,128)(2,1)S(1)}, bf16[528,512]{1,0:T(8,128)(2,1)S(1)}, u32[]{:S(2)}, u32[]{:S(2)}) collective-permute-start(bf16[528,512]{1,0:T(8,128)(2,1)S(1)} %collective-permute-done.2.refs_3_), channel_id=1, source_target_pairs={{0,14},{2,0},{4,2},{6,4},{8,6},{10,8},{12,10},{14,12},{1,15},{3,1}... | collective-permute-start | bytes 1622024 | tf_op jit(solution)/shard_map/ppermute | solution.py:40
  64.2 23.2 %collective-permute-start.5 = (bf16[528,512]{1,0:T(8,128)(2,1)S(1)}, bf16[528,512]{1,0:T(8,128)(2,1)S(1)}, u32[]{:S(2)}, u32[]{:S(2)}) collective-permute-start(bf16[528,512]{1,0:T(8,128)(2,1)S(1)} %collective-permute-done.3.refs_4_), channel_id=1, source_target_pairs={{0,14},{2,0},{4,2},{6,4},{8,6},{10,8},{12,10},{14,12},{1,15},{3,1}... | collective-permute-start | bytes 1622024 | tf_op jit(solution)/shard_map/ppermute | solution.py:40
  67.7 23.0 %collective-permute-start.9 = (bf16[528,512]{1,0:T(8,128)(2,1)}, bf16[528,512]{1,0:T(8,128)(2,1)S(1)}, u32[]{:S(2)}, u32[]{:S(2)}) collective-permute-start(bf16[528,512]{1,0:T(8,128)(2,1)} %collective-permute-done.8.refs_10_), channel_id=1, source_target_pairs={{0,2},{2,4},{4,6},{6,8},{8,10},{10,12},{12,14},{14,0},{1,3},{3,5},... | collective-permute-start | bytes 1622024 | tf_op jit(solution)/shard_map/ppermute | solution.py:40
  78.9 12.6 %copy-start.13 = (bf16[528,512]{1,0:T(8,128)(2,1)}, bf16[528,512]{1,0:T(8,128)(2,1)S(1)}, u32[]{:S(2)}) copy-start(bf16[528,512]{1,0:T(8,128)(2,1)S(1)} %collective-permute-done.11.refs_11_) | copy-start | bytes 1622020
  78.9 23.3 %collective-permute-start.12 = (bf16[528,512]{1,0:T(8,128)(2,1)S(1)}, bf16[528,512]{1,0:T(8,128)(2,1)S(1)}, u32[]{:S(2)}, u32[]{:S(2)}) collective-permute-start(bf16[528,512]{1,0:T(8,128)(2,1)S(1)} %collective-permute-done.11.refs_11_), channel_id=1, source_target_pairs={{0,2},{2,4},{4,6},{6,8},{8,10},{10,12},{12,14},{14,0},{1,3},{3,5},... | collective-permute-start | bytes 1622024 | tf_op jit(solution)/shard_map/ppermute | solution.py:40
  78.9 23.3 %collective-permute-start.6 = (bf16[528,512]{1,0:T(8,128)(2,1)S(1)}, bf16[528,512]{1,0:T(8,128)(2,1)S(1)}, u32[]{:S(2)}, u32[]{:S(2)}) collective-permute-start(bf16[528,512]{1,0:T(8,128)(2,1)S(1)} %collective-permute-done.4.refs_5_), channel_id=1, source_target_pairs={{0,14},{2,0},{4,2},{6,4},{8,6},{10,8},{12,10},{14,12},{1,15},{3,1}... | collective-permute-start | bytes 1622024 | tf_op jit(solution)/shard_map/ppermute | solution.py:40
  87.4 4.1 %copy-start.2 = (bf16[528,512]{1,0:T(8,128)(2,1)}, bf16[528,512]{1,0:T(8,128)(2,1)S(1)}, u32[]{:S(2)}) copy-start(bf16[528,512]{1,0:T(8,128)(2,1)S(1)} %collective-permute-done.5.behind_ref.refs_6_) | copy-start | bytes 1622020
  90.6 1.0 copy-start.4
  91.6 16.4 %collective-permute-start.13 = (bf16[528,256]{1,0:T(8,128)(2,1)}, bf16[528,256]{1,0:T(8,128)(2,1)S(1)}, u32[]{:S(2)}, u32[]{:S(2)}) collective-permute-start(bf16[528,256]{1,0:T(8,128)(2,1)} %get-tuple-element.14), channel_id=1, source_target_pairs={{0,2},{2,4},{4,6},{6,8},{8,10},{10,12},{12,14},{14,0},{1,3},{3,5},... | collective-permute-start | bytes 811016 | tf_op jit(solution)/shard_map/ppermute | solution.py:40
  91.7 16.3 %collective-permute-start.14 = (bf16[528,256]{1,0:T(8,128)(2,1)}, bf16[528,256]{1,0:T(8,128)(2,1)}, u32[]{:S(2)}, u32[]{:S(2)}) collective-permute-start(bf16[528,256]{1,0:T(8,128)(2,1)} %get-tuple-element.15), channel_id=1, source_target_pairs={{0,14},{2,0},{4,2},{6,4},{8,6},{10,8},{12,10},{14,12},{1,15},{3,1}... | collective-permute-start | bytes 811016 | tf_op jit(solution)/shard_map/ppermute | solution.py:40
  102.2 1.0 copy-start.5
  102.2 1.2 copy-start.6
  103.4 10.0 %collective-permute-start.15 = (bf16[528,256]{1,0:T(8,128)(2,1)}, bf16[528,256]{1,0:T(8,128)(2,1)}, u32[]{:S(2)}, u32[]{:S(2)}) collective-permute-start(bf16[528,256]{1,0:T(8,128)(2,1)} %get-tuple-element.16), channel_id=1, source_target_pairs={{0,2},{2,4},{4,6},{6,8},{8,10},{10,12},{12,14},{14,0},{1,3},{3,5},... | collective-permute-start | bytes 811016 | tf_op jit(solution)/shard_map/ppermute | solution.py:40
  103.4 10.0 %collective-permute-start.16 = (bf16[528,256]{1,0:T(8,128)(2,1)}, bf16[528,256]{1,0:T(8,128)(2,1)}, u32[]{:S(2)}, u32[]{:S(2)}) collective-permute-start(bf16[528,256]{1,0:T(8,128)(2,1)} %get-tuple-element.17), channel_id=1, source_target_pairs={{0,14},{2,0},{4,2},{6,4},{8,6},{10,8},{12,10},{14,12},{1,15},{3,1}... | collective-permute-start | bytes 811016 | tf_op jit(solution)/shard_map/ppermute | solution.py:40
  113.4 1.0 copy-start.3
  114.4 1.0 copy-start.7
  126.1 4.4 %collective-permute-start.17 = (bf16[1024,512]{1,0:T(8,128)(2,1)}, bf16[1024,512]{1,0:T(8,128)(2,1)S(1)}, u32[]{:S(2)}, u32[]{:S(2)}) collective-permute-start(bf16[1024,512]{1,0:T(8,128)(2,1)} %get-tuple-element.19), channel_id=1, source_target_pairs={{0,1},{1,0},{2,3},{3,2},{4,5},{5,4},{6,7},{7,6},{8,9},{9,8},{10,11... | collective-permute-start | bytes 3145736 | tf_op jit(solution)/shard_map/ppermute | solution.py:44
  128.0 2.5 %copy-start.1 = (f32[1024,512]{1,0:T(8,128)S(1)}, f32[1024,512]{1,0:T(8,128)}, u32[]{:S(2)}) copy-start(f32[1024,512]{1,0:T(8,128)} %get-tuple-element.18.mine_ref) | copy-start | bytes 6291460
  134.5 27.1 %all-to-all-start.1 = ((bf16[8,128,384]{2,1,0:T(8,128)(2,1)}), bf16[8,128,384]{2,1,0:T(8,128)(2,1)S(1)}, u32[]{:S(2)}, u32[]{:S(2)}) async-start(bf16[8,128,384]{2,1,0:T(8,128)(2,1)} %bitcast.7), calls=%async_computation.1 | async-start | bytes 1572864 | tf_op jit(solution)/shard_map/all_to_all | solution.py:356
  161.7 1.9 %collective-permute-start.18 = (bf16[512,384]{1,0:T(8,128)(2,1)S(1)}, bf16[512,384]{1,0:T(8,128)(2,1)S(1)}, u32[]{:S(2)}, u32[]{:S(2)}) collective-permute-start(bf16[512,384]{1,0:T(8,128)(2,1)S(1)} %get-tuple-element.23), channel_id=1, source_target_pairs={{0,1},{1,0},{2,3},{3,2},{4,5},{5,4},{6,7},{7,6},{8,9},{9,8},{10,11... | collective-permute-start | bytes 1179656 | tf_op jit(solution)/shard_map/ppermute | solution.py:44
Sparse Core Ops, SparseCore 0:
  44.3 65.6 all-gather.1

commit v3 on v2

v3 whole, which is shorter than its diff:
```python
import jax
import jax.numpy as jnp
from jax import lax
from jax.experimental import pallas as pl
from jax.experimental.pallas import tpu as pltpu
from jax.sharding import PartitionSpec as P

MODEL_WIDTH = 8192
HEAD_SIZE = 128
EPS = 1e-05
THETA = 500000.0
F32 = jnp.float32
BF16 = jnp.bfloat16
VMEM = pltpu.MemorySpace.VMEM
SMEM = pltpu.MemorySpace.SMEM
HBM = pltpu.MemorySpace.HBM
SECTIONS = 8
INSTS = 16
STRIPE = 32
EXTRA = 16
QUERY_COLS = 4 * HEAD_SIZE
KEY_AT = QUERY_COLS
VALUE_AT = QUERY_COLS + HEAD_SIZE
WIDE = QUERY_COLS + 2 * HEAD_SIZE


def params(mebibytes):
    return pltpu.CompilerParams(vmem_limit_bytes=mebibytes * 1024 * 1024)


def whole(count, space=VMEM):
    return [pl.BlockSpec(memory_space=space)] * count


def scalar():
    return pl.BlockSpec(memory_space=SMEM)


def z_shift(array, step):
    return lax.ppermute(array, "section", [(i, (i + step) % SECTIONS) for i in range(SECTIONS)])


def swap_cores(array):
    return lax.ppermute(array, "tp", [(0, 1), (1, 0)])


def stripe_kernel(core_ref, token_ref, gain_ref, *out_refs):
    width, half = token_ref.shape[2], out_refs[0].shape[1]
    rows = token_ref.shape[1] // 2
    feature = lax.broadcasted_iota(jnp.int32, (width, half), 0)
    lane = lax.broadcasted_iota(jnp.int32, (width, half), 1)
    wanted = (lane // STRIPE) * (2 * STRIPE) + core_ref[0] * STRIPE + lane % STRIPE
    pick = jnp.where(feature == wanted, 1.0, 0.0).astype(BF16)
    for index, out_ref in enumerate(out_refs):
        floats = token_ref[0, index * rows : (index + 1) * rows].astype(F32)
        scaled = (floats * gain_ref[...]).astype(BF16)
        out_ref[:rows] = jnp.dot(scaled, pick, preferred_element_type=F32).astype(BF16)
        squares = jnp.sum(floats * floats, axis=1, keepdims=True)
        squares = jnp.broadcast_to(squares, (rows, HEAD_SIZE)).T[:EXTRA]
        high = squares.astype(BF16)
        low = (squares - high.astype(F32)).astype(BF16)
        row = lax.broadcasted_iota(jnp.int32, squares.shape, 0)
        out_ref[rows:] = jnp.where(row == 0, high, jnp.where(row == 1, low, jnp.zeros_like(low)))


def stripes(core, tokens, gain):
    _, seq_len, width = tokens.shape
    shape = jax.ShapeDtypeStruct((seq_len // 2 + EXTRA, width // 2), BF16)
    return pl.pallas_call(
        stripe_kernel,
        in_specs=[scalar()] + whole(2),
        out_specs=whole(2),
        out_shape=[shape, shape],
        compiler_params=params(20),
    )(core, tokens, gain)


def cut_far_kernel(before_ref, behind_ref, left_ref, right_ref):
    half = left_ref.shape[1]
    left_ref[...] = before_ref[:, :half]
    right_ref[...] = behind_ref[:, half:]


def cut_far(before, behind):
    rows, cols = before.shape
    shape = jax.ShapeDtypeStruct((rows, cols // 2), BF16)
    return pl.pallas_call(
        cut_far_kernel,
        in_specs=whole(2),
        out_specs=whole(2),
        out_shape=[shape, shape],
        cost_estimate=pl.CostEstimate(flops=55_000_000_000, transcendentals=0, bytes_accessed=2_000_000),
        compiler_params=params(8),
    )(before, behind)


def spread(block):
    blocks = [block] * SECTIONS
    before, behind = block, block
    for step in range(1, 4):
        before, behind = z_shift(before, 1), z_shift(behind, -1)
        blocks[SECTIONS - step], blocks[step] = before, behind
    left, right = cut_far(before, behind)
    return [blocks[d] for d in NEAR], [z_shift(left, 1), z_shift(right, -1)]


def cut_kernel(core_ref, query_ref, key_ref, value_ref, keep_ref, send_ref):
    core = core_ref[0]
    for ref, first in ((keep_ref, core), (send_ref, 1 - core)):
        rows = pl.ds(pl.multiple_of(first * STRIPE, STRIPE), STRIPE)
        start = 0
        for source in (query_ref, key_ref, value_ref):
            ref[:, start : start + source.shape[1]] = source[rows, :]
            start += source.shape[1]


def sort_kernel(core_ref, keep_ref, other_ref, out_ref):
    first = core_ref[0] == 0
    keep, other = keep_ref[...], other_ref[...]
    groups = out_ref.shape[0] // 2
    for side in range(2):
        mine = first if side == 0 else jnp.logical_not(first)
        columns = jnp.where(mine, keep, other)
        for group in range(groups):
            start = 0
            for size, at in ((QUERY_COLS, 0), (HEAD_SIZE, KEY_AT), (HEAD_SIZE, VALUE_AT)):
                out_ref[side * groups + group, :, at : at + size] = columns[
                    :, start + group * size : start + (group + 1) * size
                ]
                start += groups * size


def gather_weights(core, query_weight, key_weight, value_matrix):
    cols = query_weight.shape[1] + key_weight.shape[1] + value_matrix.shape[1]
    shape = jax.ShapeDtypeStruct((STRIPE, cols), BF16)
    keep, send = pl.pallas_call(
        cut_kernel,
        in_specs=[scalar()] + whole(3),
        out_specs=whole(2),
        out_shape=[shape, shape],
        compiler_params=params(8),
    )(core, query_weight, key_weight, value_matrix)
    blocks = pl.pallas_call(
        sort_kernel,
        in_specs=[scalar()] + whole(2),
        out_specs=pl.BlockSpec(memory_space=VMEM),
        out_shape=jax.ShapeDtypeStruct((SECTIONS, STRIPE, WIDE), BF16),
        compiler_params=params(8),
    )(core, keep, swap_cores(send))
    blocks = lax.all_to_all(blocks, "section", 0, 0, tiled=True)
    everything = lax.all_gather(
        blocks.reshape(SECTIONS * STRIPE, WIDE), "inst", axis=0, tiled=True
    )
    return everything.reshape(INSTS, SECTIONS, STRIPE, WIDE)


NEAR = (0, 1, 7, 2, 6, 3, 5)


def add_squares(squares, extra):
    extra = extra.astype(F32)
    return squares + extra[0:1] + extra[1:2]


def near_kernel(section_ref, weight_hbm, *refs):
    block_hbm = refs[:14]
    total_ref, squares_ref, weight, blocks, total, weight_sems, block_sems = refs[14:]
    loads = []
    for place, distance in enumerate(NEAR):
        source = lax.rem(section_ref[0] + distance, SECTIONS)
        load = [
            pltpu.make_async_copy(
                weight_hbm.at[:, source], weight.at[place], weight_sems.at[place]
            )
        ]
        for index in (2 * place, 2 * place + 1):
            load.append(
                pltpu.make_async_copy(block_hbm[index], blocks.at[index], block_sems.at[index])
            )
        loads.append(load)
    ahead = 2
    for load in loads[:ahead]:
        for copy in load:
            copy.start()
    rows = total_ref.shape[0] // 2
    width = block_hbm[0].shape[1]
    squares = [jnp.zeros((1, width), F32)] * 2
    for place in range(len(NEAR)):
        for copy in loads[place]:
            copy.wait()
        if place + ahead < len(NEAR):
            for copy in loads[place + ahead]:
                copy.start()
        matrix = weight[place].reshape(INSTS * STRIPE, WIDE)
        for half in range(2):
            span = slice(half * rows, (half + 1) * rows)
            block = blocks.at[2 * place + half]
            part = jnp.dot(block[:rows], matrix, preferred_element_type=F32)
            squares[half] = add_squares(squares[half], block[rows:])
            if place == 0:
                total[span] = part
            elif place + 1 < len(NEAR):
                total[span] += part
            else:
                total_ref[span] = (part + total[span]).astype(BF16)
    for half in range(2):
        squares_ref[half * 8 : (half + 1) * 8] = jnp.broadcast_to(squares[half], (8, width))


def near_sum(section, weight, blocks):
    rows, width = blocks[0].shape
    seq_len = 2 * (rows - EXTRA)
    return pl.pallas_call(
        near_kernel,
        in_specs=[scalar()] + whole(1 + len(blocks), HBM),
        out_specs=whole(2),
        out_shape=[
            jax.ShapeDtypeStruct((seq_len, WIDE), BF16),
            jax.ShapeDtypeStruct((16, width), F32),
        ],
        scratch_shapes=[
            pltpu.VMEM((len(NEAR), INSTS, STRIPE, WIDE), BF16),
            pltpu.VMEM((len(blocks), *blocks[0].shape), BF16),
            pltpu.VMEM((seq_len, WIDE), F32),
            pltpu.SemaphoreType.DMA((len(NEAR),)),
            pltpu.SemaphoreType.DMA((len(blocks),)),
        ],
        compiler_params=params(60),
    )(section, weight, *blocks)


def far_kernel(section_ref, core_ref, weight_hbm, total_hbm, sums_ref, *refs):
    block_hbm = refs[:4]
    mine_hbm, send_hbm, squares_ref = refs[4:7]
    weight, total, blocks, out, sems, block_sems, out_sems = refs[7:]
    rows = total.shape[1]
    source = lax.rem(section_ref[0] + SECTIONS // 2, SECTIONS)
    load = pltpu.make_async_copy(weight_hbm.at[:, source], weight, sems.at[2])
    load.start()
    loads = []
    for half in range(2):
        span = slice(half * rows, (half + 1) * rows)
        group = [pltpu.make_async_copy(total_hbm.at[span], total.at[half], sems.at[half])]
        for index in (2 * half, 2 * half + 1):
            group.append(
                pltpu.make_async_copy(block_hbm[index], blocks.at[index], block_sems.at[index])
            )
        for copy in group:
            copy.start()
        loads.append(group)
    load.wait()
    matrix = weight[...].reshape(INSTS * STRIPE, WIDE)
    half_cols = QUERY_COLS // 2
    first = core_ref[0] == 0
    stores = []
    for half in range(2):
        span = slice(half * rows, (half + 1) * rows)
        for copy in loads[half]:
            copy.wait()
        block = jnp.concatenate([blocks[2 * half], blocks[2 * half + 1]], axis=1)
        part = jnp.dot(block[:rows], matrix, preferred_element_type=F32)
        part = (part + total[half].astype(F32)).astype(BF16)
        low, high = part[:, :half_cols], part[:, half_cols:QUERY_COLS]
        both = part[:, KEY_AT:]
        for side, (query, target) in enumerate(
            (
                (jnp.where(first, high, low), send_hbm),
                (jnp.where(first, low, high), mine_hbm),
            )
        ):
            index = 2 * half + side
            out[index, :, :half_cols] = query
            out[index, :, half_cols:] = both
            store = pltpu.make_async_copy(out.at[index], target.at[span], out_sems.at[index])
            store.start()
            stores.append(store)
        at = slice(half * 8, (half + 1) * 8)
        squares_ref[at] = add_squares(sums_ref[at], block[rows:])
    for store in stores:
        store.wait()


def far_sum(section, core, weight, total, sums, blocks):
    seq_len = total.shape[0]
    rows = seq_len // 2
    shape = jax.ShapeDtypeStruct((seq_len, QUERY_COLS), BF16)
    return pl.pallas_call(
        far_kernel,
        in_specs=[scalar()] * 2 + whole(2, HBM) + whole(1) + whole(len(blocks), HBM),
        out_specs=whole(2, HBM) + whole(1),
        out_shape=[shape, shape, jax.ShapeDtypeStruct(sums.shape, F32)],
        scratch_shapes=[
            pltpu.VMEM((INSTS, STRIPE, WIDE), BF16),
            pltpu.VMEM((2, rows, WIDE), BF16),
            pltpu.VMEM((4, *blocks[0].shape), BF16),
            pltpu.VMEM((4, rows, QUERY_COLS), BF16),
            pltpu.SemaphoreType.DMA((3,)),
            pltpu.SemaphoreType.DMA((4,)),
            pltpu.SemaphoreType.DMA((4,)),
        ],
        compiler_params=params(60),
    )(section, core, weight, total, sums, *blocks)


def turn(head, cosine, sine):
    return head * cosine + pltpu.roll(head, HEAD_SIZE // 2, 1) * sine


def attend_kernel(
    section_ref, core_ref, mine_ref, other_ref, squares_ref, cos_ref, sin_ref, *refs
):
    piece_refs, (out_ref, key_ref, value_ref) = refs[:SECTIONS], refs[SECTIONS:]
    seq_len = mine_ref.shape[0]
    step = 256
    scale_by = 1.4426950408889634 / (HEAD_SIZE**0.5)
    low = F32(-1e30)
    near = lax.broadcasted_iota(jnp.int32, (step, step), 0) >= lax.broadcasted_iota(
        jnp.int32, (step, step), 1
    )
    for start in range(0, seq_len, step):
        span = slice(start, start + step)
        stop = start + step
        half = squares_ref.shape[1]
        at = start // half * 8
        squares = squares_ref[at : at + 1, start % half : start % half + step]
        inverse = 1.0 / jnp.sqrt(squares / MODEL_WIDTH + EPS)
        inverse = jnp.broadcast_to(inverse, (HEAD_SIZE, step)).T
        inverse = jnp.concatenate([inverse] * (QUERY_COLS // HEAD_SIZE), axis=1)
        total = mine_ref[span].astype(F32) + other_ref[span].astype(F32)
        total = total * inverse
        cosine, sine = cos_ref[span], sin_ref[span]
        key = turn(total[:, 2 * HEAD_SIZE : 3 * HEAD_SIZE], cosine, sine).astype(BF16)
        value = total[:, 3 * HEAD_SIZE :].astype(BF16)
        key_ref[span] = key
        value_ref[span] = value
        out_ref[span, 2 * HEAD_SIZE :] = jnp.where(core_ref[0] == 0, key, value)
        query = jnp.concatenate(
            [
                turn(total[:, :HEAD_SIZE], cosine, sine),
                turn(total[:, HEAD_SIZE : 2 * HEAD_SIZE], cosine, sine),
            ],
            axis=0,
        ).astype(BF16)
        score = lax.dot_general(
            query, key_ref[:stop], (((1,), (1,)), ((), ())), preferred_element_type=F32
        )
        mask = jnp.concatenate([near, near], axis=0)
        last = jnp.where(mask, score[:, start:], low)
        score = jnp.concatenate([score[:, :start], last], axis=1) if start else last
        top = jnp.max(score, axis=1, keepdims=True)
        expo = jnp.exp2((score - top) * scale_by)
        weight_sum = jnp.sum(expo, axis=1, keepdims=True)
        mixed = jnp.dot(expo.astype(BF16), value_ref[:stop], preferred_element_type=F32)
        mixed = (mixed / weight_sum).astype(BF16)
        out_ref[span, :HEAD_SIZE] = mixed[:step]
        out_ref[span, HEAD_SIZE : 2 * HEAD_SIZE] = mixed[step:]


    rows = piece_refs[0].shape[0]
    for turn_of, piece_ref in enumerate(piece_refs):
        target = lax.rem(section_ref[0] + turn_of + 4 * core_ref[0], SECTIONS)
        piece_ref[...] = out_ref[pl.ds(pl.multiple_of(target * rows, rows), rows)]


def attend(section, core, mine, other, squares, cosine, sine):
    seq_len = mine.shape[0]
    shape = (seq_len, 3 * HEAD_SIZE)
    piece = jax.ShapeDtypeStruct((seq_len // SECTIONS, shape[1]), BF16)
    return pl.pallas_call(
        attend_kernel,
        in_specs=[scalar()] * 2 + whole(5),
        out_specs=whole(SECTIONS),
        out_shape=[piece] * SECTIONS,
        scratch_shapes=[pltpu.VMEM(shape, BF16)] + [pltpu.VMEM((seq_len, HEAD_SIZE), BF16)] * 2,
        compiler_params=params(24),
    )(section, core, mine, other, squares, cosine, sine)


def send_rows(pieces):
    arrived = []
    for turn_of, piece in enumerate(pieces):
        pairs = [
            (2 * s + c, 2 * ((s + turn_of + 4 * c) % SECTIONS) + s // 4)
            for s in range(SECTIONS)
            for c in range(2)
        ]
        arrived.append(lax.ppermute(piece, ("section", "tp"), pairs))
    return arrived


def place_kernel(section_ref, core_ref, *refs):
    arrived = refs[:SECTIONS]
    attended_ref, key_ref, value_ref, pair_sems, head_sems = refs[SECTIONS:]
    pair = 2 * HEAD_SIZE
    copies = []
    for turn_of, piece in enumerate(arrived):
        source = lax.rem(section_ref[0] + SECTIONS - turn_of, SECTIONS)
        group = lax.rem(source, 4)
        from_first = source // 4 == core_ref[0]
        at = group * (2 * pair) + jnp.where(from_first, 0, pair)
        copy = pltpu.make_async_copy(
            piece.at[:, :pair],
            attended_ref.at[0, :, pl.ds(pl.multiple_of(at, HEAD_SIZE), pair)],
            pair_sems.at[turn_of],
        )
        copy.start()
        columns = pl.ds(pl.multiple_of(group * HEAD_SIZE, HEAD_SIZE), HEAD_SIZE)
        to_key = pltpu.make_async_copy(
            piece.at[:, pair:], key_ref.at[0, :, columns], head_sems.at[turn_of]
        )
        to_value = pltpu.make_async_copy(
            piece.at[:, pair:], value_ref.at[0, :, columns], head_sems.at[turn_of]
        )
        pl.when(from_first)(to_key.start)
        pl.when(jnp.logical_not(from_first))(to_value.start)
        copies.append((copy, to_key, to_value, from_first))
    for copy, to_key, to_value, from_first in copies:
        copy.wait()
        pl.when(from_first)(to_key.wait)
        pl.when(jnp.logical_not(from_first))(to_value.wait)


def place(section, core, arrived):
    rows = arrived[0].shape[0]
    return pl.pallas_call(
        place_kernel,
        in_specs=[scalar()] * 2 + whole(SECTIONS, pl.ANY),
        out_specs=whole(3, pl.ANY),
        out_shape=[
            jax.ShapeDtypeStruct((1, rows, 16 * HEAD_SIZE), BF16),
            jax.ShapeDtypeStruct((1, rows, 4 * HEAD_SIZE), BF16),
            jax.ShapeDtypeStruct((1, rows, 4 * HEAD_SIZE), BF16),
        ],
        scratch_shapes=[pltpu.SemaphoreType.DMA((SECTIONS,))] * 2,
        compiler_params=params(8),
    )(section, core, *arrived)


def tables(rows):
    index = jnp.arange(HEAD_SIZE // 2).astype(F32)
    freqs = jnp.exp(index * (-2.0 / HEAD_SIZE) * jnp.log(F32(THETA)))
    angles = jnp.arange(rows).astype(F32)[:, None] * freqs[None, :]
    cosine, sine = jnp.cos(angles), jnp.sin(angles)
    return jnp.concatenate([cosine, cosine], axis=1), jnp.concatenate([-sine, sine], axis=1)


def local(tokens, norm_gain, query_weight, key_weight, value_matrix):
    seq_len = tokens.shape[1]
    section = lax.axis_index("section").astype(jnp.int32).reshape(1)
    core_index = lax.axis_index("tp").astype(jnp.int32)
    core = core_index.reshape(1)

    halves = stripes(core, tokens, norm_gain.reshape(1, -1))
    weight = gather_weights(core, query_weight, key_weight, value_matrix)
    cosine, sine = tables(seq_len)
    (upper, upper_far), (lower, lower_far) = (spread(half) for half in halves)
    near = [block for pair in zip(upper, lower) for block in pair]
    total, sums = near_sum(section, weight, near)
    mine, send, squares = far_sum(section, core, weight, total, sums, upper_far + lower_far)
    pieces = attend(section, core, mine, swap_cores(send), squares, cosine, sine)
    return place(section, core, send_rows(pieces))


def solution(mesh):
    in_specs = (
        P("inst", None, "section"),
        P("section"),
        P(("section", "inst"), "tp"),
        P(("section", "inst"), "tp"),
        P(("section", "inst"), "tp"),
    )
    out_specs = (P("inst", "section", "tp"),) * 3
    return jax.shard_map(local, mesh=mesh, in_specs=in_specs, out_specs=out_specs, check_vma=False)
```

time: 172 us -> 164 us (0.953)
  waiting for transfers between devices: 88.5 us -> 66.3 us
  starting transfers between devices: 38.5 us -> 50.6 us
  Pallas kernels: 19.8 us -> 22.7 us
    all_to_all x1 -> x0, waiting for transfers between devices: 23.5 us -> none  [local(): heads = lax.all_to_all(heads, 'section', 0, 0, tiled=True)]
    ppermute x0 -> x8, starting transfers between devices: none -> 18 us  [send_rows(): arrived.append(lax.ppermute(piece, ('section', 'tp'), pairs))]
    ppermute x16, waiting for transfers between devices: 57.1 us -> 50.3 us  [z_shift(): lax.ppermute(array, 'section', [(i, (i + step) % SECTIONS) for i in range...]
    ppermute x0 -> x8, waiting for transfers between devices: none -> 6.58 us  [send_rows(): arrived.append(lax.ppermute(piece, ('section', 'tp'), pairs))]
    ppermute x16, starting transfers between devices: 25.1 us -> 19.5 us  [z_shift(): lax.ppermute(array, 'section', [(i, (i + step) % SECTIONS) for i in range...]
    pallas_call x4 -> x5, Pallas kernels: 17.1 us -> 21 us  [the longest x1 9.5 us: near_sum(): pl.pallas_call(near_kernel, in_specs=[scalar()] + whole(1 + len(blocks),...]
    all_to_all x1 -> x0, starting transfers between devices: 3.55 us -> none  [local(): heads = lax.all_to_all(heads, 'section', 0, 0, tiled=True)]
    all_to_all x1, starting transfers between devices: 4.08 us -> 6.45 us  [gather_weights(): blocks = lax.all_to_all(blocks, 'section', 0, 0, tiled=True)]
  transfers between devices with their start and end apart: 22 -> 28, of which waited for: 13 -> 14; matrix products, arithmetic and copies ran while one was open for 1% -> 1% of each run, Pallas kernels for 2% -> 7%
where the time goes in v3:
time: 164 us
  waiting for transfers between devices  66.3 us (40%)
  starting transfers between devices  50.6 us (31%)
  Pallas kernels  22.7 us (14%)
  between operations  14.4 us (9%)
  local copies, waits for them, and re-layouts  7.57 us (5%)
  other arithmetic  2.25 us (1%)
    ppermute x16, waiting for transfers between devices, z_shift(): lax.ppermute(array, 'section', [(i, (i + step) % SECTIONS) for i in range...  50.3 us
    ppermute x16, starting transfers between devices, z_shift(): lax.ppermute(array, 'section', [(i, (i + step) % SECTIONS) for i in range...  19.5 us
    ppermute x8, starting transfers between devices, send_rows(): arrived.append(lax.ppermute(piece, ('section', 'tp'), pairs))  18 us
    pallas_call x1, Pallas kernels, near_sum(): pl.pallas_call(near_kernel, in_specs=[scalar()] + whole(1 + len(blocks),...  9.5 us
    all_to_all x1, waiting for transfers between devices, gather_weights(): blocks = lax.all_to_all(blocks, 'section', 0, 0, tiled=True)  8.14 us
    unnamed x52, local copies, waits for them, and re-layouts  7.57 us
    ppermute x2, starting transfers between devices, swap_cores(): return lax.ppermute(array, 'tp', [(0, 1), (1, 0)])  6.6 us
    ppermute x8, waiting for transfers between devices, send_rows(): arrived.append(lax.ppermute(piece, ('section', 'tp'), pairs))  6.58 us
  transfers between devices with their start and end apart: 28, of which 14 were waited for; matrix products, arithmetic and copies ran while one was open for 1% of the time, Pallas kernels for 7%

profile of v3, /device:TPU:1, one launch (start us, length us, event | category | flops | bytes accessed | tf_op | source)
XLA Modules:
  0.0 163.8 jit_solution(15261741002623246658)
XLA Ops:
  7.2 0.9 copy-done.8
  8.1 0.8 copy-done.9
  9.0 0.8 copy-done.10
  9.8 3.3 %collective-permute-start = (bf16[32,3072]{1,0:T(8,128)(2,1)S(1)}, bf16[32,3072]{1,0:T(8,128)(2,1)S(1)}, u32[]{:S(2)}, u32[]{:S(2)}) collective-permute-start(bf16[32,3072]{1,0:T(8,128)(2,1)S(1)} %get-tuple-element.25), channel_id=1, source_target_pairs={{0,1},{1,0},{2,3},{3,2},{4,5},{5,4},{6,7},{7,6},{8,9},{9,8},{10,11... | collective-permute-start | bytes 589832 | tf_op jit(solution)/shard_map/ppermute | solution.py:44
  13.2 1.1 collective-permute-done.other_ref
  14.2 0.8 shard_map.77
  15.0 6.5 %all-to-all-start = ((bf16[8,32,768]{2,1,0:T(8,128)(2,1)}), bf16[8,32,768]{2,1,0:T(8,128)(2,1)S(1)}, u32[]{:S(2)}, u32[]{:S(2)}) async-start(bf16[8,32,768]{2,1,0:T(8,128)(2,1)} %shard_map.77), calls=%async_computation | async-start | bytes 786432 | tf_op jit(solution)/shard_map/all_to_all | solution.py:150
  21.5 1.6 copy-done
  23.1 0.7 copy-done.12
  23.8 1.5 shard_map.78
  25.3 1.5 collective-permute-start.3
  26.8 1.3 collective-permute-start.1
  28.1 8.1 %all-to-all-done = bf16[8,32,768]{2,1,0:T(8,128)(2,1)S(1)} async-done(((bf16[8,32,768]{2,1,0:T(8,128)(2,1)}), bf16[8,32,768]{2,1,0:T(8,128)(2,1)S(1)}, u32[]{:S(2)}, u32[]{:S(2)}) %all-to-all-start) | async-done | bytes 393248 | tf_op jit(solution)/shard_map/all_to_all | solution.py:150
  36.3 0.7 copy-done.13
  37.1 1.5 collective-permute-start.4
  38.6 6.0 %collective-permute-done.3.refs_4_ = bf16[528,512]{1,0:T(8,128)(2,1)S(1)} collective-permute-done((bf16[528,512]{1,0:T(8,128)(2,1)S(1)}, bf16[528,512]{1,0:T(8,128)(2,1)S(1)}, u32[]{:S(2)}, u32[]{:S(2)}) %collective-permute-start.3) | collective-permute-done | bytes 540704 | tf_op jit(solution)/shard_map/ppermute | solution.py:40
  44.6 2.7 %collective-permute-start.5 = (bf16[528,512]{1,0:T(8,128)(2,1)S(1)}, bf16[528,512]{1,0:T(8,128)(2,1)S(1)}, u32[]{:S(2)}, u32[]{:S(2)}) collective-permute-start(bf16[528,512]{1,0:T(8,128)(2,1)S(1)} %collective-permute-done.1.refs_2_), channel_id=1, source_target_pairs={{0,14},{2,0},{4,2},{6,4},{8,6},{10,8},{12,10},{14,12},{1,15},{3,1}... | collective-permute-start | bytes 1622024 | tf_op jit(solution)/shard_map/ppermute | solution.py:40
  47.3 7.7 %collective-permute-done.2.refs_3_ = bf16[528,512]{1,0:T(8,128)(2,1)S(1)} collective-permute-done((bf16[528,512]{1,0:T(8,128)(2,1)S(1)}, bf16[528,512]{1,0:T(8,128)(2,1)S(1)}, u32[]{:S(2)}, u32[]{:S(2)}) %collective-permute-start.2) | collective-permute-done | bytes 540704 | tf_op jit(solution)/shard_map/ppermute | solution.py:40
  55.0 2.2 %collective-permute-start.6 = (bf16[528,512]{1,0:T(8,128)(2,1)S(1)}, bf16[528,512]{1,0:T(8,128)(2,1)S(1)}, u32[]{:S(2)}, u32[]{:S(2)}) collective-permute-start(bf16[528,512]{1,0:T(8,128)(2,1)S(1)} %collective-permute-done.2.refs_3_), channel_id=1, source_target_pairs={{0,14},{2,0},{4,2},{6,4},{8,6},{10,8},{12,10},{14,12},{1,15},{3,1}... | collective-permute-start | bytes 1622024 | tf_op jit(solution)/shard_map/ppermute | solution.py:40
  57.2 10.6 %collective-permute-done.7.refs_8_ = bf16[528,512]{1,0:T(8,128)(2,1)S(1)} collective-permute-done((bf16[528,512]{1,0:T(8,128)(2,1)S(1)}, bf16[528,512]{1,0:T(8,128)(2,1)S(1)}, u32[]{:S(2)}, u32[]{:S(2)}) %collective-permute-start.7) | collective-permute-done | bytes 540704 | tf_op jit(solution)/shard_map/ppermute | solution.py:40
  67.8 2.7 %collective-permute-start.9 = (bf16[528,512]{1,0:T(8,128)(2,1)S(1)}, bf16[528,512]{1,0:T(8,128)(2,1)S(1)}, u32[]{:S(2)}, u32[]{:S(2)}) collective-permute-start(bf16[528,512]{1,0:T(8,128)(2,1)S(1)} %collective-permute-done.5.refs_6_), channel_id=1, source_target_pairs={{0,14},{2,0},{4,2},{6,4},{8,6},{10,8},{12,10},{14,12},{1,15},{3,1}... | collective-permute-start | bytes 1622024 | tf_op jit(solution)/shard_map/ppermute | solution.py:40
  70.5 7.6 %collective-permute-done.6.refs_7_ = bf16[528,512]{1,0:T(8,128)(2,1)S(1)} collective-permute-done((bf16[528,512]{1,0:T(8,128)(2,1)S(1)}, bf16[528,512]{1,0:T(8,128)(2,1)S(1)}, u32[]{:S(2)}, u32[]{:S(2)}) %collective-permute-start.6) | collective-permute-done | bytes 540704 | tf_op jit(solution)/shard_map/ppermute | solution.py:40
  78.1 2.2 %collective-permute-start.10 = (bf16[528,512]{1,0:T(8,128)(2,1)S(1)}, bf16[528,512]{1,0:T(8,128)(2,1)S(1)}, u32[]{:S(2)}, u32[]{:S(2)}) collective-permute-start(bf16[528,512]{1,0:T(8,128)(2,1)S(1)} %collective-permute-done.6.refs_7_), channel_id=1, source_target_pairs={{0,14},{2,0},{4,2},{6,4},{8,6},{10,8},{12,10},{14,12},{1,15},{3,1}... | collective-permute-start | bytes 1622024 | tf_op jit(solution)/shard_map/ppermute | solution.py:40
  80.3 10.7 %collective-permute-done.11.refs_12_.before_ref = bf16[528,512]{1,0:T(8,128)(2,1)S(1)} collective-permute-done((bf16[528,512]{1,0:T(8,128)(2,1)S(1)}, bf16[528,512]{1,0:T(8,128)(2,1)S(1)}, u32[]{:S(2)}, u32[]{:S(2)}) %collective-permute-start.11) | collective-permute-done | bytes 540704 | tf_op jit(solution)/shard_map/ppermute | solution.py:40
  91.1 0.9 shard_map.80
  92.6 2.3 %collective-permute-start.14 = (bf16[528,256]{1,0:T(8,128)(2,1)S(1)}, bf16[528,256]{1,0:T(8,128)(2,1)S(1)}, u32[]{:S(2)}, u32[]{:S(2)}) collective-permute-start(bf16[528,256]{1,0:T(8,128)(2,1)S(1)} %get-tuple-element.31), channel_id=1, source_target_pairs={{0,14},{2,0},{4,2},{6,4},{8,6},{10,8},{12,10},{14,12},{1,15},{3,1}... | collective-permute-start | bytes 811016 | tf_op jit(solution)/shard_map/ppermute | solution.py:40
  94.9 6.3 %collective-permute-done.10.refs_11_.behind_ref = bf16[528,512]{1,0:T(8,128)(2,1)S(1)} collective-permute-done((bf16[528,512]{1,0:T(8,128)(2,1)S(1)}, bf16[528,512]{1,0:T(8,128)(2,1)S(1)}, u32[]{:S(2)}, u32[]{:S(2)}) %collective-permute-start.10) | collective-permute-done | bytes 540704 | tf_op jit(solution)/shard_map/ppermute | solution.py:40
  101.2 1.3 collective-permute-done.12.refs_13_.before_ref
  102.6 0.8 copy-done.7
  103.4 0.6 collective-permute-start.15
  104.0 2.1 %collective-permute-start.16 = (bf16[528,256]{1,0:T(8,128)(2,1)S(1)}, bf16[528,256]{1,0:T(8,128)(2,1)S(1)}, u32[]{:S(2)}, u32[]{:S(2)}) collective-permute-start(bf16[528,256]{1,0:T(8,128)(2,1)S(1)} %get-tuple-element.33), channel_id=1, source_target_pairs={{0,14},{2,0},{4,2},{6,4},{8,6},{10,8},{12,10},{14,12},{1,15},{3,1}... | collective-permute-start | bytes 811016 | tf_op jit(solution)/shard_map/ppermute | solution.py:40
  106.0 9.5 %shard_map.79 = (bf16[1024,768]{1,0:T(8,128)(2,1)}, f32[16,512]{1,0:T(8,128)}) custom-call(s32[1]{0:T(128)} %bitcast.section_ref, bf16[16,8,32,768]{3,2,1,0:T(8,128)(2,1)} %bitcast.6, bf16[528,512]{1,0:T(8,128)(2,1)} %copy-done.2, bf16[528,512]{1,0:T(8,128)(2,1)} %copy-done.3, bf16[528,512]{1,0:T(8,128)(2,1)} %copy-done.15, bf16[528,512]{1,0:T(8,128)(2,1)} %copy-done.16, ...), custom_call_target="tpu_custom_call" | custom-call | tf_op jit(solution)/shard_map/pallas_call | solution.py:213
  115.6 0.6 copy-done.22
  116.5 5.4 %shard_map.82 = (bf16[1024,512]{1,0:T(8,128)(2,1)}, bf16[1024,512]{1,0:T(8,128)(2,1)}, f32[16,512]{1,0:T(8,128)}) custom-call(s32[1]{0:T(128)} %bitcast.section_ref, s32[1]{0:T(128)} %bitcast.1.core_ref, bf16[16,8,32,768]{3,2,1,0:T(8,128)(2,1)} %bitcast.7, bf16[1024,768]{1,0:T(8,128)(2,1)} %get-tuple-element.28.total_hbm, ...), custom_call_target="tpu_custom_call" | custom-call | tf_op jit(solution)/shard_map/pallas_call | solution.py:287
  122.0 3.3 %collective-permute-start.17 = (bf16[1024,512]{1,0:T(8,128)(2,1)}, bf16[1024,512]{1,0:T(8,128)(2,1)S(1)}, u32[]{:S(2)}, u32[]{:S(2)}) collective-permute-start(bf16[1024,512]{1,0:T(8,128)(2,1)} %get-tuple-element.35), channel_id=1, source_target_pairs={{0,1},{1,0},{2,3},{3,2},{4,5},{5,4},{6,7},{7,6},{8,9},{9,8},{10,11... | collective-permute-start | bytes 3145736 | tf_op jit(solution)/shard_map/ppermute | solution.py:44
  125.3 1.9 %fusion = (f32[1024,64]{1,0:T(8,128)S(1)}, f32[1024,64]{1,0:T(8,128)S(1)}, f32[1024,64]{1,0:T(8,128)S(1)}) fusion(f32[64]{0:T(128)S(1)} %multiply_exponential_fusion, f32[1024]{0:T(1024)S(1)} %iota_convert_fusion), kind=kLoop, calls=%fused_computation.4 | loop fusion | flops 131072 | bytes 790784 | tf_op jit(solution)/shard_map/neg | solution.py:444
  127.8 3.6 %shard_map.83 = (bf16[128,384]{1,0:T(8,128)(2,1)S(1)}, bf16[128,384]{1,0:T(8,128)(2,1)S(1)}, bf16[128,384]{1,0:T(8,128)(2,1)S(1)}, bf16[128,384]{1,0:T(8,128)(2,...) custom-call(s32[1]{0:T(128)} %bitcast.section_ref, ...), custom_call_target="tpu_custom_call" | custom-call | tf_op jit(solution)/shard_map/pallas_call | solution.py:369
  131.3 5.0 %collective-permute-start.18 = (bf16[128,384]{1,0:T(8,128)(2,1)S(1)}, bf16[128,384]{1,0:T(8,128)(2,1)S(1)}, u32[]{:S(2)}, u32[]{:S(2)}) collective-permute-start(bf16[128,384]{1,0:T(8,128)(2,1)S(1)} %get-tuple-element.37), channel_id=1, source_target_pairs={{0,0},{1,8},{2,2},{3,10},{4,4},{5,12},{6,6},{7,14},{8,9},{9,1},{10... | collective-permute-start | bytes 294920 | tf_op jit(solution)/shard_map/ppermute | solution.py:387
  136.4 1.9 %collective-permute-start.20 = (bf16[128,384]{1,0:T(8,128)(2,1)S(1)}, bf16[128,384]{1,0:T(8,128)(2,1)S(1)}, u32[]{:S(2)}, u32[]{:S(2)}) collective-permute-start(bf16[128,384]{1,0:T(8,128)(2,1)S(1)} %get-tuple-element.39), channel_id=1, source_target_pairs={{0,4},{1,12},{2,6},{3,14},{4,8},{5,0},{6,10},{7,2},{8,13},{9,5},{1... | collective-permute-start | bytes 294920 | tf_op jit(solution)/shard_map/ppermute | solution.py:387
  138.3 1.0 collective-permute-start.21
  139.4 2.2 %collective-permute-start.22 = (bf16[128,384]{1,0:T(8,128)(2,1)S(1)}, bf16[128,384]{1,0:T(8,128)(2,1)S(1)}, u32[]{:S(2)}, u32[]{:S(2)}) collective-permute-start(bf16[128,384]{1,0:T(8,128)(2,1)S(1)} %get-tuple-element.41), channel_id=1, source_target_pairs={{0,8},{1,0},{2,10},{3,2},{4,12},{5,4},{6,14},{7,6},{8,1},{9,9},{10... | collective-permute-start | bytes 294920 | tf_op jit(solution)/shard_map/ppermute | solution.py:387
  142.2 4.4 %collective-permute-start.23 = (bf16[128,384]{1,0:T(8,128)(2,1)S(1)}, bf16[128,384]{1,0:T(8,128)(2,1)S(1)}, u32[]{:S(2)}, u32[]{:S(2)}) collective-permute-start(bf16[128,384]{1,0:T(8,128)(2,1)S(1)} %get-tuple-element.42), channel_id=1, source_target_pairs={{0,10},{1,2},{2,12},{3,4},{4,14},{5,6},{6,0},{7,8},{8,3},{9,11},{1... | collective-permute-start | bytes 294920 | tf_op jit(solution)/shard_map/ppermute | solution.py:387
  146.6 2.0 %collective-permute-start.24 = (bf16[128,384]{1,0:T(8,128)(2,1)S(1)}, bf16[128,384]{1,0:T(8,128)(2,1)S(1)}, u32[]{:S(2)}, u32[]{:S(2)}) collective-permute-start(bf16[128,384]{1,0:T(8,128)(2,1)S(1)} %get-tuple-element.43), channel_id=1, source_target_pairs={{0,12},{1,4},{2,14},{3,6},{4,0},{5,8},{6,2},{7,10},{8,5},{9,13},{1... | collective-permute-start | bytes 294920 | tf_op jit(solution)/shard_map/ppermute | solution.py:387
  148.6 1.4 collective-permute-start.25
  150.0 1.9 %collective-permute-done.21.refs_3_ = bf16[128,384]{1,0:T(8,128)(2,1)S(1)} collective-permute-done((bf16[128,384]{1,0:T(8,128)(2,1)S(1)}, bf16[128,384]{1,0:T(8,128)(2,1)S(1)}, u32[]{:S(2)}, u32[]{:S(2)}) %collective-permute-start.21) | collective-permute-done | bytes 98336 | tf_op jit(solution)/shard_map/ppermute | solution.py:387
  151.9 1.4 collective-permute-done.24.refs_6_
  153.3 2.7 %collective-permute-done.25.refs_7_ = bf16[128,384]{1,0:T(8,128)(2,1)S(1)} collective-permute-done((bf16[128,384]{1,0:T(8,128)(2,1)S(1)}, bf16[128,384]{1,0:T(8,128)(2,1)S(1)}, u32[]{:S(2)}, u32[]{:S(2)}) %collective-permute-start.25) | collective-permute-done | bytes 98336 | tf_op jit(solution)/shard_map/ppermute | solution.py:387
  155.9 1.0 shard_map.84
  (74 shorter events, 2.5 us)
Async XLA Ops:
  7.2 1.0 copy-start.8
  8.1 0.8 copy-start.9
  9.8 4.4 %collective-permute-start = (bf16[32,3072]{1,0:T(8,128)(2,1)S(1)}, bf16[32,3072]{1,0:T(8,128)(2,1)S(1)}, u32[]{:S(2)}, u32[]{:S(2)}) collective-permute-start(bf16[32,3072]{1,0:T(8,128)(2,1)S(1)} %get-tuple-element.25), channel_id=1, source_target_pairs={{0,1},{1,0},{2,3},{3,2},{4,5},{5,4},{6,7},{7,6},{8,9},{9,8},{10,11... | collective-permute-start | bytes 589832 | tf_op jit(solution)/shard_map/ppermute | solution.py:44
  15.0 21.2 %all-to-all-start = ((bf16[8,32,768]{2,1,0:T(8,128)(2,1)}), bf16[8,32,768]{2,1,0:T(8,128)(2,1)S(1)}, u32[]{:S(2)}, u32[]{:S(2)}) async-start(bf16[8,32,768]{2,1,0:T(8,128)(2,1)} %shard_map.77), calls=%async_computation | async-start | bytes 786432 | tf_op jit(solution)/shard_map/all_to_all | solution.py:150
  21.5 84.6 %all-gather.2.cloned.1.call-start = ((), (), s32[]{:S(2)}) async-start(), calls=%async_computation.1 | async-start | bytes 6684672 | tf_op jit(solution)/shard_map/all_gather | solution.py:151
  21.5 1.6 copy-start
  25.3 66.7 %copy-start.2 = (bf16[528,512]{1,0:T(8,128)(2,1)}, bf16[528,512]{1,0:T(8,128)(2,1)S(1)}, u32[]{:S(2)}) copy-start(bf16[528,512]{1,0:T(8,128)(2,1)S(1)} %get-tuple-element.26.refs_0_) | copy-start | bytes 1622020
  25.3 66.7 %copy-start.3 = (bf16[528,512]{1,0:T(8,128)(2,1)}, bf16[528,512]{1,0:T(8,128)(2,1)S(1)}, u32[]{:S(2)}) copy-start(bf16[528,512]{1,0:T(8,128)(2,1)S(1)} %get-tuple-element.27.refs_1_) | copy-start | bytes 1622020
  25.3 19.3 %collective-permute-start.3 = (bf16[528,512]{1,0:T(8,128)(2,1)S(1)}, bf16[528,512]{1,0:T(8,128)(2,1)S(1)}, u32[]{:S(2)}, u32[]{:S(2)}) collective-permute-start(bf16[528,512]{1,0:T(8,128)(2,1)S(1)} %get-tuple-element.26.refs_0_), channel_id=1, source_target_pairs={{0,2},{2,4},{4,6},{6,8},{8,10},{10,12},{12,14},{14,0},{1,3},{3,5},... | collective-permute-start | bytes 1622024 | tf_op jit(solution)/shard_map/ppermute | solution.py:40
  26.8 17.8 %collective-permute-start.1 = (bf16[528,512]{1,0:T(8,128)(2,1)S(1)}, bf16[528,512]{1,0:T(8,128)(2,1)S(1)}, u32[]{:S(2)}, u32[]{:S(2)}) collective-permute-start(bf16[528,512]{1,0:T(8,128)(2,1)S(1)} %get-tuple-element.26.refs_0_), channel_id=1, source_target_pairs={{0,14},{2,0},{4,2},{6,4},{8,6},{10,8},{12,10},{14,12},{1,15},{3,1}... | collective-permute-start | bytes 1622024 | tf_op jit(solution)/shard_map/ppermute | solution.py:40
  37.0 17.9 %collective-permute-start.2 = (bf16[528,512]{1,0:T(8,128)(2,1)S(1)}, bf16[528,512]{1,0:T(8,128)(2,1)S(1)}, u32[]{:S(2)}, u32[]{:S(2)}) collective-permute-start(bf16[528,512]{1,0:T(8,128)(2,1)S(1)} %get-tuple-element.27.refs_1_), channel_id=1, source_target_pairs={{0,14},{2,0},{4,2},{6,4},{8,6},{10,8},{12,10},{14,12},{1,15},{3,1}... | collective-permute-start | bytes 1622024 | tf_op jit(solution)/shard_map/ppermute | solution.py:40
  37.1 20.0 %collective-permute-start.4 = (bf16[528,512]{1,0:T(8,128)(2,1)S(1)}, bf16[528,512]{1,0:T(8,128)(2,1)S(1)}, u32[]{:S(2)}, u32[]{:S(2)}) collective-permute-start(bf16[528,512]{1,0:T(8,128)(2,1)S(1)} %get-tuple-element.27.refs_1_), channel_id=1, source_target_pairs={{0,2},{2,4},{4,6},{6,8},{8,10},{10,12},{12,14},{14,0},{1,3},{3,5},... | collective-permute-start | bytes 1622024 | tf_op jit(solution)/shard_map/ppermute | solution.py:40
  44.6 12.6 %copy-start.14 = (bf16[528,512]{1,0:T(8,128)(2,1)}, bf16[528,512]{1,0:T(8,128)(2,1)S(1)}, u32[]{:S(2)}) copy-start(bf16[528,512]{1,0:T(8,128)(2,1)S(1)} %collective-permute-done.3.refs_4_) | copy-start | bytes 1622020
  44.6 23.2 %collective-permute-start.7 = (bf16[528,512]{1,0:T(8,128)(2,1)S(1)}, bf16[528,512]{1,0:T(8,128)(2,1)S(1)}, u32[]{:S(2)}, u32[]{:S(2)}) collective-permute-start(bf16[528,512]{1,0:T(8,128)(2,1)S(1)} %collective-permute-done.3.refs_4_), channel_id=1, source_target_pairs={{0,2},{2,4},{4,6},{6,8},{8,10},{10,12},{12,14},{14,0},{1,3},{3,5},... | collective-permute-start | bytes 1622024 | tf_op jit(solution)/shard_map/ppermute | solution.py:40
  44.6 23.2 %copy-start.15 = (bf16[528,512]{1,0:T(8,128)(2,1)}, bf16[528,512]{1,0:T(8,128)(2,1)S(1)}, u32[]{:S(2)}) copy-start(bf16[528,512]{1,0:T(8,128)(2,1)S(1)} %collective-permute-done.1.refs_2_) | copy-start | bytes 1622020
  44.6 23.2 %collective-permute-start.5 = (bf16[528,512]{1,0:T(8,128)(2,1)S(1)}, bf16[528,512]{1,0:T(8,128)(2,1)S(1)}, u32[]{:S(2)}, u32[]{:S(2)}) collective-permute-start(bf16[528,512]{1,0:T(8,128)(2,1)S(1)} %collective-permute-done.1.refs_2_), channel_id=1, source_target_pairs={{0,14},{2,0},{4,2},{6,4},{8,6},{10,8},{12,10},{14,12},{1,15},{3,1}... | collective-permute-start | bytes 1622024 | tf_op jit(solution)/shard_map/ppermute | solution.py:40
  55.0 36.1 %copy-start.16 = (bf16[528,512]{1,0:T(8,128)(2,1)}, bf16[528,512]{1,0:T(8,128)(2,1)S(1)}, u32[]{:S(2)}) copy-start(bf16[528,512]{1,0:T(8,128)(2,1)S(1)} %collective-permute-done.2.refs_3_) | copy-start | bytes 1622020
  55.0 23.2 %collective-permute-start.6 = (bf16[528,512]{1,0:T(8,128)(2,1)S(1)}, bf16[528,512]{1,0:T(8,128)(2,1)S(1)}, u32[]{:S(2)}, u32[]{:S(2)}) collective-permute-start(bf16[528,512]{1,0:T(8,128)(2,1)S(1)} %collective-permute-done.2.refs_3_), channel_id=1, source_target_pairs={{0,14},{2,0},{4,2},{6,4},{8,6},{10,8},{12,10},{14,12},{1,15},{3,1}... | collective-permute-start | bytes 1622024 | tf_op jit(solution)/shard_map/ppermute | solution.py:40
  57.1 33.9 %copy-start.17 = (bf16[528,512]{1,0:T(8,128)(2,1)}, bf16[528,512]{1,0:T(8,128)(2,1)S(1)}, u32[]{:S(2)}) copy-start(bf16[528,512]{1,0:T(8,128)(2,1)S(1)} %collective-permute-done.4.refs_5_) | copy-start | bytes 1622020
  57.1 23.2 %collective-permute-start.8 = (bf16[528,512]{1,0:T(8,128)(2,1)S(1)}, bf16[528,512]{1,0:T(8,128)(2,1)S(1)}, u32[]{:S(2)}, u32[]{:S(2)}) collective-permute-start(bf16[528,512]{1,0:T(8,128)(2,1)S(1)} %collective-permute-done.4.refs_5_), channel_id=1, source_target_pairs={{0,2},{2,4},{4,6},{6,8},{8,10},{10,12},{12,14},{14,0},{1,3},{3,5},... | collective-permute-start | bytes 1622024 | tf_op jit(solution)/shard_map/ppermute | solution.py:40
  67.8 23.3 %copy-start.18 = (bf16[528,512]{1,0:T(8,128)(2,1)}, bf16[528,512]{1,0:T(8,128)(2,1)S(1)}, u32[]{:S(2)}) copy-start(bf16[528,512]{1,0:T(8,128)(2,1)S(1)} %collective-permute-done.7.refs_8_) | copy-start | bytes 1622020
  67.8 23.3 %collective-permute-start.11 = (bf16[528,512]{1,0:T(8,128)(2,1)S(1)}, bf16[528,512]{1,0:T(8,128)(2,1)S(1)}, u32[]{:S(2)}, u32[]{:S(2)}) collective-permute-start(bf16[528,512]{1,0:T(8,128)(2,1)S(1)} %collective-permute-done.7.refs_8_), channel_id=1, source_target_pairs={{0,2},{2,4},{4,6},{6,8},{8,10},{10,12},{12,14},{14,0},{1,3},{3,5},... | collective-permute-start | bytes 1622024 | tf_op jit(solution)/shard_map/ppermute | solution.py:40
  67.8 23.3 %copy-start.19 = (bf16[528,512]{1,0:T(8,128)(2,1)}, bf16[528,512]{1,0:T(8,128)(2,1)S(1)}, u32[]{:S(2)}) copy-start(bf16[528,512]{1,0:T(8,128)(2,1)S(1)} %collective-permute-done.5.refs_6_) | copy-start | bytes 1622020
  67.8 23.3 %collective-permute-start.9 = (bf16[528,512]{1,0:T(8,128)(2,1)S(1)}, bf16[528,512]{1,0:T(8,128)(2,1)S(1)}, u32[]{:S(2)}, u32[]{:S(2)}) collective-permute-start(bf16[528,512]{1,0:T(8,128)(2,1)S(1)} %collective-permute-done.5.refs_6_), channel_id=1, source_target_pairs={{0,14},{2,0},{4,2},{6,4},{8,6},{10,8},{12,10},{14,12},{1,15},{3,1}... | collective-permute-start | bytes 1622024 | tf_op jit(solution)/shard_map/ppermute | solution.py:40
  78.1 13.8 %copy-start.20 = (bf16[528,512]{1,0:T(8,128)(2,1)}, bf16[528,512]{1,0:T(8,128)(2,1)S(1)}, u32[]{:S(2)}) copy-start(bf16[528,512]{1,0:T(8,128)(2,1)S(1)} %collective-permute-done.6.refs_7_) | copy-start | bytes 1622020
  78.1 23.1 %collective-permute-start.10 = (bf16[528,512]{1,0:T(8,128)(2,1)S(1)}, bf16[528,512]{1,0:T(8,128)(2,1)S(1)}, u32[]{:S(2)}, u32[]{:S(2)}) collective-permute-start(bf16[528,512]{1,0:T(8,128)(2,1)S(1)} %collective-permute-done.6.refs_7_), channel_id=1, source_target_pairs={{0,14},{2,0},{4,2},{6,4},{8,6},{10,8},{12,10},{14,12},{1,15},{3,1}... | collective-permute-start | bytes 1622024 | tf_op jit(solution)/shard_map/ppermute | solution.py:40
  80.3 11.7 %copy-start.21 = (bf16[528,512]{1,0:T(8,128)(2,1)}, bf16[528,512]{1,0:T(8,128)(2,1)S(1)}, u32[]{:S(2)}) copy-start(bf16[528,512]{1,0:T(8,128)(2,1)S(1)} %collective-permute-done.8.refs_9_) | copy-start | bytes 1622020
  80.3 22.2 %collective-permute-start.12 = (bf16[528,512]{1,0:T(8,128)(2,1)S(1)}, bf16[528,512]{1,0:T(8,128)(2,1)S(1)}, u32[]{:S(2)}, u32[]{:S(2)}) collective-permute-start(bf16[528,512]{1,0:T(8,128)(2,1)S(1)} %collective-permute-done.8.refs_9_), channel_id=1, source_target_pairs={{0,2},{2,4},{4,6},{6,8},{8,10},{10,12},{12,14},{14,0},{1,3},{3,5},... | collective-permute-start | bytes 1622024 | tf_op jit(solution)/shard_map/ppermute | solution.py:40
  91.1 0.9 copy-start.4
  91.1 1.1 copy-start.5
  92.2 23.4 %collective-permute-start.13 = (bf16[528,256]{1,0:T(8,128)(2,1)}, bf16[528,256]{1,0:T(8,128)(2,1)S(1)}, u32[]{:S(2)}, u32[]{:S(2)}) collective-permute-start(bf16[528,256]{1,0:T(8,128)(2,1)} %get-tuple-element.30), channel_id=1, source_target_pairs={{0,2},{2,4},{4,6},{6,8},{8,10},{10,12},{12,14},{14,0},{1,3},{3,5},... | collective-permute-start | bytes 811016 | tf_op jit(solution)/shard_map/ppermute | solution.py:40
  92.6 23.0 %collective-permute-start.14 = (bf16[528,256]{1,0:T(8,128)(2,1)S(1)}, bf16[528,256]{1,0:T(8,128)(2,1)S(1)}, u32[]{:S(2)}, u32[]{:S(2)}) collective-permute-start(bf16[528,256]{1,0:T(8,128)(2,1)S(1)} %get-tuple-element.31), channel_id=1, source_target_pairs={{0,14},{2,0},{4,2},{6,4},{8,6},{10,8},{12,10},{14,12},{1,15},{3,1}... | collective-permute-start | bytes 811016 | tf_op jit(solution)/shard_map/ppermute | solution.py:40
  101.2 1.4 copy-start.6
  103.4 12.2 %collective-permute-start.15 = (bf16[528,256]{1,0:T(8,128)(2,1)S(1)}, bf16[528,256]{1,0:T(8,128)(2,1)S(1)}, u32[]{:S(2)}, u32[]{:S(2)}) collective-permute-start(bf16[528,256]{1,0:T(8,128)(2,1)S(1)} %get-tuple-element.32), channel_id=1, source_target_pairs={{0,2},{2,4},{4,6},{6,8},{8,10},{10,12},{12,14},{14,0},{1,3},{3,5},... | collective-permute-start | bytes 811016 | tf_op jit(solution)/shard_map/ppermute | solution.py:40
  104.0 11.6 %collective-permute-start.16 = (bf16[528,256]{1,0:T(8,128)(2,1)S(1)}, bf16[528,256]{1,0:T(8,128)(2,1)S(1)}, u32[]{:S(2)}, u32[]{:S(2)}) collective-permute-start(bf16[528,256]{1,0:T(8,128)(2,1)S(1)} %get-tuple-element.33), channel_id=1, source_target_pairs={{0,14},{2,0},{4,2},{6,4},{8,6},{10,8},{12,10},{14,12},{1,15},{3,1}... | collective-permute-start | bytes 811016 | tf_op jit(solution)/shard_map/ppermute | solution.py:40
  115.6 0.8 copy-start.24
  115.6 0.9 copy-start.25
  122.0 5.8 %collective-permute-start.17 = (bf16[1024,512]{1,0:T(8,128)(2,1)}, bf16[1024,512]{1,0:T(8,128)(2,1)S(1)}, u32[]{:S(2)}, u32[]{:S(2)}) collective-permute-start(bf16[1024,512]{1,0:T(8,128)(2,1)} %get-tuple-element.35), channel_id=1, source_target_pairs={{0,1},{1,0},{2,3},{3,2},{4,5},{5,4},{6,7},{7,6},{8,9},{9,8},{10,11... | collective-permute-start | bytes 3145736 | tf_op jit(solution)/shard_map/ppermute | solution.py:44
  125.3 2.5 %copy-start.1 = (bf16[1024,512]{1,0:T(8,128)(2,1)S(1)}, bf16[1024,512]{1,0:T(8,128)(2,1)}, u32[]{:S(2)}) copy-start(bf16[1024,512]{1,0:T(8,128)(2,1)} %get-tuple-element.34.mine_ref) | copy-start | bytes 3145732
  125.3 2.5 %copy-start.11 = (f32[16,512]{1,0:T(8,128)S(1)}, f32[16,512]{1,0:T(8,128)}, u32[]{:S(2)}) copy-start(f32[16,512]{1,0:T(8,128)} %get-tuple-element.36.squares_ref) | copy-start | bytes 98308
  131.3 10.8 %collective-permute-start.18 = (bf16[128,384]{1,0:T(8,128)(2,1)S(1)}, bf16[128,384]{1,0:T(8,128)(2,1)S(1)}, u32[]{:S(2)}, u32[]{:S(2)}) collective-permute-start(bf16[128,384]{1,0:T(8,128)(2,1)S(1)} %get-tuple-element.37), channel_id=1, source_target_pairs={{0,0},{1,8},{2,2},{3,10},{4,4},{5,12},{6,6},{7,14},{8,9},{9,1},{10... | collective-permute-start | bytes 294920 | tf_op jit(solution)/shard_map/ppermute | solution.py:387
  136.3 10.3 %collective-permute-start.19 = (bf16[128,384]{1,0:T(8,128)(2,1)S(1)}, bf16[128,384]{1,0:T(8,128)(2,1)S(1)}, u32[]{:S(2)}, u32[]{:S(2)}) collective-permute-start(bf16[128,384]{1,0:T(8,128)(2,1)S(1)} %get-tuple-element.38), channel_id=1, source_target_pairs={{0,2},{1,10},{2,4},{3,12},{4,6},{5,14},{6,8},{7,0},{8,11},{9,3},{1... | collective-permute-start | bytes 294920 | tf_op jit(solution)/shard_map/ppermute | solution.py:387
  136.4 12.2 %collective-permute-start.20 = (bf16[128,384]{1,0:T(8,128)(2,1)S(1)}, bf16[128,384]{1,0:T(8,128)(2,1)S(1)}, u32[]{:S(2)}, u32[]{:S(2)}) collective-permute-start(bf16[128,384]{1,0:T(8,128)(2,1)S(1)} %get-tuple-element.39), channel_id=1, source_target_pairs={{0,4},{1,12},{2,6},{3,14},{4,8},{5,0},{6,10},{7,2},{8,13},{9,5},{1... | collective-permute-start | bytes 294920 | tf_op jit(solution)/shard_map/ppermute | solution.py:387
  138.3 13.6 %collective-permute-start.21 = (bf16[128,384]{1,0:T(8,128)(2,1)S(1)}, bf16[128,384]{1,0:T(8,128)(2,1)S(1)}, u32[]{:S(2)}, u32[]{:S(2)}) collective-permute-start(bf16[128,384]{1,0:T(8,128)(2,1)S(1)} %get-tuple-element.40), channel_id=1, source_target_pairs={{0,6},{1,14},{2,8},{3,0},{4,10},{5,2},{6,12},{7,4},{8,15},{9,7},{1... | collective-permute-start | bytes 294920 | tf_op jit(solution)/shard_map/ppermute | solution.py:387
  139.4 12.5 %collective-permute-start.22 = (bf16[128,384]{1,0:T(8,128)(2,1)S(1)}, bf16[128,384]{1,0:T(8,128)(2,1)S(1)}, u32[]{:S(2)}, u32[]{:S(2)}) collective-permute-start(bf16[128,384]{1,0:T(8,128)(2,1)S(1)} %get-tuple-element.41), channel_id=1, source_target_pairs={{0,8},{1,0},{2,10},{3,2},{4,12},{5,4},{6,14},{7,6},{8,1},{9,9},{10... | collective-permute-start | bytes 294920 | tf_op jit(solution)/shard_map/ppermute | solution.py:387
  142.2 9.8 %collective-permute-start.23 = (bf16[128,384]{1,0:T(8,128)(2,1)S(1)}, bf16[128,384]{1,0:T(8,128)(2,1)S(1)}, u32[]{:S(2)}, u32[]{:S(2)}) collective-permute-start(bf16[128,384]{1,0:T(8,128)(2,1)S(1)} %get-tuple-element.42), channel_id=1, source_target_pairs={{0,10},{1,2},{2,12},{3,4},{4,14},{5,6},{6,0},{7,8},{8,3},{9,11},{1... | collective-permute-start | bytes 294920 | tf_op jit(solution)/shard_map/ppermute | solution.py:387
  146.6 6.7 %collective-permute-start.24 = (bf16[128,384]{1,0:T(8,128)(2,1)S(1)}, bf16[128,384]{1,0:T(8,128)(2,1)S(1)}, u32[]{:S(2)}, u32[]{:S(2)}) collective-permute-start(bf16[128,384]{1,0:T(8,128)(2,1)S(1)} %get-tuple-element.43), channel_id=1, source_target_pairs={{0,12},{1,4},{2,14},{3,6},{4,0},{5,8},{6,2},{7,10},{8,5},{9,13},{1... | collective-permute-start | bytes 294920 | tf_op jit(solution)/shard_map/ppermute | solution.py:387
  148.6 7.3 %collective-permute-start.25 = (bf16[128,384]{1,0:T(8,128)(2,1)S(1)}, bf16[128,384]{1,0:T(8,128)(2,1)S(1)}, u32[]{:S(2)}, u32[]{:S(2)}) collective-permute-start(bf16[128,384]{1,0:T(8,128)(2,1)S(1)} %get-tuple-element.44), channel_id=1, source_target_pairs={{0,14},{1,6},{2,0},{3,8},{4,2},{5,10},{6,4},{7,12},{8,7},{9,15},{1... | collective-permute-start | bytes 294920 | tf_op jit(solution)/shard_map/ppermute | solution.py:387
  (6 other events, 4.6 us)
Sparse Core Ops, SparseCore 0:
  37.1 63.8 all-gather.1

commit v4 on v3

--- a/solution.py
+++ b/solution.py
@@ -1,3 +1,5 @@
+import functools
+
 import jax
 import jax.numpy as jnp
 from jax import lax
@@ -229,10 +231,18 @@
     )(section, weight, *blocks)
 
 
+OFFSETS = (0, 5, 2, 7)
+
+
+def target_rows(section, core, turn_of, rows):
+    target = lax.rem(section + OFFSETS[turn_of] + 4 * core, SECTIONS)
+    return pl.ds(pl.multiple_of(target * rows, rows), rows)
+
+
 def far_kernel(section_ref, core_ref, weight_hbm, total_hbm, sums_ref, *refs):
     block_hbm = refs[:4]
-    mine_hbm, send_hbm, squares_ref = refs[4:7]
-    weight, total, blocks, out, sems, block_sems, out_sems = refs[7:]
+    mine_hbm, send_hbm, pair_hbm, squares_ref = refs[4:8]
+    weight, total, blocks, out, sems, block_sems, out_sems = refs[8:]
     rows = total.shape[1]
     source = lax.rem(section_ref[0] + SECTIONS // 2, SECTIONS)
     load = pltpu.make_async_copy(weight_hbm.at[:, source], weight, sems.at[2])
@@ -250,8 +260,6 @@
         loads.append(group)
     load.wait()
     matrix = weight[...].reshape(INSTS * STRIPE, WIDE)
-    half_cols = QUERY_COLS // 2
-    first = core_ref[0] == 0
     stores = []
     for half in range(2):
         span = slice(half * rows, (half + 1) * rows)
@@ -259,23 +267,24 @@
             copy.wait()
         block = jnp.concatenate([blocks[2 * half], blocks[2 * half + 1]], axis=1)
         part = jnp.dot(block[:rows], matrix, preferred_element_type=F32)
-        part = (part + total[half].astype(F32)).astype(BF16)
-        low, high = part[:, :half_cols], part[:, half_cols:QUERY_COLS]
-        both = part[:, KEY_AT:]
-        for side, (query, target) in enumerate(
-            (
-                (jnp.where(first, high, low), send_hbm),
-                (jnp.where(first, low, high), mine_hbm),
+        out[span] = (part + total[half].astype(F32)).astype(BF16)
+        at = slice(half * 8, (half + 1) * 8)
+        squares_ref[at] = add_squares(sums_ref[at], block[rows:])
+        store = pltpu.make_async_copy(
+            out.at[span, QUERY_COLS:], pair_hbm.at[span], out_sems.at[half]
+        )
+        store.start()
+        stores.append(store)
+    chunk = 2 * rows // SECTIONS
+    for core, target in ((1 - core_ref[0], send_hbm), (core_ref[0], mine_hbm)):
+        for turn_of in range(4):
+            store = pltpu.make_async_copy(
+                out.at[target_rows(section_ref[0], core, turn_of, chunk), :QUERY_COLS],
+                target.at[turn_of * chunk : (turn_of + 1) * chunk],
+                out_sems.at[len(stores)],
             )
-        ):
-            index = 2 * half + side
-            out[index, :, :half_cols] = query
-            out[index, :, half_cols:] = both
-            store = pltpu.make_async_copy(out.at[index], target.at[span], out_sems.at[index])
             store.start()
             stores.append(store)
-        at = slice(half * 8, (half + 1) * 8)
-        squares_ref[at] = add_squares(sums_ref[at], block[rows:])
     for store in stores:
         store.wait()
 
@@ -283,20 +292,25 @@
 def far_sum(section, core, weight, total, sums, blocks):
     seq_len = total.shape[0]
     rows = seq_len // 2
-    shape = jax.ShapeDtypeStruct((seq_len, QUERY_COLS), BF16)
+    queries = jax.ShapeDtypeStruct((rows, QUERY_COLS), BF16)
     return pl.pallas_call(
         far_kernel,
         in_specs=[scalar()] * 2 + whole(2, HBM) + whole(1) + whole(len(blocks), HBM),
-        out_specs=whole(2, HBM) + whole(1),
-        out_shape=[shape, shape, jax.ShapeDtypeStruct(sums.shape, F32)],
+        out_specs=whole(3, HBM) + whole(1),
+        out_shape=[
+            queries,
+            queries,
+            jax.ShapeDtypeStruct((seq_len, WIDE - QUERY_COLS), BF16),
+            jax.ShapeDtypeStruct(sums.shape, F32),
+        ],
         scratch_shapes=[
             pltpu.VMEM((INSTS, STRIPE, WIDE), BF16),
             pltpu.VMEM((2, rows, WIDE), BF16),
             pltpu.VMEM((4, *blocks[0].shape), BF16),
-            pltpu.VMEM((4, rows, QUERY_COLS), BF16),
+            pltpu.VMEM((seq_len, WIDE), BF16),
             pltpu.SemaphoreType.DMA((3,)),
             pltpu.SemaphoreType.DMA((4,)),
-            pltpu.SemaphoreType.DMA((4,)),
+            pltpu.SemaphoreType.DMA((10,)),
         ],
         compiler_params=params(60),
     )(section, core, weight, total, sums, *blocks)
@@ -306,81 +320,107 @@
     return head * cosine + pltpu.roll(head, HEAD_SIZE // 2, 1) * sine
 
 
-def attend_kernel(
-    section_ref, core_ref, mine_ref, other_ref, squares_ref, cos_ref, sin_ref, *refs
-):
-    piece_refs, (out_ref, key_ref, value_ref) = refs[:SECTIONS], refs[SECTIONS:]
-    seq_len = mine_ref.shape[0]
+def prepare_keys(mine, other, squares_ref, cos_ref, sin_ref, key_ref, value_ref, inverse_ref):
     step = 256
-    scale_by = 1.4426950408889634 / (HEAD_SIZE**0.5)
-    low = F32(-1e30)
-    near = lax.broadcasted_iota(jnp.int32, (step, step), 0) >= lax.broadcasted_iota(
-        jnp.int32, (step, step), 1
-    )
-    for start in range(0, seq_len, step):
+    half = squares_ref.shape[1]
+    for start in range(0, key_ref.shape[0], step):
         span = slice(start, start + step)
-        stop = start + step
-        half = squares_ref.shape[1]
         at = start // half * 8
         squares = squares_ref[at : at + 1, start % half : start % half + step]
         inverse = 1.0 / jnp.sqrt(squares / MODEL_WIDTH + EPS)
         inverse = jnp.broadcast_to(inverse, (HEAD_SIZE, step)).T
-        inverse = jnp.concatenate([inverse] * (QUERY_COLS // HEAD_SIZE), axis=1)
-        total = mine_ref[span].astype(F32) + other_ref[span].astype(F32)
-        total = total * inverse
-        cosine, sine = cos_ref[span], sin_ref[span]
-        key = turn(total[:, 2 * HEAD_SIZE : 3 * HEAD_SIZE], cosine, sine).astype(BF16)
-        value = total[:, 3 * HEAD_SIZE :].astype(BF16)
-        key_ref[span] = key
-        value_ref[span] = value
-        out_ref[span, 2 * HEAD_SIZE :] = jnp.where(core_ref[0] == 0, key, value)
-        query = jnp.concatenate(
-            [
-                turn(total[:, :HEAD_SIZE], cosine, sine),
-                turn(total[:, HEAD_SIZE : 2 * HEAD_SIZE], cosine, sine),
-            ],
-            axis=0,
-        ).astype(BF16)
+        inverse_ref[span] = inverse
+        pair = mine[span].astype(F32) + other[span].astype(F32)
+        key = turn(pair[:, :HEAD_SIZE] * inverse, cos_ref[span], sin_ref[span])
+        key_ref[span] = key.astype(BF16)
+        value_ref[span] = (pair[:, HEAD_SIZE:] * inverse).astype(BF16)
+
+
+def attend_rows(turn_of, section, core, operands, piece_ref):
+    mine_ref, other_ref, cos_ref, sin_ref, key_ref, value_ref, inverse_ref = operands
+    rows = piece_ref.shape[0]
+    seq_len = key_ref.shape[0]
+    heads = QUERY_COLS // HEAD_SIZE
+    scale_by = 1.4426950408889634 / (HEAD_SIZE**0.5)
+    span = target_rows(section, core, turn_of, rows)
+    first = lax.rem(section + OFFSETS[turn_of] + 4 * core, SECTIONS) * rows
+    here = slice(turn_of * rows, (turn_of + 1) * rows)
+    total = mine_ref[here].astype(F32) + other_ref[here].astype(F32)
+    cosine, sine, inverse = cos_ref[span], sin_ref[span], inverse_ref[span]
+    query = jnp.concatenate(
+        [
+            turn(total[:, h * HEAD_SIZE : (h + 1) * HEAD_SIZE] * inverse, cosine, sine)
+            for h in range(heads)
+        ],
+        axis=0,
+    ).astype(BF16)
+
+    def run(count):
         score = lax.dot_general(
-            query, key_ref[:stop], (((1,), (1,)), ((), ())), preferred_element_type=F32
+            query, key_ref[:count], (((1,), (1,)), ((), ())), preferred_element_type=F32
         )
-        mask = jnp.concatenate([near, near], axis=0)
-        last = jnp.where(mask, score[:, start:], low)
-        score = jnp.concatenate([score[:, :start], last], axis=1) if start else last
+        row = lax.broadcasted_iota(jnp.int32, (rows, count), 0) + first
+        mask = row >= lax.broadcasted_iota(jnp.int32, (rows, count), 1)
+        mask = jnp.concatenate([mask] * heads, axis=0)
+        score = jnp.where(mask, score, F32(-1e30))
         top = jnp.max(score, axis=1, keepdims=True)
         expo = jnp.exp2((score - top) * scale_by)
         weight_sum = jnp.sum(expo, axis=1, keepdims=True)
-        mixed = jnp.dot(expo.astype(BF16), value_ref[:stop], preferred_element_type=F32)
+        mixed = jnp.dot(expo.astype(BF16), value_ref[:count], preferred_element_type=F32)
         mixed = (mixed / weight_sum).astype(BF16)
-        out_ref[span, :HEAD_SIZE] = mixed[:step]
-        out_ref[span, HEAD_SIZE : 2 * HEAD_SIZE] = mixed[step:]
-
-
-    rows = piece_refs[0].shape[0]
-    for turn_of, piece_ref in enumerate(piece_refs):
-        target = lax.rem(section_ref[0] + turn_of + 4 * core_ref[0], SECTIONS)
-        piece_ref[...] = out_ref[pl.ds(pl.multiple_of(target * rows, rows), rows)]
-
-
-def attend(section, core, mine, other, squares, cosine, sine):
-    seq_len = mine.shape[0]
-    shape = (seq_len, 3 * HEAD_SIZE)
-    piece = jax.ShapeDtypeStruct((seq_len // SECTIONS, shape[1]), BF16)
-    return pl.pallas_call(
-        attend_kernel,
-        in_specs=[scalar()] * 2 + whole(5),
-        out_specs=whole(SECTIONS),
-        out_shape=[piece] * SECTIONS,
-        scratch_shapes=[pltpu.VMEM(shape, BF16)] + [pltpu.VMEM((seq_len, HEAD_SIZE), BF16)] * 2,
-        compiler_params=params(24),
-    )(section, core, mine, other, squares, cosine, sine)
+        for h in range(heads):
+            piece_ref[:, h * HEAD_SIZE : (h + 1) * HEAD_SIZE] = mixed[h * rows : (h + 1) * rows]
+
+    early = first < seq_len // 2
+    pl.when(early)(lambda: run(seq_len // 2))
+    pl.when(jnp.logical_not(early))(lambda: run(seq_len))
+    piece_ref[:, KEY_AT:VALUE_AT] = key_ref[span]
+    piece_ref[:, VALUE_AT:] = value_ref[span]
+
+
+def first_kernel(section_ref, core_ref, *refs):
+    mine_ref, other_ref, pair_ref, other_pair_ref, squares_ref, cos_ref, sin_ref = refs[:7]
+    piece_ref, *made = refs[7:]
+    prepare_keys(pair_ref, other_pair_ref, squares_ref, cos_ref, sin_ref, *made)
+    operands = (mine_ref, other_ref, cos_ref, sin_ref, *made)
+    attend_rows(0, section_ref[0], core_ref[0], operands, piece_ref)
+
+
+def next_kernel(turn_of, section_ref, core_ref, *refs):
+    attend_rows(turn_of, section_ref[0], core_ref[0], refs[:-1], refs[-1])
+
+
+def attend(section, core, mine, other, pair, other_pair, squares, cosine, sine):
+    seq_len = pair.shape[0]
+    piece = jax.ShapeDtypeStruct((seq_len // SECTIONS, WIDE), BF16)
+    head = jax.ShapeDtypeStruct((seq_len, HEAD_SIZE), BF16)
+    inverse = jax.ShapeDtypeStruct((seq_len, HEAD_SIZE), F32)
+    piece_of_first, *made = pl.pallas_call(
+        first_kernel,
+        in_specs=[scalar()] * 2 + whole(7),
+        out_specs=whole(4),
+        out_shape=[piece, head, head, inverse],
+        compiler_params=params(16),
+    )(section, core, mine, other, pair, other_pair, squares, cosine, sine)
+    pieces = [piece_of_first]
+    for turn_of in range(1, 4):
+        pieces.append(
+            pl.pallas_call(
+                functools.partial(next_kernel, turn_of),
+                in_specs=[scalar()] * 2 + whole(7),
+                out_specs=pl.BlockSpec(memory_space=VMEM),
+                out_shape=piece,
+                compiler_params=params(16),
+            )(section, core, mine, other, cosine, sine, *made)
+        )
+    return pieces
 
 
 def send_rows(pieces):
     arrived = []
-    for turn_of, piece in enumerate(pieces):
+    for offset, piece in zip(OFFSETS, pieces):
         pairs = [
-            (2 * s + c, 2 * ((s + turn_of + 4 * c) % SECTIONS) + s // 4)
+            (2 * s + c, 2 * ((s + offset + 4 * c) % SECTIONS) + s // 4)
             for s in range(SECTIONS)
             for c in range(2)
         ]
@@ -388,52 +428,41 @@
     return arrived
 
 
-def place_kernel(section_ref, core_ref, *refs):
-    arrived = refs[:SECTIONS]
-    attended_ref, key_ref, value_ref, pair_sems, head_sems = refs[SECTIONS:]
-    pair = 2 * HEAD_SIZE
+def place_kernel(section_ref, *refs):
+    arrived = refs[:4]
+    outs, sems = refs[4:7], refs[7]
     copies = []
-    for turn_of, piece in enumerate(arrived):
-        source = lax.rem(section_ref[0] + SECTIONS - turn_of, SECTIONS)
-        group = lax.rem(source, 4)
-        from_first = source // 4 == core_ref[0]
-        at = group * (2 * pair) + jnp.where(from_first, 0, pair)
-        copy = pltpu.make_async_copy(
-            piece.at[:, :pair],
-            attended_ref.at[0, :, pl.ds(pl.multiple_of(at, HEAD_SIZE), pair)],
-            pair_sems.at[turn_of],
-        )
-        copy.start()
-        columns = pl.ds(pl.multiple_of(group * HEAD_SIZE, HEAD_SIZE), HEAD_SIZE)
-        to_key = pltpu.make_async_copy(
-            piece.at[:, pair:], key_ref.at[0, :, columns], head_sems.at[turn_of]
-        )
-        to_value = pltpu.make_async_copy(
-            piece.at[:, pair:], value_ref.at[0, :, columns], head_sems.at[turn_of]
-        )
-        pl.when(from_first)(to_key.start)
-        pl.when(jnp.logical_not(from_first))(to_value.start)
-        copies.append((copy, to_key, to_value, from_first))
-    for copy, to_key, to_value, from_first in copies:
+    for offset, piece in zip(OFFSETS, arrived):
+        group = lax.rem(section_ref[0] + SECTIONS - offset, 4)
+        for out, start, size in zip(
+            outs, (0, KEY_AT, VALUE_AT), (QUERY_COLS, HEAD_SIZE, HEAD_SIZE)
+        ):
+            at = pl.multiple_of(group * size, HEAD_SIZE)
+            copy = pltpu.make_async_copy(
+                piece.at[:, start : start + size],
+                out.at[0, :, pl.ds(at, size)],
+                sems.at[len(copies)],
+            )
+            copy.start()
+            copies.append(copy)
+    for copy in copies:
         copy.wait()
-        pl.when(from_first)(to_key.wait)
-        pl.when(jnp.logical_not(from_first))(to_value.wait)
-
-
-def place(section, core, arrived):
+
+
+def place(section, arrived):
     rows = arrived[0].shape[0]
     return pl.pallas_call(
         place_kernel,
-        in_specs=[scalar()] * 2 + whole(SECTIONS, pl.ANY),
+        in_specs=[scalar()] + whole(4, pl.ANY),
         out_specs=whole(3, pl.ANY),
         out_shape=[
-            jax.ShapeDtypeStruct((1, rows, 16 * HEAD_SIZE), BF16),
+            jax.ShapeDtypeStruct((1, rows, 4 * QUERY_COLS), BF16),
             jax.ShapeDtypeStruct((1, rows, 4 * HEAD_SIZE), BF16),
             jax.ShapeDtypeStruct((1, rows, 4 * HEAD_SIZE), BF16),
         ],
-        scratch_shapes=[pltpu.SemaphoreType.DMA((SECTIONS,))] * 2,
+        scratch_shapes=[pltpu.SemaphoreType.DMA((12,))],
         compiler_params=params(8),
-    )(section, core, *arrived)
+    )(section, *arrived)
 
 
 def tables(rows):
@@ -456,9 +485,12 @@
     (upper, upper_far), (lower, lower_far) = (spread(half) for half in halves)
     near = [block for pair in zip(upper, lower) for block in pair]
     total, sums = near_sum(section, weight, near)
-    mine, send, squares = far_sum(section, core, weight, total, sums, upper_far + lower_far)
-    pieces = attend(section, core, mine, swap_cores(send), squares, cosine, sine)
-    return place(section, core, send_rows(pieces))
+    mine, send, pair, squares = far_sum(
+        section, core, weight, total, sums, upper_far + lower_far
+    )
+    other, other_pair = swap_cores(send), swap_cores(pair)
+    pieces = attend(section, core, mine, other, pair, other_pair, squares, cosine, sine)
+    return place(section, send_rows(pieces))
 
 
 def solution(mesh):

time: 164 us -> 159 us (0.970)
  starting transfers between devices: 50.6 us -> 42.5 us
  Pallas kernels: 22.7 us -> 25.2 us
    ppermute x8 -> x4, starting transfers between devices: 18 us -> 9.98 us  [send_rows(): arrived.append(lax.ppermute(piece, ('section', 'tp'), pairs))]
    pallas_call x2 -> x5, Pallas kernels: 4.57 us -> 6.92 us  [the longest x3 3.67 us: attend(): pl.pallas_call(functools.partial(next_kernel, turn_of), in_specs=[scalar(...]
    ppermute x8 -> x4, waiting for transfers between devices: 6.58 us -> 6.96 us  [send_rows(): arrived.append(lax.ppermute(piece, ('section', 'tp'), pairs))]
    ppermute x2 -> x3, starting transfers between devices: 6.6 us -> 6.48 us  [swap_cores(): return lax.ppermute(array, 'tp', [(0, 1), (1, 0)])]
    unnamed x52 -> x54, local copies, waits for them, and re-layouts: 7.57 us -> 7.58 us
  transfers between devices with their start and end apart: 28 -> 25, of which waited for: 14 -> 13; matrix products, arithmetic and copies ran while one was open for 1% -> 1% of each run, Pallas kernels for 7% -> 9%
where the time goes in v4:
time: 159 us; the launch traced here: 158 us
  waiting for transfers between devices  66.5 us (42%)
  starting transfers between devices  42.5 us (27%)
  Pallas kernels  25.2 us (16%)
  between operations  14.4 us (9%)
  local copies, waits for them, and re-layouts  7.58 us (5%)
  other arithmetic  2.25 us (1%)
    ppermute x16, waiting for transfers between devices, z_shift(): lax.ppermute(array, 'section', [(i, (i + step) % SECTIONS) for i in range...  50.2 us
    ppermute x16, starting transfers between devices, z_shift(): lax.ppermute(array, 'section', [(i, (i + step) % SECTIONS) for i in range...  19.6 us
    ppermute x4, starting transfers between devices, send_rows(): arrived.append(lax.ppermute(piece, ('section', 'tp'), pairs))  9.98 us
    pallas_call x1, Pallas kernels, near_sum(): pl.pallas_call(near_kernel, in_specs=[scalar()] + whole(1 + len(blocks),...  9.49 us
    all_to_all x1, waiting for transfers between devices, gather_weights(): blocks = lax.all_to_all(blocks, 'section', 0, 0, tiled=True)  8.14 us
    unnamed x54, local copies, waits for them, and re-layouts  7.58 us
    ppermute x4, waiting for transfers between devices, send_rows(): arrived.append(lax.ppermute(piece, ('section', 'tp'), pairs))  6.96 us
    ppermute x3, starting transfers between devices, swap_cores(): return lax.ppermute(array, 'tp', [(0, 1), (1, 0)])  6.48 us
  transfers between devices with their start and end apart: 25, of which 13 were waited for; matrix products, arithmetic and copies ran while one was open for 1% of the time, Pallas kernels for 9%

profile of v4, /device:TPU:1, one launch (start us, length us, event | category | flops | bytes accessed | tf_op | source)
XLA Modules:
  0.0 158.4 jit_solution(15910516638126033710)
XLA Ops:
  7.2 0.9 copy-done.9
  8.1 0.8 copy-done.10
  9.0 0.8 copy-done.11
  9.8 3.3 %collective-permute-start = (bf16[32,3072]{1,0:T(8,128)(2,1)S(1)}, bf16[32,3072]{1,0:T(8,128)(2,1)S(1)}, u32[]{:S(2)}, u32[]{:S(2)}) collective-permute-start(bf16[32,3072]{1,0:T(8,128)(2,1)S(1)} %get-tuple-element.22), channel_id=1, source_target_pairs={{0,1},{1,0},{2,3},{3,2},{4,5},{5,4},{6,7},{7,6},{8,9},{9,8},{10,11... | collective-permute-start | bytes 589832 | tf_op jit(solution)/shard_map/ppermute | solution.py:46
  13.2 1.1 collective-permute-done.other_ref
  14.2 0.8 shard_map.77
  15.0 6.5 %all-to-all-start = ((bf16[8,32,768]{2,1,0:T(8,128)(2,1)}), bf16[8,32,768]{2,1,0:T(8,128)(2,1)S(1)}, u32[]{:S(2)}, u32[]{:S(2)}) async-start(bf16[8,32,768]{2,1,0:T(8,128)(2,1)} %shard_map.77), calls=%async_computation | async-start | bytes 786432 | tf_op jit(solution)/shard_map/all_to_all | solution.py:152
  21.5 1.6 copy-done.1
  23.1 0.7 copy-done.13
  23.8 1.5 shard_map.78
  25.3 1.5 collective-permute-start.3
  26.8 1.3 collective-permute-start.1
  28.1 8.1 %all-to-all-done = bf16[8,32,768]{2,1,0:T(8,128)(2,1)S(1)} async-done(((bf16[8,32,768]{2,1,0:T(8,128)(2,1)}), bf16[8,32,768]{2,1,0:T(8,128)(2,1)S(1)}, u32[]{:S(2)}, u32[]{:S(2)}) %all-to-all-start) | async-done | bytes 393248 | tf_op jit(solution)/shard_map/all_to_all | solution.py:152
  36.3 0.7 copy-done.14
  37.1 1.5 collective-permute-start.4
  38.6 6.0 %collective-permute-done.3.refs_4_ = bf16[528,512]{1,0:T(8,128)(2,1)S(1)} collective-permute-done((bf16[528,512]{1,0:T(8,128)(2,1)S(1)}, bf16[528,512]{1,0:T(8,128)(2,1)S(1)}, u32[]{:S(2)}, u32[]{:S(2)}) %collective-permute-start.3) | collective-permute-done | bytes 540704 | tf_op jit(solution)/shard_map/ppermute | solution.py:42
  44.6 2.7 %collective-permute-start.5 = (bf16[528,512]{1,0:T(8,128)(2,1)S(1)}, bf16[528,512]{1,0:T(8,128)(2,1)S(1)}, u32[]{:S(2)}, u32[]{:S(2)}) collective-permute-start(bf16[528,512]{1,0:T(8,128)(2,1)S(1)} %collective-permute-done.1.refs_2_), channel_id=1, source_target_pairs={{0,14},{2,0},{4,2},{6,4},{8,6},{10,8},{12,10},{14,12},{1,15},{3,1}... | collective-permute-start | bytes 1622024 | tf_op jit(solution)/shard_map/ppermute | solution.py:42
  47.3 7.7 %collective-permute-done.2.refs_3_ = bf16[528,512]{1,0:T(8,128)(2,1)S(1)} collective-permute-done((bf16[528,512]{1,0:T(8,128)(2,1)S(1)}, bf16[528,512]{1,0:T(8,128)(2,1)S(1)}, u32[]{:S(2)}, u32[]{:S(2)}) %collective-permute-start.2) | collective-permute-done | bytes 540704 | tf_op jit(solution)/shard_map/ppermute | solution.py:42
  55.0 2.2 %collective-permute-start.6 = (bf16[528,512]{1,0:T(8,128)(2,1)S(1)}, bf16[528,512]{1,0:T(8,128)(2,1)S(1)}, u32[]{:S(2)}, u32[]{:S(2)}) collective-permute-start(bf16[528,512]{1,0:T(8,128)(2,1)S(1)} %collective-permute-done.2.refs_3_), channel_id=1, source_target_pairs={{0,14},{2,0},{4,2},{6,4},{8,6},{10,8},{12,10},{14,12},{1,15},{3,1}... | collective-permute-start | bytes 1622024 | tf_op jit(solution)/shard_map/ppermute | solution.py:42
  57.2 10.6 %collective-permute-done.7.refs_8_ = bf16[528,512]{1,0:T(8,128)(2,1)S(1)} collective-permute-done((bf16[528,512]{1,0:T(8,128)(2,1)S(1)}, bf16[528,512]{1,0:T(8,128)(2,1)S(1)}, u32[]{:S(2)}, u32[]{:S(2)}) %collective-permute-start.7) | collective-permute-done | bytes 540704 | tf_op jit(solution)/shard_map/ppermute | solution.py:42
  67.8 2.7 %collective-permute-start.9 = (bf16[528,512]{1,0:T(8,128)(2,1)S(1)}, bf16[528,512]{1,0:T(8,128)(2,1)S(1)}, u32[]{:S(2)}, u32[]{:S(2)}) collective-permute-start(bf16[528,512]{1,0:T(8,128)(2,1)S(1)} %collective-permute-done.5.refs_6_), channel_id=1, source_target_pairs={{0,14},{2,0},{4,2},{6,4},{8,6},{10,8},{12,10},{14,12},{1,15},{3,1}... | collective-permute-start | bytes 1622024 | tf_op jit(solution)/shard_map/ppermute | solution.py:42
  70.5 7.6 %collective-permute-done.6.refs_7_ = bf16[528,512]{1,0:T(8,128)(2,1)S(1)} collective-permute-done((bf16[528,512]{1,0:T(8,128)(2,1)S(1)}, bf16[528,512]{1,0:T(8,128)(2,1)S(1)}, u32[]{:S(2)}, u32[]{:S(2)}) %collective-permute-start.6) | collective-permute-done | bytes 540704 | tf_op jit(solution)/shard_map/ppermute | solution.py:42
  78.1 2.2 %collective-permute-start.10 = (bf16[528,512]{1,0:T(8,128)(2,1)S(1)}, bf16[528,512]{1,0:T(8,128)(2,1)S(1)}, u32[]{:S(2)}, u32[]{:S(2)}) collective-permute-start(bf16[528,512]{1,0:T(8,128)(2,1)S(1)} %collective-permute-done.6.refs_7_), channel_id=1, source_target_pairs={{0,14},{2,0},{4,2},{6,4},{8,6},{10,8},{12,10},{14,12},{1,15},{3,1}... | collective-permute-start | bytes 1622024 | tf_op jit(solution)/shard_map/ppermute | solution.py:42
  80.3 10.7 %collective-permute-done.11.refs_12_.before_ref = bf16[528,512]{1,0:T(8,128)(2,1)S(1)} collective-permute-done((bf16[528,512]{1,0:T(8,128)(2,1)S(1)}, bf16[528,512]{1,0:T(8,128)(2,1)S(1)}, u32[]{:S(2)}, u32[]{:S(2)}) %collective-permute-start.11) | collective-permute-done | bytes 540704 | tf_op jit(solution)/shard_map/ppermute | solution.py:42
  91.1 0.9 shard_map.80
  92.6 2.3 %collective-permute-start.14 = (bf16[528,256]{1,0:T(8,128)(2,1)S(1)}, bf16[528,256]{1,0:T(8,128)(2,1)S(1)}, u32[]{:S(2)}, u32[]{:S(2)}) collective-permute-start(bf16[528,256]{1,0:T(8,128)(2,1)S(1)} %get-tuple-element.28), channel_id=1, source_target_pairs={{0,14},{2,0},{4,2},{6,4},{8,6},{10,8},{12,10},{14,12},{1,15},{3,1}... | collective-permute-start | bytes 811016 | tf_op jit(solution)/shard_map/ppermute | solution.py:42
  94.9 6.3 %collective-permute-done.10.refs_11_.behind_ref = bf16[528,512]{1,0:T(8,128)(2,1)S(1)} collective-permute-done((bf16[528,512]{1,0:T(8,128)(2,1)S(1)}, bf16[528,512]{1,0:T(8,128)(2,1)S(1)}, u32[]{:S(2)}, u32[]{:S(2)}) %collective-permute-start.10) | collective-permute-done | bytes 540704 | tf_op jit(solution)/shard_map/ppermute | solution.py:42
  101.2 1.3 collective-permute-done.12.refs_13_.before_ref
  102.6 0.8 copy-done.7
  103.4 0.6 collective-permute-start.15
  104.0 2.0 %collective-permute-start.16 = (bf16[528,256]{1,0:T(8,128)(2,1)S(1)}, bf16[528,256]{1,0:T(8,128)(2,1)S(1)}, u32[]{:S(2)}, u32[]{:S(2)}) collective-permute-start(bf16[528,256]{1,0:T(8,128)(2,1)S(1)} %get-tuple-element.30), channel_id=1, source_target_pairs={{0,14},{2,0},{4,2},{6,4},{8,6},{10,8},{12,10},{14,12},{1,15},{3,1}... | collective-permute-start | bytes 811016 | tf_op jit(solution)/shard_map/ppermute | solution.py:42
  106.0 9.5 %shard_map.79 = (bf16[1024,768]{1,0:T(8,128)(2,1)}, f32[16,512]{1,0:T(8,128)}) custom-call(s32[1]{0:T(128)} %bitcast.section_ref, bf16[16,8,32,768]{3,2,1,0:T(8,128)(2,1)} %bitcast.6, bf16[528,512]{1,0:T(8,128)(2,1)} %copy-done.2, bf16[528,512]{1,0:T(8,128)(2,1)} %copy-done.3, bf16[528,512]{1,0:T(8,128)(2,1)} %copy-done.16, bf16[528,512]{1,0:T(8,128)(2,1)} %copy-done.17, ...), custom_call_target="tpu_custom_call" | custom-call | tf_op jit(solution)/shard_map/pallas_call | solution.py:215
  115.6 0.6 copy-done.23
  116.6 5.5 %shard_map.82 = (bf16[512,512]{1,0:T(8,128)(2,1)}, bf16[512,512]{1,0:T(8,128)(2,1)}, bf16[1024,256]{1,0:T(8,128)(2,1)}, f32[16,512]{1,0:T(8,128)}) custom-call(s32[1]{0:T(128)} %bitcast.section_ref, s32[1]{0:T(128)} %bitcast.1.core_ref, bf16[16,8,32,768]{3,2,1,0:T(8,128)(2,1)} %bitcast.7, bf16[1024,768]{1,0:T(8,128)(2,1)} %get-tuple-element.25.total_hbm, ...), custom_call_target="tpu_custom_call" | custom-call | tf_op jit(solution)/shard_map/pallas_call | solution.py:296
  122.1 3.1 %collective-permute-start.17 = (bf16[512,512]{1,0:T(8,128)(2,1)}, bf16[512,512]{1,0:T(8,128)(2,1)S(1)}, u32[]{:S(2)}, u32[]{:S(2)}) collective-permute-start(bf16[512,512]{1,0:T(8,128)(2,1)} %get-tuple-element.32), channel_id=1, source_target_pairs={{0,1},{1,0},{2,3},{3,2},{4,5},{5,4},{6,7},{7,6},{8,9},{9,8},{10,11... | collective-permute-start | bytes 1572872 | tf_op jit(solution)/shard_map/ppermute | solution.py:46
  125.3 1.9 %fusion = (f32[1024,64]{1,0:T(8,128)S(1)}, f32[1024,64]{1,0:T(8,128)S(1)}, f32[1024,64]{1,0:T(8,128)S(1)}) fusion(f32[64]{0:T(128)S(1)} %multiply_exponential_fusion, f32[1024]{0:T(1024)S(1)} %iota_convert_fusion), kind=kLoop, calls=%fused_computation.4 | loop fusion | flops 131072 | bytes 790784 | tf_op jit(solution)/shard_map/neg | solution.py:473
  127.6 2.3 %shard_map.83 = (bf16[128,768]{1,0:T(8,128)(2,1)S(1)}, bf16[1024,128]{1,0:T(8,128)(2,1)S(1)}, bf16[1024,128]{1,0:T(8,128)(2,1)S(1)}, f32[1024,128]{1,0:T(8,128)S(1)}) custom-call(s32[1]{0:T(128)} %bitcast.section_ref, s32[1]{0:T(128)} %bitcast.1.core_ref, bf16[512,512]{1,0:T(8,128)(2,1)S(1)} %copy-done, ...), custom_call_target="tpu_custom_call" | custom-call | tf_op jit(solution)/shard_map/pallas_call | solution.py:398
  129.9 1.0 shard_map.86
  130.9 0.7 collective-permute-start.22
  131.7 1.7 %shard_map.85 = bf16[128,768]{1,0:T(8,128)(2,1)S(1)} custom-call(s32[1]{0:T(128)} %bitcast.section_ref, s32[1]{0:T(128)} %bitcast.1.core_ref, bf16[512,512]{1,0:T(8,128)(2,1)S(1)} %copy-done, bf16[512,512]{1,0:T(8,128)(2,1)S(1)} %collective-permute-done.17.refs_1_, f32[1024,128]{1,0:T(8,128)S(1)} %get-tuple-element.42.refs_5_.refs_2_, ...), custom_call_target="tpu_custom_call" | custom-call | tf_op jit(solution)/shard_map/pallas_call | solution.py:408
  133.4 0.6 collective-permute-start.21
  134.0 1.0 shard_map.84
  134.9 1.0 collective-permute-start.20
  135.9 7.7 %collective-permute-start.19 = (bf16[128,768]{1,0:T(8,128)(2,1)S(1)}, bf16[128,768]{1,0:T(8,128)(2,1)S(1)}, u32[]{:S(2)}, u32[]{:S(2)}) collective-permute-start(bf16[128,768]{1,0:T(8,128)(2,1)S(1)} %get-tuple-element.35), channel_id=1, source_target_pairs={{0,0},{1,8},{2,2},{3,10},{4,4},{5,12},{6,6},{7,14},{8,9},{9,1},{10... | collective-permute-start | bytes 589832 | tf_op jit(solution)/shard_map/ppermute | solution.py:427
  143.6 2.1 %collective-permute-done.21.refs_2_ = bf16[128,768]{1,0:T(8,128)(2,1)S(1)} collective-permute-done((bf16[128,768]{1,0:T(8,128)(2,1)S(1)}, bf16[128,768]{1,0:T(8,128)(2,1)S(1)}, u32[]{:S(2)}, u32[]{:S(2)}) %collective-permute-start.21) | collective-permute-done | bytes 196640 | tf_op jit(solution)/shard_map/ppermute | solution.py:427
  145.7 1.3 collective-permute-done.20.refs_1_
  147.1 3.5 %collective-permute-done.19.refs_0_ = bf16[128,768]{1,0:T(8,128)(2,1)S(1)} collective-permute-done((bf16[128,768]{1,0:T(8,128)(2,1)S(1)}, bf16[128,768]{1,0:T(8,128)(2,1)S(1)}, u32[]{:S(2)}, u32[]{:S(2)}) %collective-permute-start.19) | collective-permute-done | bytes 196640 | tf_op jit(solution)/shard_map/ppermute | solution.py:427
  150.6 1.0 shard_map.87
  (73 shorter events, 1.8 us)
Async XLA Ops:
  7.2 1.0 copy-start.9
  8.1 0.8 copy-start.10
  9.0 0.8 copy-start.11
  9.8 4.4 %collective-permute-start = (bf16[32,3072]{1,0:T(8,128)(2,1)S(1)}, bf16[32,3072]{1,0:T(8,128)(2,1)S(1)}, u32[]{:S(2)}, u32[]{:S(2)}) collective-permute-start(bf16[32,3072]{1,0:T(8,128)(2,1)S(1)} %get-tuple-element.22), channel_id=1, source_target_pairs={{0,1},{1,0},{2,3},{3,2},{4,5},{5,4},{6,7},{7,6},{8,9},{9,8},{10,11... | collective-permute-start | bytes 589832 | tf_op jit(solution)/shard_map/ppermute | solution.py:46
  15.0 21.2 %all-to-all-start = ((bf16[8,32,768]{2,1,0:T(8,128)(2,1)}), bf16[8,32,768]{2,1,0:T(8,128)(2,1)S(1)}, u32[]{:S(2)}, u32[]{:S(2)}) async-start(bf16[8,32,768]{2,1,0:T(8,128)(2,1)} %shard_map.77), calls=%async_computation | async-start | bytes 786432 | tf_op jit(solution)/shard_map/all_to_all | solution.py:152
  21.5 84.6 %all-gather.2.cloned.1.call-start = ((), (), s32[]{:S(2)}) async-start(), calls=%async_computation.1 | async-start | bytes 6684672 | tf_op jit(solution)/shard_map/all_gather | solution.py:153
  21.5 1.6 %copy-start.1 = (bf16[1,1024,1024]{2,1,0:T(8,128)(2,1)S(1)}, bf16[1,1024,1024]{2,1,0:T(8,128)(2,1)}, u32[]{:S(2)}) copy-start(bf16[1,1024,1024]{2,1,0:T(8,128)(2,1)} %token_ref.1) | copy-start | bytes 6291460
  25.3 66.7 %copy-start.2 = (bf16[528,512]{1,0:T(8,128)(2,1)}, bf16[528,512]{1,0:T(8,128)(2,1)S(1)}, u32[]{:S(2)}) copy-start(bf16[528,512]{1,0:T(8,128)(2,1)S(1)} %get-tuple-element.23.refs_0_) | copy-start | bytes 1622020
  25.3 66.7 %copy-start.3 = (bf16[528,512]{1,0:T(8,128)(2,1)}, bf16[528,512]{1,0:T(8,128)(2,1)S(1)}, u32[]{:S(2)}) copy-start(bf16[528,512]{1,0:T(8,128)(2,1)S(1)} %get-tuple-element.24.refs_1_) | copy-start | bytes 1622020
  25.3 19.3 %collective-permute-start.3 = (bf16[528,512]{1,0:T(8,128)(2,1)S(1)}, bf16[528,512]{1,0:T(8,128)(2,1)S(1)}, u32[]{:S(2)}, u32[]{:S(2)}) collective-permute-start(bf16[528,512]{1,0:T(8,128)(2,1)S(1)} %get-tuple-element.23.refs_0_), channel_id=1, source_target_pairs={{0,2},{2,4},{4,6},{6,8},{8,10},{10,12},{12,14},{14,0},{1,3},{3,5},... | collective-permute-start | bytes 1622024 | tf_op jit(solution)/shard_map/ppermute | solution.py:42
  26.8 17.8 %collective-permute-start.1 = (bf16[528,512]{1,0:T(8,128)(2,1)S(1)}, bf16[528,512]{1,0:T(8,128)(2,1)S(1)}, u32[]{:S(2)}, u32[]{:S(2)}) collective-permute-start(bf16[528,512]{1,0:T(8,128)(2,1)S(1)} %get-tuple-element.23.refs_0_), channel_id=1, source_target_pairs={{0,14},{2,0},{4,2},{6,4},{8,6},{10,8},{12,10},{14,12},{1,15},{3,1}... | collective-permute-start | bytes 1622024 | tf_op jit(solution)/shard_map/ppermute | solution.py:42
  37.0 17.9 %collective-permute-start.2 = (bf16[528,512]{1,0:T(8,128)(2,1)S(1)}, bf16[528,512]{1,0:T(8,128)(2,1)S(1)}, u32[]{:S(2)}, u32[]{:S(2)}) collective-permute-start(bf16[528,512]{1,0:T(8,128)(2,1)S(1)} %get-tuple-element.24.refs_1_), channel_id=1, source_target_pairs={{0,14},{2,0},{4,2},{6,4},{8,6},{10,8},{12,10},{14,12},{1,15},{3,1}... | collective-permute-start | bytes 1622024 | tf_op jit(solution)/shard_map/ppermute | solution.py:42
  37.1 20.0 %collective-permute-start.4 = (bf16[528,512]{1,0:T(8,128)(2,1)S(1)}, bf16[528,512]{1,0:T(8,128)(2,1)S(1)}, u32[]{:S(2)}, u32[]{:S(2)}) collective-permute-start(bf16[528,512]{1,0:T(8,128)(2,1)S(1)} %get-tuple-element.24.refs_1_), channel_id=1, source_target_pairs={{0,2},{2,4},{4,6},{6,8},{8,10},{10,12},{12,14},{14,0},{1,3},{3,5},... | collective-permute-start | bytes 1622024 | tf_op jit(solution)/shard_map/ppermute | solution.py:42
  44.6 12.6 %copy-start.15 = (bf16[528,512]{1,0:T(8,128)(2,1)}, bf16[528,512]{1,0:T(8,128)(2,1)S(1)}, u32[]{:S(2)}) copy-start(bf16[528,512]{1,0:T(8,128)(2,1)S(1)} %collective-permute-done.3.refs_4_) | copy-start | bytes 1622020
  44.6 23.2 %collective-permute-start.7 = (bf16[528,512]{1,0:T(8,128)(2,1)S(1)}, bf16[528,512]{1,0:T(8,128)(2,1)S(1)}, u32[]{:S(2)}, u32[]{:S(2)}) collective-permute-start(bf16[528,512]{1,0:T(8,128)(2,1)S(1)} %collective-permute-done.3.refs_4_), channel_id=1, source_target_pairs={{0,2},{2,4},{4,6},{6,8},{8,10},{10,12},{12,14},{14,0},{1,3},{3,5},... | collective-permute-start | bytes 1622024 | tf_op jit(solution)/shard_map/ppermute | solution.py:42
  44.6 23.2 %copy-start.16 = (bf16[528,512]{1,0:T(8,128)(2,1)}, bf16[528,512]{1,0:T(8,128)(2,1)S(1)}, u32[]{:S(2)}) copy-start(bf16[528,512]{1,0:T(8,128)(2,1)S(1)} %collective-permute-done.1.refs_2_) | copy-start | bytes 1622020
  44.6 23.2 %collective-permute-start.5 = (bf16[528,512]{1,0:T(8,128)(2,1)S(1)}, bf16[528,512]{1,0:T(8,128)(2,1)S(1)}, u32[]{:S(2)}, u32[]{:S(2)}) collective-permute-start(bf16[528,512]{1,0:T(8,128)(2,1)S(1)} %collective-permute-done.1.refs_2_), channel_id=1, source_target_pairs={{0,14},{2,0},{4,2},{6,4},{8,6},{10,8},{12,10},{14,12},{1,15},{3,1}... | collective-permute-start | bytes 1622024 | tf_op jit(solution)/shard_map/ppermute | solution.py:42
  55.0 36.1 %copy-start.17 = (bf16[528,512]{1,0:T(8,128)(2,1)}, bf16[528,512]{1,0:T(8,128)(2,1)S(1)}, u32[]{:S(2)}) copy-start(bf16[528,512]{1,0:T(8,128)(2,1)S(1)} %collective-permute-done.2.refs_3_) | copy-start | bytes 1622020
  55.0 23.2 %collective-permute-start.6 = (bf16[528,512]{1,0:T(8,128)(2,1)S(1)}, bf16[528,512]{1,0:T(8,128)(2,1)S(1)}, u32[]{:S(2)}, u32[]{:S(2)}) collective-permute-start(bf16[528,512]{1,0:T(8,128)(2,1)S(1)} %collective-permute-done.2.refs_3_), channel_id=1, source_target_pairs={{0,14},{2,0},{4,2},{6,4},{8,6},{10,8},{12,10},{14,12},{1,15},{3,1}... | collective-permute-start | bytes 1622024 | tf_op jit(solution)/shard_map/ppermute | solution.py:42
  57.1 33.9 %copy-start.18 = (bf16[528,512]{1,0:T(8,128)(2,1)}, bf16[528,512]{1,0:T(8,128)(2,1)S(1)}, u32[]{:S(2)}) copy-start(bf16[528,512]{1,0:T(8,128)(2,1)S(1)} %collective-permute-done.4.refs_5_) | copy-start | bytes 1622020
  57.1 23.2 %collective-permute-start.8 = (bf16[528,512]{1,0:T(8,128)(2,1)S(1)}, bf16[528,512]{1,0:T(8,128)(2,1)S(1)}, u32[]{:S(2)}, u32[]{:S(2)}) collective-permute-start(bf16[528,512]{1,0:T(8,128)(2,1)S(1)} %collective-permute-done.4.refs_5_), channel_id=1, source_target_pairs={{0,2},{2,4},{4,6},{6,8},{8,10},{10,12},{12,14},{14,0},{1,3},{3,5},... | collective-permute-start | bytes 1622024 | tf_op jit(solution)/shard_map/ppermute | solution.py:42
  67.8 23.3 %copy-start.19 = (bf16[528,512]{1,0:T(8,128)(2,1)}, bf16[528,512]{1,0:T(8,128)(2,1)S(1)}, u32[]{:S(2)}) copy-start(bf16[528,512]{1,0:T(8,128)(2,1)S(1)} %collective-permute-done.7.refs_8_) | copy-start | bytes 1622020
  67.8 23.3 %collective-permute-start.11 = (bf16[528,512]{1,0:T(8,128)(2,1)S(1)}, bf16[528,512]{1,0:T(8,128)(2,1)S(1)}, u32[]{:S(2)}, u32[]{:S(2)}) collective-permute-start(bf16[528,512]{1,0:T(8,128)(2,1)S(1)} %collective-permute-done.7.refs_8_), channel_id=1, source_target_pairs={{0,2},{2,4},{4,6},{6,8},{8,10},{10,12},{12,14},{14,0},{1,3},{3,5},... | collective-permute-start | bytes 1622024 | tf_op jit(solution)/shard_map/ppermute | solution.py:42
  67.8 23.3 %copy-start.20 = (bf16[528,512]{1,0:T(8,128)(2,1)}, bf16[528,512]{1,0:T(8,128)(2,1)S(1)}, u32[]{:S(2)}) copy-start(bf16[528,512]{1,0:T(8,128)(2,1)S(1)} %collective-permute-done.5.refs_6_) | copy-start | bytes 1622020
  67.8 23.3 %collective-permute-start.9 = (bf16[528,512]{1,0:T(8,128)(2,1)S(1)}, bf16[528,512]{1,0:T(8,128)(2,1)S(1)}, u32[]{:S(2)}, u32[]{:S(2)}) collective-permute-start(bf16[528,512]{1,0:T(8,128)(2,1)S(1)} %collective-permute-done.5.refs_6_), channel_id=1, source_target_pairs={{0,14},{2,0},{4,2},{6,4},{8,6},{10,8},{12,10},{14,12},{1,15},{3,1}... | collective-permute-start | bytes 1622024 | tf_op jit(solution)/shard_map/ppermute | solution.py:42
  78.1 13.9 %copy-start.21 = (bf16[528,512]{1,0:T(8,128)(2,1)}, bf16[528,512]{1,0:T(8,128)(2,1)S(1)}, u32[]{:S(2)}) copy-start(bf16[528,512]{1,0:T(8,128)(2,1)S(1)} %collective-permute-done.6.refs_7_) | copy-start | bytes 1622020
  78.1 23.1 %collective-permute-start.10 = (bf16[528,512]{1,0:T(8,128)(2,1)S(1)}, bf16[528,512]{1,0:T(8,128)(2,1)S(1)}, u32[]{:S(2)}, u32[]{:S(2)}) collective-permute-start(bf16[528,512]{1,0:T(8,128)(2,1)S(1)} %collective-permute-done.6.refs_7_), channel_id=1, source_target_pairs={{0,14},{2,0},{4,2},{6,4},{8,6},{10,8},{12,10},{14,12},{1,15},{3,1}... | collective-permute-start | bytes 1622024 | tf_op jit(solution)/shard_map/ppermute | solution.py:42
  80.3 11.7 %copy-start.22 = (bf16[528,512]{1,0:T(8,128)(2,1)}, bf16[528,512]{1,0:T(8,128)(2,1)S(1)}, u32[]{:S(2)}) copy-start(bf16[528,512]{1,0:T(8,128)(2,1)S(1)} %collective-permute-done.8.refs_9_) | copy-start | bytes 1622020
  80.3 22.2 %collective-permute-start.12 = (bf16[528,512]{1,0:T(8,128)(2,1)S(1)}, bf16[528,512]{1,0:T(8,128)(2,1)S(1)}, u32[]{:S(2)}, u32[]{:S(2)}) collective-permute-start(bf16[528,512]{1,0:T(8,128)(2,1)S(1)} %collective-permute-done.8.refs_9_), channel_id=1, source_target_pairs={{0,2},{2,4},{4,6},{6,8},{8,10},{10,12},{12,14},{14,0},{1,3},{3,5},... | collective-permute-start | bytes 1622024 | tf_op jit(solution)/shard_map/ppermute | solution.py:42
  91.1 0.9 copy-start.4
  91.1 1.1 copy-start.5
  92.1 23.4 %collective-permute-start.13 = (bf16[528,256]{1,0:T(8,128)(2,1)}, bf16[528,256]{1,0:T(8,128)(2,1)S(1)}, u32[]{:S(2)}, u32[]{:S(2)}) collective-permute-start(bf16[528,256]{1,0:T(8,128)(2,1)} %get-tuple-element.27), channel_id=1, source_target_pairs={{0,2},{2,4},{4,6},{6,8},{8,10},{10,12},{12,14},{14,0},{1,3},{3,5},... | collective-permute-start | bytes 811016 | tf_op jit(solution)/shard_map/ppermute | solution.py:42
  92.6 23.0 %collective-permute-start.14 = (bf16[528,256]{1,0:T(8,128)(2,1)S(1)}, bf16[528,256]{1,0:T(8,128)(2,1)S(1)}, u32[]{:S(2)}, u32[]{:S(2)}) collective-permute-start(bf16[528,256]{1,0:T(8,128)(2,1)S(1)} %get-tuple-element.28), channel_id=1, source_target_pairs={{0,14},{2,0},{4,2},{6,4},{8,6},{10,8},{12,10},{14,12},{1,15},{3,1}... | collective-permute-start | bytes 811016 | tf_op jit(solution)/shard_map/ppermute | solution.py:42
  101.2 1.4 copy-start.6
  102.5 0.8 copy-start.7
  103.4 12.2 %collective-permute-start.15 = (bf16[528,256]{1,0:T(8,128)(2,1)S(1)}, bf16[528,256]{1,0:T(8,128)(2,1)S(1)}, u32[]{:S(2)}, u32[]{:S(2)}) collective-permute-start(bf16[528,256]{1,0:T(8,128)(2,1)S(1)} %get-tuple-element.29), channel_id=1, source_target_pairs={{0,2},{2,4},{4,6},{6,8},{8,10},{10,12},{12,14},{14,0},{1,3},{3,5},... | collective-permute-start | bytes 811016 | tf_op jit(solution)/shard_map/ppermute | solution.py:42
  104.0 11.6 %collective-permute-start.16 = (bf16[528,256]{1,0:T(8,128)(2,1)S(1)}, bf16[528,256]{1,0:T(8,128)(2,1)S(1)}, u32[]{:S(2)}, u32[]{:S(2)}) collective-permute-start(bf16[528,256]{1,0:T(8,128)(2,1)S(1)} %get-tuple-element.30), channel_id=1, source_target_pairs={{0,14},{2,0},{4,2},{6,4},{8,6},{10,8},{12,10},{14,12},{1,15},{3,1}... | collective-permute-start | bytes 811016 | tf_op jit(solution)/shard_map/ppermute | solution.py:42
  115.6 0.9 copy-start.25
  115.6 0.9 copy-start.26
  122.1 5.4 %collective-permute-start.17 = (bf16[512,512]{1,0:T(8,128)(2,1)}, bf16[512,512]{1,0:T(8,128)(2,1)S(1)}, u32[]{:S(2)}, u32[]{:S(2)}) collective-permute-start(bf16[512,512]{1,0:T(8,128)(2,1)} %get-tuple-element.32), channel_id=1, source_target_pairs={{0,1},{1,0},{2,3},{3,2},{4,5},{5,4},{6,7},{7,6},{8,9},{9,8},{10,11... | collective-permute-start | bytes 1572872 | tf_op jit(solution)/shard_map/ppermute | solution.py:46
  125.1 2.5 %collective-permute-start.18 = (bf16[1024,256]{1,0:T(8,128)(2,1)}, bf16[1024,256]{1,0:T(8,128)(2,1)S(1)}, u32[]{:S(2)}, u32[]{:S(2)}) collective-permute-start(bf16[1024,256]{1,0:T(8,128)(2,1)} %get-tuple-element.33.refs_2_), channel_id=1, source_target_pairs={{0,1},{1,0},{2,3},{3,2},{4,5},{5,4},{6,7},{7,6},{8,9},{9,8},{10,11... | collective-permute-start | bytes 1572872 | tf_op jit(solution)/shard_map/ppermute | solution.py:46
  125.2 2.4 %copy-start = (bf16[512,512]{1,0:T(8,128)(2,1)S(1)}, bf16[512,512]{1,0:T(8,128)(2,1)}, u32[]{:S(2)}) copy-start(bf16[512,512]{1,0:T(8,128)(2,1)} %get-tuple-element.31.refs_0_) | copy-start | bytes 1572868
  125.3 2.4 %copy-start.8 = (bf16[1024,256]{1,0:T(8,128)(2,1)S(1)}, bf16[1024,256]{1,0:T(8,128)(2,1)}, u32[]{:S(2)}) copy-start(bf16[1024,256]{1,0:T(8,128)(2,1)} %get-tuple-element.33.refs_2_) | copy-start | bytes 1572868
  125.3 2.4 %copy-start.12 = (f32[16,512]{1,0:T(8,128)S(1)}, f32[16,512]{1,0:T(8,128)}, u32[]{:S(2)}) copy-start(f32[16,512]{1,0:T(8,128)} %get-tuple-element.34.refs_4_) | copy-start | bytes 98308
  130.9 12.7 %collective-permute-start.22 = (bf16[128,768]{1,0:T(8,128)(2,1)S(1)}, bf16[128,768]{1,0:T(8,128)(2,1)S(1)}, u32[]{:S(2)}, u32[]{:S(2)}) collective-permute-start(bf16[128,768]{1,0:T(8,128)(2,1)S(1)} %shard_map.86), channel_id=1, source_target_pairs={{0,14},{1,6},{2,0},{3,8},{4,2},{5,10},{6,4},{7,12},{8,7},{9,15},{1... | collective-permute-start | bytes 589832 | tf_op jit(solution)/shard_map/ppermute | solution.py:427
  133.4 12.3 %collective-permute-start.21 = (bf16[128,768]{1,0:T(8,128)(2,1)S(1)}, bf16[128,768]{1,0:T(8,128)(2,1)S(1)}, u32[]{:S(2)}, u32[]{:S(2)}) collective-permute-start(bf16[128,768]{1,0:T(8,128)(2,1)S(1)} %shard_map.85), channel_id=1, source_target_pairs={{0,4},{1,12},{2,6},{3,14},{4,8},{5,0},{6,10},{7,2},{8,13},{9,5},{1... | collective-permute-start | bytes 589832 | tf_op jit(solution)/shard_map/ppermute | solution.py:427
  134.9 12.1 %collective-permute-start.20 = (bf16[128,768]{1,0:T(8,128)(2,1)S(1)}, bf16[128,768]{1,0:T(8,128)(2,1)S(1)}, u32[]{:S(2)}, u32[]{:S(2)}) collective-permute-start(bf16[128,768]{1,0:T(8,128)(2,1)S(1)} %shard_map.84), channel_id=1, source_target_pairs={{0,10},{1,2},{2,12},{3,4},{4,14},{5,6},{6,0},{7,8},{8,3},{9,11},{1... | collective-permute-start | bytes 589832 | tf_op jit(solution)/shard_map/ppermute | solution.py:427
  135.9 14.7 %collective-permute-start.19 = (bf16[128,768]{1,0:T(8,128)(2,1)S(1)}, bf16[128,768]{1,0:T(8,128)(2,1)S(1)}, u32[]{:S(2)}, u32[]{:S(2)}) collective-permute-start(bf16[128,768]{1,0:T(8,128)(2,1)S(1)} %get-tuple-element.35), channel_id=1, source_target_pairs={{0,0},{1,8},{2,2},{3,10},{4,4},{5,12},{6,6},{7,14},{8,9},{9,1},{10... | collective-permute-start | bytes 589832 | tf_op jit(solution)/shard_map/ppermute | solution.py:427
  (4 other events, 2.9 us)
Sparse Core Ops, SparseCore 0:
  37.1 63.8 all-gather.1
